TPU v7x, 32 devices: a whole 2x2x4 slice. The times are simulated.
32 devices in a mesh: dp: 16 (over z, y, x), tensor: 2 (over core).
Axes of the slice: x: 2, y: 2, z: 4, core: 2. Of those that a mesh axis runs over, the one named last changes fastest.
Arguments:
- tokens: bfloat16 [50176, 192], P(('dp', 'tensor')), may hold values from -6 to 6
- cotangent: bfloat16 [50176, 192], P(('dp', 'tensor')), may hold values from -6 to 6
- keep_mask: int32 [256, 196], P('dp'), may hold values from 0 to 1, as said below
- triple_weight: float32 [3, 192, 192], P(None, None, 'tensor'), may hold values from -0.4375 to 0.4375
- outward_weight: float32 [192, 192], P('tensor'), may hold values from -3.5 to 3.5
- widen_weight: float32 [192, 768], P(None, 'tensor'), may hold values from -0.4375 to 0.4375
- narrow_weight: float32 [768, 192], P('tensor'), may hold values from -0.21875 to 0.21875
- vectors: float32 [6, 192], replicated, may hold values from -0.5 to 2.26
- hidden_bias: float32 [768], P('tensor'), may hold values from -0.5 to 0.5
- head_params: float32 [4, 4], P(None, 'tensor'), may hold values from -1.5 to 1.5
- triple_moment: float32 [2, 55296], P('tensor', 'dp'), may hold values from -0.0009765625 to 0.0009765625
- triple_square: float32 [2, 55296], P('tensor', 'dp'), may hold values from 1.2e-07 to 4.7e-07
- outward_moment: float32 [2, 18432], P('tensor', 'dp'), may hold values from -0.0009765625 to 0.0009765625
- outward_square: float32 [2, 18432], P('tensor', 'dp'), may hold values from 1.2e-07 to 4.7e-07
- widen_moment: float32 [2, 73728], P('tensor', 'dp'), may hold values from -0.0009765625 to 0.0009765625
- widen_square: float32 [2, 73728], P('tensor', 'dp'), may hold values from 1.2e-07 to 4.7e-07
- narrow_moment: float32 [2, 73728], P('tensor', 'dp'), may hold values from -0.0009765625 to 0.0009765625
- narrow_square: float32 [2, 73728], P('tensor', 'dp'), may hold values from 1.2e-07 to 4.7e-07
- vector_moment: float32 [6, 192], replicated, may hold values from -0.0048828125 to 0.0048828125
- vector_square: float32 [6, 192], replicated, may hold values from 3.4e-06 to 1.35e-05
- hidden_moment: float32 [768], P('tensor'), may hold values from -0.0048828125 to 0.0048828125
- hidden_square: float32 [768], P('tensor'), may hold values from 6e-08 to 2.4e-07
- head_moment: float32 [4, 4], P(None, 'tensor'), may hold values from -0.0048828125 to 0.0048828125
- head_square: float32 [4, 4], P(None, 'tensor'), may hold values from 3.4e-06 to 1.35e-05
Outputs:
- result: float32 [50176, 192], P(('dp', 'tensor'))
- grad_input: float32 [50176, 192], P(('dp', 'tensor'))
- triple_moments: float32 [2, 55296], P('tensor', 'dp')
- triple_squares: float32 [2, 55296], P('tensor', 'dp')
- triple_updated: float32 [2, 55296], P('tensor', 'dp')
- outward_moments: float32 [2, 18432], P('tensor', 'dp')
- outward_squares: float32 [2, 18432], P('tensor', 'dp')
- outward_updated: float32 [2, 18432], P('tensor', 'dp')
- widen_moments: float32 [2, 73728], P('tensor', 'dp')
- widen_squares: float32 [2, 73728], P('tensor', 'dp')
- widen_updated: float32 [2, 73728], P('tensor', 'dp')
- narrow_moments: float32 [2, 73728], P('tensor', 'dp')
- narrow_squares: float32 [2, 73728], P('tensor', 'dp')
- narrow_updated: float32 [2, 73728], P('tensor', 'dp')
- vector_moments: float32 [6, 192], replicated
- vector_squares: float32 [6, 192], replicated
- vector_updated: float32 [6, 192], replicated
- hidden_moments: float32 [768], P('tensor')
- hidden_squares: float32 [768], P('tensor')
- hidden_updated: float32 [768], P('tensor')
- head_moments: float32 [4, 4], P(None, 'tensor')
- head_squares: float32 [4, 4], P(None, 'tensor')
- head_updated: float32 [4, 4], P(None, 'tensor')
- grad_norm: float32 [], replicated
Inputs may be any that keep to these rules, and one draw needn't show every extreme that they name: `keep_mask`: each image keeps at least one of its 196 patches.
All inputs are finite; a program needn't handle non-finite values.
Results may differ from a plain program's by a relative error of at most 0.006.
The roundings to bfloat16 on the way count: a program that leaves them out, or rounds other values in their place, can miss the bound.
Values may be sent and summed in bfloat16 or wider, within the bound.
No kernel may reach another device: no remote copies, remote signals or barrier semaphores. Data moves between devices by JAX's collectives and lax.ppermute only.
A program may use at most 128 MiB of HBM per device.

v0:
```python
import math

import jax
import jax.numpy as jnp
from jax import lax
from jax.sharding import PartitionSpec as P

GRID = 14
STEP = 10


EPS_NORM = 1e-06
NEG_FILL = -1e30
CLIP_AT = 1.0
BETA_ONE = 0.9
BETA_TWO = 0.95
ADAM_EPS = 1e-08
RATES = (0.1, 0.5, 0.1, 0.05, 0.3, 0.1, 0.3)
DECAYS = (0.05, 0.05, 0.05, 0.05, 0.0, 0.0, 0.0)
PRECISE = lax.Precision.HIGHEST


def layer_norm(features, gains, shifts):
    average = jnp.mean(features, axis=-1, keepdims=True)
    centred = features - average
    variance = jnp.mean(centred * centred, axis=-1, keepdims=True)
    return centred * lax.rsqrt(variance + EPS_NORM) * gains + shifts


def offsets_table(patch_count, grid_side):
    placing = jnp.arange(patch_count, dtype=jnp.int32)
    column = (placing % grid_side).astype(jnp.float32)
    rowpos = (placing // grid_side).astype(jnp.float32)
    across = column[None, :] - column[:, None]
    upward = rowpos[None, :] - rowpos[:, None]
    return jnp.stack([across, upward, across * across + upward * upward])


def masked_softmax(scores, kept_keys):
    scores = jnp.where(kept_keys, scores, NEG_FILL)
    highest = jnp.max(scores, axis=-1, keepdims=True)
    exponent = jnp.exp(scores - highest)
    return exponent / jnp.sum(exponent, axis=-1, keepdims=True)


def softmax_back(probability, upstream):
    return probability * (upstream - jnp.sum(upstream * probability, axis=-1, keepdims=True))


def exact_gelu(values_in):
    return jax.nn.gelu(values_in, approximate=False)


def adam_update(weight, gradient, moment, squares, learn_rate, decay_rate):
    moment_new = BETA_ONE * moment + (1.0 - BETA_ONE) * gradient
    squares_new = BETA_TWO * squares + (1.0 - BETA_TWO) * gradient * gradient
    quotient = (
        moment_new
        / (1.0 - BETA_ONE**STEP)
        / (jnp.sqrt(squares_new / (1.0 - BETA_TWO**STEP)) + ADAM_EPS)
    )
    return (moment_new, squares_new, weight - learn_rate * (quotient + decay_rate * weight))


def layer_pass(
    tokens,
    cotangent,
    keep_here,
    row_kept,
    triple_weight,
    outward_weight,
    widen_weight,
    narrow_weight,
    vectors,
    hidden_bias,
    head_params,
):
    images = keep_here.shape[0]
    patches = keep_here.shape[1]
    heads_here = head_params.shape[1]
    width_here = triple_weight.shape[2]
    head_size = width_here // heads_here
    all_rows = images * patches
    scaling = 1.0 / math.sqrt(head_size)
    kept_keys = (keep_here > 0)[:, None, None, :]
    offsets = offsets_table(patches, GRID)
    inputs = tokens.astype(jnp.float32)
    normed_one, norm_one_pull = jax.vjp(layer_norm, inputs, vectors[0], vectors[1])
    normed_low = normed_one.astype(jnp.bfloat16)
    first_in = lax.all_gather(normed_low, "tensor", axis=0, tiled=True)
    triple_low = triple_weight.astype(jnp.bfloat16)
    projected = jnp.einsum(
        "td,cdf->ctf", first_in, triple_low, preferred_element_type=jnp.float32
    ).astype(jnp.bfloat16)
    projected = projected.reshape(3, images, patches, heads_here, head_size)
    queries = projected[0]
    key_rows = projected[1]
    value_rows = projected[2]
    scores = (
        jnp.einsum("iqhe,ikhe->ihqk", queries, key_rows, preferred_element_type=jnp.float32)
        * scaling
    )
    content = masked_softmax(scores, kept_keys)
    placed = jnp.einsum("ch,cqk->hqk", head_params[:3], offsets, precision=PRECISE)
    located = masked_softmax(placed[None], kept_keys)
    gating_flat = jax.nn.sigmoid(head_params[3])
    gating = gating_flat[None, :, None, None]
    attention = ((1.0 - gating) * content + gating * located).astype(jnp.bfloat16)
    mixture = jnp.einsum(
        "ihqk,ikhe->iqhe", attention, value_rows, preferred_element_type=jnp.float32
    )
    mixture = mixture.astype(jnp.bfloat16).reshape(all_rows, width_here)
    outward_low = outward_weight.astype(jnp.bfloat16)
    attn_terms = jnp.dot(mixture, outward_low, preferred_element_type=jnp.float32)
    attn_out = lax.psum_scatter(attn_terms, "tensor", scatter_dimension=0, tiled=True)
    middle = inputs + attn_out + vectors[4]
    normed_two, norm_two_pull = jax.vjp(layer_norm, middle, vectors[2], vectors[3])
    second_low = normed_two.astype(jnp.bfloat16)
    second_in = lax.all_gather(second_low, "tensor", axis=0, tiled=True)
    widen_low = widen_weight.astype(jnp.bfloat16)
    before = jnp.dot(second_in, widen_low, preferred_element_type=jnp.float32) + hidden_bias
    activated, gelu_pull = jax.vjp(exact_gelu, before)
    activated_low = activated.astype(jnp.bfloat16)
    narrow_low = narrow_weight.astype(jnp.bfloat16)
    mlp_terms = jnp.dot(activated_low, narrow_low, preferred_element_type=jnp.float32)
    mlp_out = lax.psum_scatter(
        mlp_terms.astype(jnp.bfloat16), "tensor", scatter_dimension=0, tiled=True
    ).astype(jnp.float32)
    result = middle + mlp_out + vectors[5]
    incoming = cotangent.astype(jnp.float32) * row_kept
    incoming_low = incoming.astype(jnp.bfloat16)
    incoming_all = lax.all_gather(incoming_low, "tensor", axis=0, tiled=True)
    narrow_grad = jnp.einsum(
        "tf,td->fd", activated_low, incoming_all, preferred_element_type=jnp.float32
    )
    grad_activated = jnp.einsum(
        "td,fd->tf", incoming_all, narrow_low, preferred_element_type=jnp.float32
    )
    grad_before = gelu_pull(grad_activated)[0]
    hidden_grad = jnp.sum(grad_before, axis=0)
    grad_low = grad_before.astype(jnp.bfloat16)
    widen_grad = jnp.einsum("td,tf->df", second_in, grad_low, preferred_element_type=jnp.float32)
    second_terms = jnp.einsum("tf,df->td", grad_low, widen_low, preferred_element_type=jnp.float32)
    grad_second = lax.psum_scatter(second_terms, "tensor", scatter_dimension=0, tiled=True)
    grad_middle, gain_two_grad, shift_two_grad = norm_two_pull(grad_second)
    grad_middle = grad_middle + incoming
    middle_low = grad_middle.astype(jnp.bfloat16)
    middle_all = lax.all_gather(middle_low, "tensor", axis=0, tiled=True)
    outward_grad = jnp.einsum("tf,td->fd", mixture, middle_all, preferred_element_type=jnp.float32)
    grad_mixture = jnp.einsum(
        "td,fd->tf", middle_all, outward_low, preferred_element_type=jnp.float32
    )
    grad_mixture = grad_mixture.astype(jnp.bfloat16).reshape(images, patches, heads_here, head_size)
    grad_attention = jnp.einsum(
        "iqhe,ikhe->ihqk", grad_mixture, value_rows, preferred_element_type=jnp.float32
    )
    grad_values = jnp.einsum(
        "ihqk,iqhe->ikhe", attention, grad_mixture, preferred_element_type=jnp.float32
    ).astype(jnp.bfloat16)
    gating_raw = jnp.sum(grad_attention * (located - content), axis=(0, 2, 3))
    mixing_grad = gating_raw * gating_flat * (1.0 - gating_flat)
    grad_scores = softmax_back(content, (1.0 - gating) * grad_attention).astype(jnp.bfloat16)
    grad_placed = jnp.sum(softmax_back(located, gating * grad_attention), axis=0)
    reach_grad = jnp.einsum("hqk,cqk->ch", grad_placed, offsets, precision=PRECISE)
    grad_queries = (
        jnp.einsum("ihqk,ikhe->iqhe", grad_scores, key_rows, preferred_element_type=jnp.float32)
        * scaling
    ).astype(jnp.bfloat16)
    grad_keys = (
        jnp.einsum("ihqk,iqhe->ikhe", grad_scores, queries, preferred_element_type=jnp.float32)
        * scaling
    ).astype(jnp.bfloat16)
    grad_projected = jnp.stack([grad_queries, grad_keys, grad_values]).reshape(
        3, all_rows, width_here
    )
    triple_grad = jnp.einsum(
        "td,ctf->cdf", first_in, grad_projected, preferred_element_type=jnp.float32
    )
    first_terms = jnp.einsum(
        "ctf,cdf->td", grad_projected, triple_low, preferred_element_type=jnp.float32
    )
    grad_first = lax.psum_scatter(first_terms, "tensor", scatter_dimension=0, tiled=True)
    grad_inner, gain_one_grad, shift_one_grad = norm_one_pull(grad_first)
    grad_input = grad_inner + grad_middle
    vector_grads = jnp.stack(
        [
            gain_one_grad,
            shift_one_grad,
            gain_two_grad,
            shift_two_grad,
            jnp.sum(grad_middle, axis=0),
            jnp.sum(incoming, axis=0),
        ]
    )
    head_grads = jnp.concatenate([reach_grad, mixing_grad[None, :]])
    matrices = (triple_grad, outward_grad, widen_grad, narrow_grad)
    return (result, grad_input, matrices, hidden_grad, head_grads, vector_grads)


def on_device(
    tokens,
    cotangent,
    keep_mask,
    triple_weight,
    outward_weight,
    widen_weight,
    narrow_weight,
    vectors,
    hidden_bias,
    head_params,
    triple_moment,
    triple_square,
    outward_moment,
    outward_square,
    widen_moment,
    widen_square,
    narrow_moment,
    narrow_square,
    vector_moment,
    vector_square,
    hidden_moment,
    hidden_square,
    head_moment,
    head_square,
):
    tensor_rank = lax.axis_index("tensor")
    data_rank = lax.axis_index("dp")
    data_count = lax.axis_size("dp")
    own_rows = tokens.shape[0]
    kept_flat = keep_mask.reshape(-1)
    row_kept = lax.dynamic_slice_in_dim(kept_flat, tensor_rank * own_rows, own_rows).astype(
        jnp.float32
    )[:, None]
    result, grad_input, matrices, hidden_grad, head_grads, vector_grads = layer_pass(
        tokens,
        cotangent,
        keep_mask,
        row_kept,
        triple_weight,
        outward_weight,
        widen_weight,
        narrow_weight,
        vectors,
        hidden_bias,
        head_params,
    )
    vector_sum = lax.psum(vector_grads, ("dp", "tensor"))
    bias_here, head_here = lax.psum((hidden_grad, head_grads), "dp")
    flattened = tuple((member.reshape(-1) for member in matrices))
    summed = lax.psum(flattened, "dp")
    shares = [
        lax.dynamic_slice_in_dim(
            member, data_rank * (member.shape[0] // data_count), member.shape[0] // data_count
        )
        for member in summed
    ]
    matrix_squares = sum((jnp.sum(member * member) for member in shares))
    head_squares = jnp.sum(bias_here * bias_here) + jnp.sum(head_here * head_here)
    partial_squares = matrix_squares + jnp.where(data_rank == 0, head_squares, 0.0)
    local_squares = jnp.sum(vector_sum * vector_sum)
    squares_all = lax.psum(partial_squares, ("dp", "tensor")) + local_squares
    grad_norm = jnp.sqrt(squares_all)
    factor = CLIP_AT / jnp.maximum(grad_norm, CLIP_AT)
    masters = (triple_weight, outward_weight, widen_weight, narrow_weight)
    states = (
        (triple_moment, triple_square),
        (outward_moment, outward_square),
        (widen_moment, widen_square),
        (narrow_moment, narrow_square),
    )
    updates = []
    for group_index in range(4):
        master = masters[group_index].reshape(-1)
        share_len = shares[group_index].shape[0]
        weight_share = lax.dynamic_slice_in_dim(master, data_rank * share_len, share_len)
        renewed = adam_update(
            weight_share,
            shares[group_index] * factor,
            states[group_index][0].reshape(-1),
            states[group_index][1].reshape(-1),
            RATES[group_index],
            DECAYS[group_index],
        )
        updates.extend([member.reshape(1, -1) for member in renewed])
    small_params = (vectors, hidden_bias, head_params)
    small_grads = (vector_sum, bias_here, head_here)
    small_states = (
        (vector_moment, vector_square),
        (hidden_moment, hidden_square),
        (head_moment, head_square),
    )
    for small_index in range(3):
        renewed = adam_update(
            small_params[small_index],
            small_grads[small_index] * factor,
            small_states[small_index][0],
            small_states[small_index][1],
            RATES[4 + small_index],
            DECAYS[4 + small_index],
        )
        updates.extend(renewed)
    return (
        result,
        grad_input,
        updates[0],
        updates[1],
        updates[2],
        updates[3],
        updates[4],
        updates[5],
        updates[6],
        updates[7],
        updates[8],
        updates[9],
        updates[10],
        updates[11],
        updates[12],
        updates[13],
        updates[14],
        updates[15],
        updates[16],
        updates[17],
        updates[18],
        updates[19],
        updates[20],
        grad_norm,
    )


def solution(mesh):
    return jax.shard_map(
        on_device,
        mesh=mesh,
        in_specs=(
            P(("dp", "tensor"), None),
            P(("dp", "tensor"), None),
            P("dp", None),
            P(None, None, "tensor"),
            P("tensor", None),
            P(None, "tensor"),
            P("tensor", None),
            P(),
            P("tensor"),
            P(None, "tensor"),
            P("tensor", "dp"),
            P("tensor", "dp"),
            P("tensor", "dp"),
            P("tensor", "dp"),
            P("tensor", "dp"),
            P("tensor", "dp"),
            P("tensor", "dp"),
            P("tensor", "dp"),
            P(),
            P(),
            P("tensor"),
            P("tensor"),
            P(None, "tensor"),
            P(None, "tensor"),
        ),
        out_specs=(
            P(("dp", "tensor"), None),
            P(("dp", "tensor"), None),
            P("tensor", "dp"),
            P("tensor", "dp"),
            P("tensor", "dp"),
            P("tensor", "dp"),
            P("tensor", "dp"),
            P("tensor", "dp"),
            P("tensor", "dp"),
            P("tensor", "dp"),
            P("tensor", "dp"),
            P("tensor", "dp"),
            P("tensor", "dp"),
            P("tensor", "dp"),
            P(),
            P(),
            P(),
            P("tensor"),
            P("tensor"),
            P("tensor"),
            P(None, "tensor"),
            P(None, "tensor"),
            P(None, "tensor"),
            P(),
        ),
        check_vma=False,
    )
```

profile of v0, /device:TPU:0, one launch (start us, length us, event | category | flops | bytes accessed | tf_op | source)
XLA Modules:
  0.0 429.3 jit_solution(14387720340846278235)
XLA Ops:
  11.3 2.2 fusion.56
  14.4 2.0 convolution_bitcast_fusion.1
  18.2 7.6 %all-gather.9.cloned.1.call-done = bf16[2,1568,192]{1,2,0:T(8,128)(2,1)} async-done(((bf16[1,1568,192]{1,2,0:T(8,128)(2,1)}), bf16[2,1568,192]{1,2,0:T(8,128)(2,1)}) %all-gather.9.cloned.1.call-update) | async-done | bytes 1204240 | tf_op jit(solution)/shard_map/all_gather | solution.py:90
  25.8 2.6 copy.92
  31.7 3.5 squeeze.11
  35.2 3.3 squeeze.12
  38.4 2.4 squeeze.10
  40.8 2.7 fusion.50
  43.5 4.4 %fusion.108 = (f32[16,2,196]{2,1,0:T(2,128)S(1)}, f32[16,2,196,196]{2,3,1,0:T(8,128)}) fusion(f32[16,2,196,196]{2,3,1,0:T(8,128)S(1)} %fusion.50, pred[16,196]{1,0:T(8,128)(4,1)S(1)} %broadcast_compare_fusion), kind=kOutput, calls=%fused_computation.204 | output fusion | flops 7376067 | bytes 9862720 | tf_op jit(solution)/shard_map/sub | solution.py:42
  48.0 12.5 %add_convert_fusion = (bf16[16,2,196,196]{2,3,1,0:T(8,128)(2,1)}, f32[16,2,196,196]{2,3,1,0:T(8,128)}) fusion(f32[2]{0:T(128)S(1)} %get-tuple-element.68, f32[2]{0:T(128)S(1)} %broadcast_subtract_fusion.2, f32[16,2,196,196]{2,3,1,0:T(8,128)} %get-tuple-element.85, f32[16,2,196]{2,1,0:T(2,128)S(1)} %get-tuple-element.84, f32[2,196,196]{1,2,0:T(8,128)} %copy.96, ...), kind=kOutput, calls=%fused_computation.15 | output fusion | flops 11076742 | bytes 12628688 | tf_op jit(solution)/shard_map/div | solution.py:43
  60.5 2.7 fusion.33
  65.7 2.3 fusion.73
  68.1 12.2 %reduce-scatter.13.cloned.1.call-done = f32[1568,192]{1,0:T(8,128)} async-done(((f32[3136,192]{1,0:T(8,128)}), f32[1568,192]{1,0:T(8,128)}) %reduce-scatter.13.cloned.1.call-update) | async-done | bytes 1204240
  80.3 3.0 copy.125
  86.4 2.1 fusion.55
  88.5 8.3 %all-gather.11.cloned.1.call-done = bf16[2,1568,192]{1,2,0:T(8,128)(2,1)} async-done(((bf16[1,1568,192]{1,2,0:T(8,128)(2,1)}), bf16[2,1568,192]{1,2,0:T(8,128)(2,1)}) %all-gather.11.cloned.1.call-update) | async-done | bytes 1204240 | tf_op jit(solution)/shard_map/all_gather | solution.py:119
  96.9 3.7 copy.100
  100.5 3.8 reshape.502
  104.3 14.3 %multiply_convert_fusion.1 = (bf16[3136,384]{1,0:T(8,128)(2,1)S(1)}, f32[3136,384]{1,0:T(8,128)}, f32[3136,384]{1,0:T(8,128)}) fusion(f32[384]{0:T(512)S(1)} %copy-done.65, bf16[3136,192]{0,1:T(8,128)(2,1)} %reshape.502, f32[192,384]{1,0:T(8,128)S(1)} %copy-done.21), kind=kOutput, calls=%fused_computation.25 | convolution fusion | flops 541974528 | bytes 13542912 | tf_op jit(solution)/shard_map/dot_general | solution.py:121
  120.0 2.1 convolution_convert_fusion
  122.1 2.6 copy.126
  125.0 3.7 copy.101
  128.7 3.8 reshape.504
  132.4 7.5 %fusion.109 = (f32[384]{0:T(512)}, bf16[3136,384]{1,0:T(8,128)(2,1)S(1)}) fusion(f32[3136,384]{1,0:T(8,128)} %get-tuple-element.65, f32[3136,384]{1,0:T(8,128)} %get-tuple-element.88, bf16[3136,192]{0,1:T(8,128)(2,1)} %reshape.504, f32[384,192]{0,1:T(8,128)} %param.30), kind=kOutput, calls=%fused_computation.205 | convolution fusion | flops 480558720 | bytes 13542912 | tf_op jit(solution)/shard_map/td,fd->tf/dot_general | solution.py:136
  141.3 2.7 fusion.45
  144.1 2.2 copy.127
  146.4 10.0 %reduce-scatter.17.cloned.1.call-done = f32[1568,192]{1,0:T(8,128)} async-done(((f32[3136,192]{1,0:T(8,128)}), f32[1568,192]{1,0:T(8,128)}) %reduce-scatter.17.cloned.1.call-update) | async-done | bytes 1204240
  156.3 3.0 copy.129
  159.3 2.3 multiply_reduce_fusion.4
  161.6 2.7 fusion.101
  168.6 3.0 fusion.43
  172.4 2.2 fusion.113
  177.1 2.6 copy.102
  181.8 3.5 reshape.474
  185.3 4.0 fusion.34
  189.3 7.8 %fusion = f32[16,2,196,196]{2,3,1,0:T(8,128)} fusion(f32[16,2,196,196]{2,3,1,0:T(8,128)} %get-tuple-element.87, f32[2]{0:T(128)} %copy-done.63, bf16[16,196,2,48]{1,0,3,2:T(8,128)(2,1)S(1)} %reshape.474, bf16[16,196,2,48]{1,0,3,2:T(8,128)(2,1)S(1)} %copy-done.7), kind=kOutput, calls=%fused_computation | convolution fusion | flops 120479040 | bytes 11038728 | tf_op jit(solution)/shard_map/sub | solution.py:47
  197.1 10.6 %multiply_reduce_fusion = (f32[2]{0:T(128)}, f32[16,2,196]{2,1,0:T(2,128)S(1)}, f32[2,196,196]{1,2,0:T(8,128)}, f32[16,2,196,196]{2,3,1,0:T(8,128)S(1)}) fusion(f32[16,2,196,196]{2,3,1,0:T(8,128)} %get-tuple-element.87, f32[16,2,196,196]{2,3,1,0:T(8,128)} %get-tuple-element.85, f32[16,2,196]{2,1,0:T(2,128)} %copy-done.41, f32[2]{0:T(128)} %copy-done.73, ...), kind=kOutput, calls=%fused_computation.9 | convolution fusion | flops 131453280 | bytes 21230744 | tf_op jit(solution)/shard_map/iqhe,ikhe->ihqk/dot_general | solution.py:154
  207.7 4.8 %multiply_convert_fusion = bf16[16,2,196,196]{2,3,1,0:T(8,128)(2,1)S(1)} fusion(f32[16,2,196,196]{2,3,1,0:T(8,128)S(1)} %get-tuple-element.89, f32[16,2,196]{2,1,0:T(2,128)S(1)} %get-tuple-element.25, f32[2]{0:T(128)S(1)} %copy-done.74, f32[16,2,196,196]{2,3,1,0:T(8,128)} %get-tuple-element.85, f32[16,2,196]{2,1,0:T(2,128)S(1)} %copy-done.42), kind=kLoop, calls=%fused_computation.13 | loop fusion | flops 6146560 | bytes 12343304 | tf_op jit(solution)/shard_map/convert_element_type | solution.py:162
  216.4 2.0 stack.34
  218.9 2.0 stack.33
  229.7 2.9 convolution_bitcast_fusion
  241.1 4.9 %convolution_bitcast_fusion.3 = f32[3,2]{0,1:T(2,128)S(1)} fusion(f32[2,196,196]{2,0,1:T(2,128)S(1)} %copy.116, f32[1,196,196]{2,0,1:T(1,128)} %copy-done.31, f32[1,196,196]{2,0,1:T(1,128)} %copy-done.32, f32[1,196,196]{2,0,1:T(1,128)} %copy-done.30), kind=kOutput, calls=%fused_computation.91 | convolution fusion | flops 2996448 | bytes 768344 | tf_op jit(solution)/shard_map/hqk,cqk->ch/dot_general | solution.py:164
  246.0 41.9 %all-reduce.1 = (f32[384]{0:T(512)S(1)}, f32[4,2]{0,1:T(2,128)S(1)}) all-reduce(f32[384]{0:T(512)S(1)} %copy-done.64, f32[4,2]{0,1:T(2,128)S(1)} %pad_maximum_fusion.3), channel_id=1, replica_groups=mesh['dp'=16,'tensor'=2] {'dp'}, use_global_device_ids=true, to_apply=%region_26.27 | all-reduce | flops 392 | bytes 3136 | tf_op jit(solution)/shard_map/psum | solution.py:248
  290.5 52.0 %all-reduce.5.cloned.1.call-done = (f32[55296]{0:T(1024)}, f32[18432]{0:T(1024)}, f32[73728]{0:T(1024)}, f32[73728]{0:T(1024)}) async-done(((f32[55296]{0:T(1024)}, f32[18432]{0:T(1024)}, f32[73728]{0:T(1024)}, f32[73728]{0:T(1024)}), (f32[55296]{0:T(1024)}, f32[18432]{0:T(1024)}, f32[73728]{0:T(1024)}, f32[73728]{0:T(1024)})) %all-reduce.5.cloned.1.call-update) | async-done | bytes 884752 | tf_op jit(solution)/shard_map/psum | solution.py:250
  350.8 4.2 reduce-scatter.19.cloned.1.call-done
  357.2 2.0 fusion.37
  359.3 3.1 fusion.41
  366.1 40.7 %all-reduce = (f32[]{:T(128)}, f32[6,192]{1,0:T(8,128)S(1)}) all-reduce(f32[]{:T(128)S(6)} %add.317, f32[6,192]{1,0:T(8,128)S(1)} %stack.38), channel_id=1, replica_groups=mesh['dp'=16,'tensor'=2] {'dp','tensor'}, use_global_device_ids=true, to_apply=%region_33.34 | all-reduce | flops 1153 | bytes 9224 | tf_op jit(solution)/shard_map/psum | solution.py:261
  (265 shorter events, 75.7 us)
Async XLA Ops:
  7.2 18.6 %all-gather.9.cloned.1.call-start = ((), (), s32[]{:S(2)}) async-start(), calls=%async_computation.4 | async-start | bytes 1916928 | tf_op jit(solution)/shard_map/all_gather | solution.py:90
  13.6 66.7 %reduce-scatter.13.cloned.1.call-start = ((), (), s32[]{:S(2)}) async-start(), calls=%async_computation.8 | async-start | bytes 4816896
  13.7 16.1 %copy-start.19 = (bf16[3,192,96]{2,1,0:T(8,128)(2,1)}, bf16[3,192,96]{2,1,0:T(8,128)(2,1)S(1)}, u32[]{:S(2)}) copy-start(bf16[3,192,96]{2,1,0:T(8,128)(2,1)S(1)} %convert_element_type.112) | copy-start | bytes 331780
  14.4 15.5 %copy-start.30 = (f32[1,196,196]{2,0,1:T(1,128)}, f32[1,196,196]{2,0,1:T(1,128)S(1)}, u32[]{:S(2)}) copy-start(f32[1,196,196]{2,0,1:T(1,128)S(1)} %get-tuple-element.81) | copy-start | bytes 460996
  18.1 29.8 %copy-start.63 = (f32[2]{0:T(128)}, f32[2]{0:T(128)S(1)}, u32[]{:S(2)}) copy-start(f32[2]{0:T(128)S(1)} %get-tuple-element.68) | copy-start | bytes 28
  18.2 29.8 %copy-start.73 = (f32[2]{0:T(128)}, f32[2]{0:T(128)S(1)}, u32[]{:S(2)}) copy-start(f32[2]{0:T(128)S(1)} %broadcast_subtract_fusion.2) | copy-start | bytes 28
  40.8 19.7 %copy-start.6 = (bf16[16,196,2,48]{1,0,3,2:T(8,128)(2,1)}, bf16[16,196,2,48]{1,0,3,2:T(8,128)(2,1)S(1)}, u32[]{:S(2)}) copy-start(bf16[16,196,2,48]{1,0,3,2:T(8,128)(2,1)S(1)} %squeeze.10) | copy-start | bytes 1806340
  48.0 12.5 %copy-start.41 = (f32[16,2,196]{2,1,0:T(2,128)}, f32[16,2,196]{2,1,0:T(2,128)S(1)}, u32[]{:S(2)}) copy-start(f32[16,2,196]{2,1,0:T(2,128)S(1)} %get-tuple-element.84) | copy-start | bytes 75268
  68.0 15.3 %copy-start = (bf16[1568,192]{0,1:T(8,128)(2,1)S(1)}, bf16[1568,192]{0,1:T(8,128)(2,1)}, u32[]{:S(2)}) copy-start(bf16[1568,192]{0,1:T(8,128)(2,1)} %param.24) | copy-start | bytes 1806340
  68.0 15.3 %copy-start.58 = (f32[1,192]{1,0:T(1,128)S(1)}, f32[1,192]{1,0:T(1,128)}, u32[]{:S(2)}) copy-start(f32[1,192]{1,0:T(1,128)} %get-tuple-element.78) | copy-start | bytes 2308
  68.0 17.0 %copy-start.50 = (f32[1,192]{1,0:T(1,128)S(1)}, f32[1,192]{1,0:T(1,128)}, u32[]{:S(2)}) copy-start(f32[1,192]{1,0:T(1,128)} %get-tuple-element.77) | copy-start | bytes 2308
  68.0 17.0 %copy-start.57 = (f32[1,192]{1,0:T(1,128)S(1)}, f32[1,192]{1,0:T(1,128)}, u32[]{:S(2)}) copy-start(f32[1,192]{1,0:T(1,128)} %get-tuple-element.76) | copy-start | bytes 2308
  68.0 28.9 %all-gather.11.cloned.1.call-start = ((), (), s32[]{:S(2)}) async-start(), calls=%async_computation.5 | async-start | bytes 1916928 | tf_op jit(solution)/shard_map/all_gather | solution.py:119
  86.2 38.8 %all-gather.13.cloned.1.call-start = ((), (), s32[]{:S(2)}) async-start(), calls=%async_computation.6 | async-start | bytes 1916928 | tf_op jit(solution)/shard_map/all_gather | solution.py:132
  86.4 78.0 %copy-start.33 = (f32[1568]{0:T(1024)}, f32[1568]{0:T(1024)S(1)}, u32[]{:S(2)}) copy-start(f32[1568]{0:T(1024)S(1)} %dynamic-slice_convert_fusion) | copy-start | bytes 18820
  86.4 17.9 %copy-start.21 = (f32[192,384]{1,0:T(8,128)S(1)}, f32[192,384]{1,0:T(8,128)}, u32[]{:S(2)}) copy-start(f32[192,384]{1,0:T(8,128)} %param.29) | copy-start | bytes 884740
  86.4 17.9 %copy-start.65 = (f32[384]{0:T(512)S(1)}, f32[384]{0:T(512)}, u32[]{:S(2)}) copy-start(f32[384]{0:T(512)} %param.32) | copy-start | bytes 4612
  88.5 55.6 %reduce-scatter.15.cloned.1.call-start = ((), (), s32[]{:S(2)}) async-start(), calls=%async_computation.9 | async-start | bytes 2408448
  104.3 15.7 %copy-start.23 = (f32[384,192]{0,1:T(8,128)S(1)}, f32[384,192]{0,1:T(8,128)}, u32[]{:S(2)}) copy-start(f32[384,192]{0,1:T(8,128)} %param.30) | copy-start | bytes 884740
  124.7 31.6 %reduce-scatter.17.cloned.1.call-start = ((), (), s32[]{:S(2)}) async-start(), calls=%async_computation.10 | async-start | bytes 4816896
  144.0 15.3 %copy-start.51 = (f32[1,192]{1,0:T(1,128)S(1)}, f32[1,192]{1,0:T(1,128)}, u32[]{:S(2)}) copy-start(f32[1,192]{1,0:T(1,128)} %get-tuple-element.77) | copy-start | bytes 2308
  144.0 17.6 %copy-start.62 = (f32[1,192]{1,0:T(1,128)S(1)}, f32[1,192]{1,0:T(1,128)}, u32[]{:S(2)}) copy-start(f32[1,192]{1,0:T(1,128)} %get-tuple-element.75) | copy-start | bytes 2308
  144.0 33.1 %all-gather.15.cloned.1.call-start = ((), (), s32[]{:S(2)}) async-start(), calls=%async_computation.7 | async-start | bytes 1916928 | tf_op jit(solution)/shard_map/all_gather | solution.py:148
  166.4 176.1 %all-reduce.5.cloned.1.call-start = ((), (), s32[]{:S(2)}) async-start(), calls=%async_computation.12 | async-start | bytes 1769472 | tf_op jit(solution)/shard_map/psum | solution.py:250
  197.1 10.6 %copy-start.42 = (f32[16,2,196]{2,1,0:T(2,128)S(1)}, f32[16,2,196]{2,1,0:T(2,128)}, u32[]{:S(2)}) copy-start(f32[16,2,196]{2,1,0:T(2,128)} %copy-done.41) | copy-start | bytes 75268
  197.1 10.6 %copy-start.74 = (f32[2]{0:T(128)S(1)}, f32[2]{0:T(128)}, u32[]{:S(2)}) copy-start(f32[2]{0:T(128)} %copy-done.73) | copy-start | bytes 28
  229.5 125.5 %reduce-scatter.19.cloned.1.call-start = ((), (), s32[]{:S(2)}) async-start(), calls=%async_computation.11 | async-start | bytes 4816896
  233.6 12.3 %copy-start.61 = (f32[1,2]{0,1:T(2,128)S(1)}, f32[1,2]{0,1:T(2,128)}, u32[]{:S(2)}) copy-start(f32[1,2]{0,1:T(2,128)} %get-tuple-element.69) | copy-start | bytes 28
  233.6 12.4 %copy-start.64 = (f32[384]{0:T(512)S(1)}, f32[384]{0:T(512)}, u32[]{:S(2)}) copy-start(f32[384]{0:T(512)} %get-tuple-element.90) | copy-start | bytes 4612
  239.1 117.8 %copy-start.44 = (f32[1,192]{1,0:T(1,128)S(1)}, f32[1,192]{1,0:T(1,128)}, u32[]{:S(2)}) copy-start(f32[1,192]{1,0:T(1,128)} %copy-done.43) | copy-start | bytes 2308
  241.1 116.1 %copy-start.38 = (f32[1568]{0:T(1024)S(1)}, f32[1568]{0:T(1024)}, u32[]{:S(2)}) copy-start(f32[1568]{0:T(1024)} %copy-done.37) | copy-start | bytes 18820
  288.0 67.0 %copy-start.54 = (f32[384]{0:T(512)}, f32[384]{0:T(512)S(1)}, u32[]{:S(2)}) copy-start(f32[384]{0:T(512)S(1)} %get-tuple-element.35) | copy-start | bytes 4612
  288.0 68.9 %copy-start.71 = (f32[4,2]{0,1:T(2,128)}, f32[4,2]{0,1:T(2,128)S(1)}, u32[]{:S(2)}) copy-start(f32[4,2]{0,1:T(2,128)S(1)} %get-tuple-element.36) | copy-start | bytes 100
  350.8 8.5 %copy-start.2 = (f32[1568,192]{0,1:T(8,128)S(1)}, f32[1568,192]{0,1:T(8,128)}, u32[]{:S(2)}) copy-start(f32[1568,192]{0,1:T(8,128)} %copy-done.1) | copy-start | bytes 3612676
  350.8 8.5 %copy-start.34 = (f32[1568]{0:T(1024)S(1)}, f32[1568]{0:T(1024)}, u32[]{:S(2)}) copy-start(f32[1568]{0:T(1024)} %copy-done.33) | copy-start | bytes 18820
  350.8 8.5 %copy-start.36 = (f32[1568]{0:T(1024)S(1)}, f32[1568]{0:T(1024)}, u32[]{:S(2)}) copy-start(f32[1568]{0:T(1024)} %copy-done.35) | copy-start | bytes 18820
  359.3 57.6 %copy-start.40 = (f32[3456]{0:T(1024)S(1)}, f32[3456]{0:T(1024)}, u32[]{:S(2)}) copy-start(f32[3456]{0:T(1024)} %get-tuple-element.94) | copy-start | bytes 41476
  362.4 57.2 %copy-start.60 = (f32[4,2]{0,1:T(2,128)S(1)}, f32[4,2]{0,1:T(2,128)}, u32[]{:S(2)}) copy-start(f32[4,2]{0,1:T(2,128)} %param.33) | copy-start | bytes 100
  362.4 57.2 %copy-start.69 = (f32[4,2]{0,1:T(2,128)S(1)}, f32[4,2]{0,1:T(2,128)}, u32[]{:S(2)}) copy-start(f32[4,2]{0,1:T(2,128)} %param.47) | copy-start | bytes 100
  362.4 57.2 %copy-start.70 = (f32[4,2]{0,1:T(2,128)S(1)}, f32[4,2]{0,1:T(2,128)}, u32[]{:S(2)}) copy-start(f32[4,2]{0,1:T(2,128)} %param.46) | copy-start | bytes 100
  362.4 57.2 %copy-start.72 = (f32[4,2]{0,1:T(2,128)S(1)}, f32[4,2]{0,1:T(2,128)}, u32[]{:S(2)}) copy-start(f32[4,2]{0,1:T(2,128)} %copy-done.71) | copy-start | bytes 100
  362.4 57.8 %copy-start.55 = (f32[384]{0:T(512)S(1)}, f32[384]{0:T(512)}, u32[]{:S(2)}) copy-start(f32[384]{0:T(512)} %copy-done.54) | copy-start | bytes 4612
  362.4 57.8 %copy-start.66 = (f32[384]{0:T(512)S(1)}, f32[384]{0:T(512)}, u32[]{:S(2)}) copy-start(f32[384]{0:T(512)} %param.32) | copy-start | bytes 4612
  362.4 57.8 %copy-start.67 = (f32[384]{0:T(512)S(1)}, f32[384]{0:T(512)}, u32[]{:S(2)}) copy-start(f32[384]{0:T(512)} %param.45) | copy-start | bytes 4612
  362.4 57.8 %copy-start.68 = (f32[384]{0:T(512)S(1)}, f32[384]{0:T(512)}, u32[]{:S(2)}) copy-start(f32[384]{0:T(512)} %param.44) | copy-start | bytes 4612
  362.4 58.4 %copy-start.45 = (f32[6,192]{1,0:T(8,128)S(1)}, f32[6,192]{1,0:T(8,128)}, u32[]{:S(2)}) copy-start(f32[6,192]{1,0:T(8,128)} %param.31) | copy-start | bytes 13828
  362.4 58.4 %copy-start.52 = (f32[6,192]{1,0:T(8,128)S(1)}, f32[6,192]{1,0:T(8,128)}, u32[]{:S(2)}) copy-start(f32[6,192]{1,0:T(8,128)} %param.43) | copy-start | bytes 13828
  362.4 58.3 %copy-start.53 = (f32[6,192]{1,0:T(8,128)S(1)}, f32[6,192]{1,0:T(8,128)}, u32[]{:S(2)}) copy-start(f32[6,192]{1,0:T(8,128)} %param.42) | copy-start | bytes 13828
  (36 other events, 150.6 us)
Sparse Core Ops, SparseCore 0:
  13.7 12.0 all-gather.8
  68.1 12.1 reduce-scatter.12
  86.3 10.5 all-gather.10
  98.9 10.5 all-gather.12
  124.8 10.2 reduce-scatter.14
  144.1 12.1 reduce-scatter.16
  166.6 10.5 all-gather.14
  229.6 112.8 all-reduce.4
  344.8 10.1 reduce-scatter.18
where the time goes:
time: 436 us; the launch traced here: 429 us
  waiting for transfers between devices  96.1 us (22%)
  local copies, waits for them, and re-layouts  87 us (20%)
  blocking collectives  82.6 us (19%)
  matrix products  78.3 us (18%)
  other arithmetic  62.5 us (14%)
  between operations  21.6 us (5%)
    psum x1, waiting for transfers between devices, on_device(): summed = lax.psum(flattened, 'dp')  52 us
    psum x1, blocking collectives, on_device(): bias_here, head_here = lax.psum((hidden_grad, head_grads), 'dp')  41.9 us
    psum x1, blocking collectives, on_device(): squares_all = lax.psum(partial_squares, ('dp', 'tensor')) + local_squares  40.7 us
    unnamed x163, local copies, waits for them, and re-layouts  32.7 us
    unnamed x13, waiting for transfers between devices  26.5 us
    dot_general x1, matrix products, layer_pass(): jnp.dot(second_in, widen_low, preferred_element_type=jnp.float32)  14.3 us
    div x1, other arithmetic, masked_softmax(): return exponent / jnp.sum(exponent, axis=-1, keepdims=True)  12.5 us
    dot_general x1, matrix products, layer_pass(): jnp.einsum('iqhe,ikhe->ihqk', grad_mixture, value_rows, preferred_element...  10.6 us
  transfers between devices with their start and end apart: 9, of which 7 were waited for; matrix products, arithmetic and copies ran while one was open for 20% of the time, Pallas kernels for 0%

commit v1 on v0

v1 whole, which is shorter than its diff:
```python
import functools
import math

import jax
import jax.numpy as jnp
from jax import lax
from jax.experimental import pallas as pl
from jax.experimental.pallas import tpu as pltpu
from jax.sharding import PartitionSpec as P

GRID = 14
STEP = 10
EPS_NORM = 1e-06
CLIP_AT = 1.0
BETA_ONE = 0.9
BETA_TWO = 0.95
ADAM_EPS = 1e-08
RATES = (0.1, 0.5, 0.1, 0.05, 0.3, 0.1, 0.3)
DECAYS = (0.05, 0.05, 0.05, 0.05, 0.0, 0.0, 0.0)
LOG2E = 1.4426950408889634
BF = jnp.bfloat16
F32 = jnp.float32
VMEM_LIMIT = 56 * 1024 * 1024
EARLY_ROWS = 96
LATE_ROWS = 32
VM = pl.BlockSpec(memory_space=pltpu.VMEM)
SM = pl.BlockSpec(memory_space=pltpu.SMEM)
PARAMS = pltpu.CompilerParams(vmem_limit_bytes=VMEM_LIMIT)


def sds(*dims, dtype=F32):
    return jax.ShapeDtypeStruct(dims, dtype)


def nn(a, b):
    return lax.dot_general(a, b, (((1,), (0,)), ((), ())), preferred_element_type=F32)


def nt(a, b):
    return lax.dot_general(a, b, (((1,), (1,)), ((), ())), preferred_element_type=F32)


def norm_parts(v):
    width = v.shape[-1]
    average = jnp.sum(v, axis=-1, keepdims=True) * (1.0 / width)
    centred = v - average
    variance = jnp.sum(centred * centred, axis=-1, keepdims=True) * (1.0 / width)
    spread = lax.rsqrt(variance + EPS_NORM)
    return centred * spread, spread


def norm_back(e, n, spread):
    width = e.shape[-1]
    mean_e = jnp.sum(e, axis=-1, keepdims=True) * (1.0 / width)
    mean_en = jnp.sum(e * n, axis=-1, keepdims=True) * (1.0 / width)
    return spread * (e - mean_e - n * mean_en)


def fold(v):
    rows = v.shape[0]
    return jnp.sum(v.reshape(rows // 8, 8, v.shape[1]), axis=0)


def gelu_parts(x):
    y = jnp.abs(x)
    t = 1.0 / (1.0 + (0.3275911 / math.sqrt(2.0)) * y)
    e = jnp.exp2((x * x) * (-0.5 * LOG2E))
    poly = t * (
        0.5 * 0.254829592
        + t
        * (
            0.5 * -0.284496736
            + t * (0.5 * 1.421413741 + t * (0.5 * -1.453152027 + t * (0.5 * 1.061405429)))
        )
    )
    q = poly * e
    phi = jnp.where(x > 0.0, 1.0 - q, q)
    return x * phi, phi + x * (e * (1.0 / math.sqrt(2.0 * math.pi)))


def offsets(kp, qp):
    def side(dim):
        at = lax.broadcasted_iota(jnp.int32, (kp, qp), dim).astype(F32)
        row = jnp.floor((at + 0.5) * (1.0 / GRID))
        return at - row * GRID, row

    kc, kr = side(0)
    qc, qr = side(1)
    a = kc - qc
    b = kr - qr
    return a, b, a * a + b * b


def head_mask(rows, width, hd, h):
    lane = lax.broadcasted_iota(jnp.int32, (rows, width), 1)
    return ((lane >= h * hd) & (lane < (h + 1) * hd)).astype(BF)


def gate_of(hp_ref, h, lanes):
    return 1.0 / (1.0 + jnp.exp(-jnp.broadcast_to(hp_ref[h : h + 1, 3:4], (1, lanes))))


def fill_places(place, hp_ref, heads, kp, qp):
    parts = offsets(kp, qp)
    for h in range(heads):
        place[h] = LOG2E * sum(
            jnp.broadcast_to(hp_ref[h : h + 1, at : at + 1], (kp, qp)) * parts[at] for at in range(3)
        )
    return parts


def pair_rows(j, patches, kp):
    return pl.ds(pl.multiple_of(j * 2 * patches, 8), patches + kp + (-(patches + kp)) % 8)


def put_planes(ref, value):
    width = value.shape[1]
    ref[0] = value[:, :128]
    ref[1, :, 0 : width - 128] = value[:, 128:]


def even_odd_tiles(ref, start, pairs):
    even = [ref[at, pl.ds(start, pairs, stride=2), :] for at in range(2)]
    odd = [ref[at, pl.ds(start + 1, pairs, stride=2), :] for at in range(2)]
    return (
        even[0],
        jnp.concatenate([even[1][:, :64], odd[0][:, :64]], axis=1),
        jnp.concatenate([odd[0][:, 64:], odd[1][:, :64]], axis=1),
    )


def four_row_tiles(ref, plane, start, groups):
    r = [ref[plane, pl.ds(start + at, groups, stride=4), :] for at in range(4)]
    return (
        jnp.concatenate([r[0][:, :96], r[1][:, :32]], axis=1),
        jnp.concatenate([r[1][:, 32:96], r[2][:, :64]], axis=1),
        jnp.concatenate([r[2][:, 64:96], r[3][:, :96]], axis=1),
    )


def pack_kernel(tri_ref, out_ref, wid_ref, nar_ref, hb_ref, hp_ref, pack_ref):
    depth, wide = wid_ref.shape
    pack_ref[0:depth, :] = wid_ref[...].astype(BF)
    pack_ref[depth : 2 * depth, :] = nar_ref[...].astype(BF)
    pack_ref[2 * depth : 3 * depth, :] = jnp.concatenate(
        [tri_ref[0], tri_ref[1], tri_ref[2], out_ref[...].T], axis=1
    ).astype(BF)
    heads_here = hp_ref.shape[0]
    hp = jnp.concatenate([hp_ref[...], jnp.zeros((heads_here, wide - 4), F32)], axis=1)
    left = jnp.concatenate([hb_ref[...], hp], axis=0)
    parts = []
    for _ in range(3):
        part = left.astype(BF).astype(F32)
        parts.append(part)
        left = left - part
    parts.append(jnp.zeros((16 - 3 * (1 + heads_here), wide), F32))
    pack_ref[3 * depth : 3 * depth + 16, :] = jnp.concatenate(parts, axis=0).astype(BF)


def run_pack(tri, out, wid, nar_t, hb, hp_t):
    depth, wide = wid.shape
    return pl.pallas_call(
        pack_kernel,
        out_shape=sds(3 * depth + 16, wide, dtype=BF),
        in_specs=[VM] * 6,
        out_specs=VM,
        compiler_params=PARAMS,
        name="pack_weights",
    )(tri, out, wid, nar_t, hb, hp_t)


def forward_kernel(*refs, patches, heads, data_count):
    (rank_ref, tok_ref, cot_ref, keep_ref, own_ref, oth_ref, vec_ref) = refs[:7]
    (res_ref, gm_ref, first_ref, q_ref, k_ref, v_ref, kt_ref, dm_ref, lse_ref, hp_ref) = refs[7:17]
    outs = refs[17:22] if not data_count else refs[17:18]
    (xs, cs, wq, wk, wv, wkt, wvt, wo, wi, wn, place, act_s, low_s, inc_s, sec_s, og) = refs[
        17 + len(outs) : 33 + len(outs)
    ]
    if data_count:
        nar_p, out_p, wid_g, vec_g, hid_g, tmp = refs[33 + len(outs) :]
    else:
        nar_g, wid_g, out_g, vec_g, hid_g = outs
    images, kp, _ = keep_ref.shape
    qp = lse_ref.shape[2]
    rows = images * patches
    width = tok_ref.shape[1]
    hd = width // heads
    half = width // 2
    half_heads = heads // 2
    wide = own_ref.shape[1]
    c_scale = LOG2E / math.sqrt(hd)
    xs[pl.ds(0, rows), :] = tok_ref[...].astype(F32)
    cs[pl.ds(0, rows), :] = cot_ref[...].astype(F32)
    xs[pl.ds(rows, 16), :] = jnp.zeros((16, width), F32)
    cs[pl.ds(rows, 16), :] = jnp.zeros((16, width), F32)
    wi[:, pl.ds(0, wide)] = own_ref[0:width, :]
    wi[:, pl.ds(wide, wide)] = oth_ref[0:width, :]
    wn[:, pl.ds(0, wide)] = own_ref[width : 2 * width, :]
    wn[:, pl.ds(wide, wide)] = oth_ref[width : 2 * width, :]
    own_tri = own_ref[2 * width : 3 * width, :]
    oth_tri = oth_ref[2 * width : 3 * width, :]
    for at, w in enumerate((wq, wk, wv, wo)):
        span = slice(at * half, (at + 1) * half)
        w[...] = jnp.concatenate([own_tri[:, span], oth_tri[:, span]], axis=1)
    wkt[...] = wk[...].T
    wvt[...] = wv[...].T
    small = []
    for ref in (own_ref, oth_ref):
        tail = ref[3 * width : 3 * width + 16, :].astype(F32)
        step = 1 + half_heads
        small.append(tail[0:step] + tail[step : 2 * step] + tail[2 * step : 3 * step])
    hb = jnp.concatenate([member[0:1] for member in small], axis=1)
    hp_ref[...] = jnp.concatenate(
        [member[1:, :128] for member in small] + [jnp.zeros((8 - heads, 128), F32)], axis=0
    )
    fill_places(place, hp_ref, heads, kp, qp)
    hid_g[...] = jnp.zeros_like(hid_g)
    vec_g[...] = jnp.zeros_like(vec_g)
    og[...] = jnp.zeros_like(og)
    v = [vec_ref[at : at + 1, :] for at in range(6)]

    def image(i, x, cot):
        keep = keep_ref[i]
        bias = (keep - 1.0) * 1e30
        bias2 = jnp.concatenate([bias, bias], axis=1)
        keep_w = jnp.concatenate([keep, keep[:, : width - 128]], axis=1)
        n1, _ = norm_parts(x)
        first = (n1 * v[0] + v[1]).astype(BF)
        first_ref[i] = first
        first_q = jnp.concatenate([first, jnp.zeros((qp - kp, width), BF)], axis=0)
        queries = nn(first_q, wq[...]).astype(BF)
        keys = nn(first, wk[...]).astype(BF)
        values = nn(first, wv[...]).astype(BF)
        keys_t = nt(wkt[...], first_q).astype(BF)
        values_t = nt(wvt[...], first_q).astype(BF)
        q_ref[i] = queries
        k_ref[i] = keys
        v_ref[i] = values
        kt_ref[i] = keys_t
        mixed = []
        for h in range(heads):
            gate = gate_of(hp_ref, h, qp)
            qm = queries * head_mask(qp, width, hd, h)
            s = nt(keys, qm) * c_scale + bias2
            m = jnp.max(s, axis=0, keepdims=True)
            e = jnp.exp2(s - m)
            z = jnp.sum(e, axis=0, keepdims=True)
            p = place[h] + bias2
            pm = jnp.max(p, axis=0, keepdims=True)
            pe = jnp.exp2(p - pm)
            pz = jnp.sum(pe, axis=0, keepdims=True)
            att = (e * ((1.0 - gate) / z) + pe * (gate / pz)).astype(BF)
            lse_ref[i, h : h + 1, :] = m + jnp.log2(z / (1.0 - gate))
            lse_ref[i, heads + h : heads + h + 1, :] = pm + jnp.log2(pz / gate)
            att_k = jnp.concatenate([att, jnp.zeros((qp - kp, qp), BF)], axis=0)
            mixed.append(nn(values_t[h * hd : (h + 1) * hd, :], att_k))
        mix_t = jnp.concatenate(mixed, axis=0)
        mix = mix_t.T[:kp].astype(BF)
        middle = x + nt(mix, wo[...]) + v[4]
        n2, spread2 = norm_parts(middle)
        second = (n2 * v[2] + v[3]).astype(BF)
        before = nn(second, wi[...]) + hb
        gelu, slope = gelu_parts(before)
        act = gelu.astype(BF)
        result = middle + nt(act, wn[...]) + v[5]
        incoming = cot * keep_w
        inc_low = incoming.astype(BF)
        grad_before = nn(inc_low, wn[...]) * slope
        hid_g[...] += fold(grad_before)
        grad_low = grad_before.astype(BF)
        grad_second = nt(grad_low, wi[...])
        grad_middle = incoming + norm_back(grad_second * v[2], n2, spread2)
        vec_g[0] += fold(grad_second * n2)
        vec_g[1] += fold(grad_second)
        vec_g[2] += fold(grad_middle)
        vec_g[3] += fold(incoming)
        gm_ref[i] = grad_middle
        mid_low = jnp.concatenate(
            [grad_middle.astype(BF), jnp.zeros((qp - kp, width), BF)], axis=0
        )
        dm_ref[i] = nn(mid_low, wo[...]).astype(BF)
        og[...] += nn(mix_t.astype(BF), mid_low)
        span = pl.ds(pl.multiple_of(i * kp, 16), kp)
        act_s[span, :] = act
        low_s[span, :] = grad_low
        inc_s[span, :] = inc_low
        sec_s[span, :] = second
        return result

    def body(j, carry):
        x = xs[pair_rows(j, patches, kp), :]
        cot = cs[pair_rows(j, patches, kp), :]
        done = [
            image(
                2 * j + at,
                x[at * patches : at * patches + kp],
                cot[at * patches : at * patches + kp],
            )
            for at in range(2)
        ]
        res_ref[pl.ds(pl.multiple_of(j * 2 * patches, 8), 2 * patches), :] = jnp.concatenate(
            [member[:patches] for member in done], axis=0
        )
        return carry

    lax.fori_loop(0, images // 2, body, 0)
    narrow = nn(inc_s[...].T, act_s[...]).T
    wid_g[...] = nn(sec_s[...].T, low_s[...])
    if not data_count:
        nar_g[...] = narrow
        out_g[...] = og[...]
        return
    put_planes(nar_p, narrow)
    put_planes(out_p, og[...])
    chunk_ref = outs[0]
    tmp[...] = jnp.zeros_like(tmp)
    early = jnp.sum(vec_g[...], axis=1)
    hidden = jnp.sum(hid_g[...], axis=0, keepdims=True)
    rest = width - 128
    wp, np_, op = width // data_count, wide // data_count // 2, half // data_count // 2
    at = 3 * (wp + np_ + op)
    for side in range(2):
        for slot in range(2):
            tmp[2 * side + slot, at : at + 4, :] = early[:, :128]
            tmp[2 * side + slot, at + 4 : at + 8, 0:rest] = early[:, 128:]
            for k in range(3):
                lane = side * wide + 128 * k
                tmp[2 * side + slot, at + 8 + k : at + 9 + k, :] = hidden[:, lane : lane + 128]
    rank = rank_ref[0]
    for r in range(data_count):
        for side in range(2):
            piece = tmp.at[2 * side + r % 2]
            for k in range(3):
                lane = side * wide + 128 * k
                piece[k * wp : (k + 1) * wp, :] = wid_g[r * wp : (r + 1) * wp, lane : lane + 128]
            base = 3 * wp
            tiles = even_odd_tiles(nar_p, side * wide + 2 * np_ * r, np_)
            for k in range(3):
                piece[base + k * np_ : base + (k + 1) * np_, :] = tiles[k]
            base += 3 * np_
            tiles = even_odd_tiles(out_p, side * half + 2 * op * r, op)
            for k in range(3):
                piece[base + k * op : base + (k + 1) * op, :] = tiles[k]
            chunk_ref[2 * r + (rank + side) % 2] = piece[...].astype(BF)


def run_forward(rank, tok, cot, keep, own, oth, vec, heads, patches, data_count):
    images, kp, _ = keep.shape
    qp = -(-patches // 128) * 128
    width = tok.shape[1]
    hidden = 2 * own.shape[1]
    rows = images * patches
    full = images * kp
    sums = [
        sds(hidden, width),
        sds(width, hidden),
        sds(width, width),
        sds(4, 8, width),
        sds(8, hidden),
    ]
    scratch = [
        pltpu.VMEM((rows + 16, width), F32),
        pltpu.VMEM((rows + 16, width), F32),
        *[pltpu.VMEM((width, width), BF)] * 6,
        pltpu.VMEM((width, hidden), BF),
        pltpu.VMEM((width, hidden), BF),
        pltpu.VMEM((heads, kp, qp), F32),
        pltpu.VMEM((full, hidden), BF),
        pltpu.VMEM((full, hidden), BF),
        pltpu.VMEM((full, width), BF),
        pltpu.VMEM((full, width), BF),
        pltpu.VMEM((width, width), F32),
    ]
    if data_count:
        outs = [sds(2 * data_count, EARLY_ROWS, 128, dtype=BF)]
        scratch += [pltpu.VMEM((2, hidden, 128), F32), pltpu.VMEM((2, width, 128), F32)]
        scratch += [pltpu.VMEM(sums[at].shape, F32) for at in (1, 3, 4)]
        scratch.append(pltpu.VMEM((4, EARLY_ROWS, 128), F32))
    else:
        outs = sums
    return pl.pallas_call(
        functools.partial(forward_kernel, patches=patches, heads=heads, data_count=data_count),
        out_shape=(
            sds(rows, width),
            sds(images, kp, width),
            sds(images, kp, width, dtype=BF),
            sds(images, qp, width, dtype=BF),
            sds(images, kp, width, dtype=BF),
            sds(images, kp, width, dtype=BF),
            sds(images, width, qp, dtype=BF),
            sds(images, qp, width, dtype=BF),
            sds(images, 2 * heads, qp),
            sds(8, 128),
            *outs,
        ),
        in_specs=[SM] + [VM] * 6,
        out_specs=(VM,) * (10 + len(outs)),
        scratch_shapes=scratch,
        compiler_params=PARAMS,
        name="forward",
    )(rank, tok, cot, keep, own, oth, vec)


def backward_kernel(*refs, patches, heads, data_count):
    (rank_ref, hp_ref, keep_ref, first_ref, q_ref, k_ref, v_ref, kt_ref, dm_ref, lse_ref) = refs[:10]
    (dp_ref, head_ref, tri_out) = refs[10:13]
    (place, place_g, gate_g, first_s, dp_s) = refs[13:18]
    images, kp, _ = keep_ref.shape
    qp = lse_ref.shape[2]
    width = first_ref.shape[2]
    hd = width // heads
    half = width // 2
    c_scale = LOG2E / math.sqrt(hd)
    back_scale = 1.0 / math.sqrt(hd)
    parts = fill_places(place, hp_ref, heads, kp, qp)
    place_g[...] = jnp.zeros_like(place_g)
    gate_g[...] = jnp.zeros_like(gate_g)

    def body(i, carry):
        keep = keep_ref[i]
        bias = (keep - 1.0) * 1e30
        bias2 = jnp.concatenate([bias, bias], axis=1)
        queries, keys, values, keys_t, dm = q_ref[i], k_ref[i], v_ref[i], kt_ref[i], dm_ref[i]
        dq_t = []
        dk = jnp.zeros((kp, width), F32)
        dv = jnp.zeros((kp, width), F32)
        for h in range(heads):
            gate = gate_of(hp_ref, h, qp)
            mask = head_mask(qp, width, hd, h)
            qm = queries * mask
            dmm = dm * mask
            s = nt(keys, qm) * c_scale + bias2
            c = jnp.exp2(s - lse_ref[i, h : h + 1, :])
            l = jnp.exp2(place[h] + bias2 - lse_ref[i, heads + h : heads + h + 1, :])
            att = (c + l).astype(BF)
            da = nt(values, dmm)
            pc = c * da
            pt = l * da
            rc = jnp.sum(pc, axis=0, keepdims=True) / (1.0 - gate)
            rl = jnp.sum(pt, axis=0, keepdims=True) / gate
            ds = (pc - c * rc).astype(BF)
            place_g[h] += pt - l * rl
            gate_g[h : h + 1, :] += rl - rc
            dv = dv + nn(att, dmm)
            dk = dk + nn(ds, qm)
            ds_k = jnp.concatenate([ds, jnp.zeros((qp - kp, qp), BF)], axis=0)
            dq_t.append(nn(keys_t[h * hd : (h + 1) * hd, :], ds_k))
        dq = (jnp.concatenate(dq_t, axis=0) * back_scale).T[:kp]
        span = pl.ds(pl.multiple_of(i * kp, 16), kp)
        for at, d in enumerate((dq, dk * back_scale, dv)):
            low = d.astype(BF)
            dp_ref[at, i] = low
            dp_s[at, span, :] = low
        first_s[span, :] = first_ref[i]
        return carry

    lax.fori_loop(0, images, body, 0)
    first_t = first_s[...].T
    for at in range(3):
        part = nn(first_t, dp_s[at])
        rows = pl.ds(at * width, width)
        if data_count:
            tri_s = refs[18]
            tri_s[0, rows, 0:half] = part[:, :half]
            tri_s[1, rows, 0:half] = part[:, half:]
        else:
            tri_out[rows, :] = part
    rank = rank_ref[0]
    lane = lax.broadcasted_iota(jnp.int32, (1, 128), 1)
    row = jnp.zeros((1, 128), F32)
    half_heads = heads // 2
    for h in range(heads):
        base = ((rank + h // half_heads) % 2) * (4 * half_heads) + h % half_heads
        g = place_g[h]
        for at in range(3):
            row = row + jnp.where(lane == base + at * half_heads, jnp.sum(g * parts[at]), 0.0)
        gate = gate_of(hp_ref, h, 128)
        total = jnp.sum(gate_g[h : h + 1, :])
        row = row + jnp.where(lane == base + 3 * half_heads, total * gate * (1.0 - gate), 0.0)
    head_ref[...] = row
    if not data_count:
        return
    tmp = refs[19]
    tmp[...] = jnp.zeros_like(tmp)
    groups = 3 * width // data_count // 4
    for r in range(data_count):
        for side in range(2):
            piece = tmp.at[2 * side + r % 2]
            tiles = four_row_tiles(tri_s, side, 4 * groups * r, groups)
            for k in range(3):
                piece[k * groups : (k + 1) * groups, :] = tiles[k]
            tri_out[2 * r + (rank + side) % 2] = piece[...].astype(BF)


def run_backward(rank, hp, keep, first, q, k, v, kt, dm, lse, heads, patches, data_count):
    images, kp, _ = keep.shape
    qp = lse.shape[2]
    width = first.shape[2]
    full = images * kp
    scratch = [
        pltpu.VMEM((heads, kp, qp), F32),
        pltpu.VMEM((heads, kp, qp), F32),
        pltpu.VMEM((8, qp), F32),
        pltpu.VMEM((full, width), BF),
        pltpu.VMEM((3, full, width), BF),
    ]
    if data_count:
        last = sds(2 * data_count, LATE_ROWS, 128, dtype=BF)
        scratch += [pltpu.VMEM((2, 3 * width, 128), F32), pltpu.VMEM((4, LATE_ROWS, 128), F32)]
    else:
        last = sds(3 * width, width)
    return pl.pallas_call(
        functools.partial(backward_kernel, patches=patches, heads=heads, data_count=data_count),
        out_shape=(sds(3, images, kp, width, dtype=BF), sds(1, 128), last),
        in_specs=[SM] + [VM] * 9,
        out_specs=(VM,) * 3,
        scratch_shapes=scratch,
        compiler_params=PARAMS,
        name="attention_backward",
    )(rank, hp, keep, first, q, k, v, kt, dm, lse)


def input_kernel(tok_ref, gm_ref, dp_ref, own_ref, oth_ref, vec_ref, gi_ref, vec_out, xs, w, vec_g, *, patches):
    images, kp, width = gm_ref.shape
    rows = images * patches
    half = width // 2
    xs[pl.ds(0, rows), :] = tok_ref[...].astype(F32)
    xs[pl.ds(rows, 16), :] = jnp.zeros((16, width), F32)
    own_tri = own_ref[2 * width : 3 * width, :]
    oth_tri = oth_ref[2 * width : 3 * width, :]
    for at in range(3):
        span = slice(at * half, (at + 1) * half)
        w[at] = jnp.concatenate([own_tri[:, span], oth_tri[:, span]], axis=1)
    vec_g[...] = jnp.zeros_like(vec_g)
    gain = vec_ref[0:1, :]

    def image(i, x):
        n1, spread = norm_parts(x)
        g = nt(dp_ref[0, i], w[0]) + nt(dp_ref[1, i], w[1]) + nt(dp_ref[2, i], w[2])
        vec_g[0] += fold(g * n1)
        vec_g[1] += fold(g)
        return gm_ref[i] + norm_back(g * gain, n1, spread)

    def body(j, carry):
        x = xs[pair_rows(j, patches, kp), :]
        done = [image(2 * j + at, x[at * patches : at * patches + kp]) for at in range(2)]
        gi_ref[pl.ds(pl.multiple_of(j * 2 * patches, 8), 2 * patches), :] = jnp.concatenate(
            [member[:patches] for member in done], axis=0
        )
        return carry

    lax.fori_loop(0, images // 2, body, 0)
    vec_out[...] = jnp.sum(vec_g[...], axis=1)


def run_input(tok, gm, dp, own, oth, vec, patches):
    images, kp, width = gm.shape
    rows = images * patches
    return pl.pallas_call(
        functools.partial(input_kernel, patches=patches),
        out_shape=(sds(rows, width), sds(2, width)),
        in_specs=[VM] * 6,
        out_specs=(VM,) * 2,
        scratch_shapes=[
            pltpu.VMEM((rows + 16, width), F32),
            pltpu.VMEM((3, width, width), BF),
            pltpu.VMEM((2, 8, width), F32),
        ],
        compiler_params=PARAMS,
        name="input_gradient",
    )(tok, gm, dp, own, oth, vec)


def spread_rows(flat_ref, from_ref, base, blocks):
    for p in range(blocks):
        for k in range(3):
            at = base + k * blocks + p
            tile = 128 * (3 * p + k)
            flat_ref[0:1, tile : tile + 128] = from_ref[at : at + 1, :]


def pick_rows(ref, start, count, flip=False):
    total = ref.shape[1] if flip else ref.shape[0]
    row = lax.broadcasted_iota(jnp.int32, (count, total), 0) + start
    col = lax.broadcasted_iota(jnp.int32, (count, total), 1)
    chosen = (row == col).astype(F32)
    return lax.dot_general(
        chosen,
        ref[...],
        (((1,), (1 if flip else 0,)), ((), ())),
        preferred_element_type=F32,
        precision=lax.Precision.HIGHEST,
    )


def early_kernel(rank_ref, got_ref, tri_ref, out_ref, wid_ref, nar_ref, *refs, data_count):
    (wid_f, nar_f, out_f, wt_f, wo_f, ww_f, wn_f, vec_ref, hid_ref, sq_ref, tot, st, so, sw, sn) = refs
    width, wide = wid_ref.shape
    half = out_ref.shape[0]
    wp, np_, op = width // data_count, wide // data_count // 2, half // data_count // 2
    tot[...] = jnp.sum(got_ref[...].astype(F32), axis=0)
    spread_rows(wid_f, tot, 0, wp)
    spread_rows(nar_f, tot, 3 * wp, np_)
    spread_rows(out_f, tot, 3 * (wp + np_), op)
    at = 3 * (wp + np_ + op)
    vec_ref[...] = jnp.concatenate([tot[at : at + 4, :], tot[at + 4 : at + 8, : width - 128]], axis=1)
    hid = [tot[at + 8 + k : at + 9 + k, :] for k in range(3)]
    hid_ref[...] = jnp.concatenate(hid, axis=1)
    matrices = tot[0:at, :]
    squares = jnp.sum(matrices * matrices)
    hidden = sum(jnp.sum(member * member) for member in hid)
    squares = squares + jnp.where(rank_ref[1] == 0, hidden, 0.0)
    sq_ref[...] = jnp.full((1, 128), squares)
    data_rank = rank_ref[1]
    groups = tri_ref.shape[0] // data_count // 4
    st[0, :, 0 : tri_ref.shape[1]] = pick_rows(tri_ref, data_rank * 4 * groups, 4 * groups)
    put_planes(so, pick_rows(out_ref, data_rank * 2 * op, 2 * op))
    sw[...] = pick_rows(wid_ref, data_rank * wp, wp)
    put_planes(sn, pick_rows(nar_ref, data_rank * 2 * np_, 2 * np_, flip=True))
    tiles = four_row_tiles(st, 0, 0, groups)
    for p in range(groups):
        for k in range(3):
            tile = 128 * (3 * p + k)
            wt_f[0:1, tile : tile + 128] = tiles[k][p : p + 1, :]
    for ref, flat, pairs in ((so, wo_f, op), (sn, wn_f, np_)):
        tiles = even_odd_tiles(ref, 0, pairs)
        for p in range(pairs):
            for k in range(3):
                tile = 128 * (3 * p + k)
                flat[0:1, tile : tile + 128] = tiles[k][p : p + 1, :]
    for p in range(wp):
        ww_f[0:1, wide * p : wide * (p + 1)] = sw[p : p + 1, :]


def run_early(rank, got, tri, out, wid, nar_t, data_count):
    width, wide = wid.shape
    half = out.shape[0]
    lens = [member.size // data_count for member in (wid, nar_t, out, tri, out, wid, nar_t)]
    share = [member.shape[0] // data_count for member in (tri, out, wid)]
    return pl.pallas_call(
        functools.partial(early_kernel, data_count=data_count),
        out_shape=(
            *[sds(1, member) for member in lens],
            sds(4, width),
            sds(1, wide),
            sds(1, 128),
        ),
        in_specs=[SM] + [VM] * 5,
        out_specs=(VM,) * 10,
        scratch_shapes=[
            pltpu.VMEM((EARLY_ROWS, 128), F32),
            pltpu.VMEM((1, share[0], 128), F32),
            pltpu.VMEM((2, share[1], 128), F32),
            pltpu.VMEM((share[2], wide), F32),
            pltpu.VMEM((2, wide // data_count, 128), F32),
        ],
        compiler_params=PARAMS,
        name="early_sums",
    )(rank, got, tri, out, wid, nar_t)


def late_kernel(got_ref, vec_ref, head_ref, sq_ref, tri_f, pay_ref, tot, *, blocks):
    width = vec_ref.shape[1]
    tot[...] = jnp.sum(got_ref[...].astype(F32), axis=0)
    spread_rows(tri_f, tot, 0, blocks)
    matrix = tot[0 : 3 * blocks, :]
    squares = sq_ref[...] + jnp.sum(matrix * matrix)
    lane = lax.broadcasted_iota(jnp.int32, (1, 128), 1)
    tails = jnp.concatenate([vec_ref[0:1, 128:], vec_ref[1:2, 128:]], axis=1)
    payload = jnp.concatenate(
        [vec_ref[:, :128], tails, jnp.where(lane == 127, squares, head_ref[...])], axis=0
    )
    pay_ref[...] = jnp.broadcast_to(payload[None], pay_ref.shape)


def run_late(got, vec, head, sq, blocks):
    count = got.shape[0]
    return pl.pallas_call(
        functools.partial(late_kernel, blocks=blocks),
        out_shape=(sds(1, 3 * 128 * blocks), sds(count, 4, 128)),
        in_specs=[VM] * 4,
        out_specs=(VM,) * 2,
        scratch_shapes=[pltpu.VMEM((LATE_ROWS, 128), F32)],
        compiler_params=PARAMS,
        name="late_sums",
    )(got, vec, head, sq)


def adam_parts(weight, gradient, moment, squares, rate, decay):
    moment_new = BETA_ONE * moment + (1.0 - BETA_ONE) * gradient
    squares_new = BETA_TWO * squares + (1.0 - BETA_TWO) * gradient * gradient
    quotient = (moment_new / (1.0 - BETA_ONE**STEP)) / (
        jnp.sqrt(squares_new / (1.0 - BETA_TWO**STEP)) + ADAM_EPS
    )
    return moment_new, squares_new, weight - rate * (quotient + decay * weight)


def adam_kernel(rank_ref, got_ref, early_ref, hid_ref, hp_ref, vec_ref, hb_ref, *refs):
    grads = refs[0:4]
    weights = refs[4:8]
    states = refs[8:22]
    outs = refs[22:43]
    norm_ref = refs[43]
    width = vec_ref.shape[1]
    half_heads = hp_ref.shape[0]
    tail = width - 128
    total = jnp.sum(got_ref[...], axis=0)
    late = jnp.concatenate(
        [
            total[0:2, :],
            jnp.concatenate([total[2:3, :tail], total[2:3, tail : 2 * tail]], axis=0),
        ],
        axis=1,
    )
    vector = jnp.concatenate([late, early_ref[...]], axis=0)
    lane = lax.broadcasted_iota(jnp.int32, (1, 128), 1)
    heads_row = jnp.where(lane < 8 * half_heads, total[3:4, :], 0.0)
    squares = (
        jnp.sum(jnp.where(lane == 127, total[3:4, :], 0.0))
        + jnp.sum(vector * vector)
        + jnp.sum(heads_row * heads_row)
    )
    norm = jnp.sqrt(jnp.full((1, 128), squares))
    norm_ref[...] = norm[:, 0:1]
    factor = (CLIP_AT / jnp.maximum(norm, CLIP_AT))[:, 0:1]
    span = 4 * half_heads
    mine = jnp.where(rank_ref[0] == 0, heads_row[:, :span], heads_row[:, span : 2 * span])
    head = jnp.concatenate(
        [
            jnp.concatenate(
                [mine[:, c * half_heads + h : c * half_heads + h + 1] for c in range(4)], axis=1
            )
            for h in range(half_heads)
        ],
        axis=0,
    )
    given = [ref[...] for ref in grads] + [vector, hid_ref[...], head]
    held = [ref[...] for ref in weights] + [vec_ref[...], hb_ref[...], hp_ref[...]]
    for at in range(7):
        renewed = adam_parts(
            held[at],
            given[at] * factor,
            states[2 * at][...],
            states[2 * at + 1][...],
            RATES[at],
            DECAYS[at],
        )
        for step in range(3):
            outs[3 * at + step][...] = renewed[step]


def run_adam(rank, got, early, hid, hp_t, vec, hb, grads, weights, states):
    shapes = []
    for at in range(7):
        shapes += [sds(*states[2 * at].shape)] * 3
    return pl.pallas_call(
        adam_kernel,
        out_shape=(*shapes, sds(1, 1)),
        in_specs=[SM] + [VM] * (6 + 4 + 4 + 14),
        out_specs=(VM,) * 22,
        compiler_params=PARAMS,
        name="adam",
    )(rank, got, early, hid, hp_t, vec, hb, *grads, *weights, *states)


def plain_chunks(halves, tensor_rank, data_count, rows):
    parts = []
    for own_first in halves:
        turned = jnp.where(
            tensor_rank == 0, own_first, jnp.concatenate([own_first[1:], own_first[:1]])
        )
        parts.append(turned.reshape(2, data_count, -1).transpose(1, 0, 2))
    flat = jnp.concatenate(parts, axis=2)
    flat = jnp.pad(flat, ((0, 0), (0, 0), (0, rows * 128 - flat.shape[2])))
    return flat.astype(BF).reshape(2 * data_count, rows, 128)


def on_device(
    tokens,
    cotangent,
    keep_mask,
    triple_weight,
    outward_weight,
    widen_weight,
    narrow_weight,
    vectors,
    hidden_bias,
    head_params,
    triple_moment,
    triple_square,
    outward_moment,
    outward_square,
    widen_moment,
    widen_square,
    narrow_moment,
    narrow_square,
    vector_moment,
    vector_square,
    hidden_moment,
    hidden_square,
    head_moment,
    head_square,
):
    tensor_rank = lax.axis_index("tensor")
    data_rank = lax.axis_index("dp")
    data_count = lax.axis_size("dp")
    axes = ("dp", "tensor")
    images = keep_mask.shape[0] // 2
    patches = keep_mask.shape[1]
    heads = 2 * head_params.shape[1]
    depth = triple_weight.shape[1]
    half = triple_weight.shape[2]
    wide = widen_weight.shape[1]
    rank = jnp.stack([tensor_rank, data_rank]).astype(jnp.int32)
    triple_rows = triple_weight.reshape(3 * depth, half)
    narrow_t = narrow_weight.T
    bias_row = hidden_bias.reshape(1, wide)
    head_t = head_params.T
    fast = (
        depth == 192
        and half == 96
        and wide == 384
        and depth % data_count == 0
        and wide % (2 * data_count) == 0
        and half % (2 * data_count) == 0
        and 3 * depth % (4 * data_count) == 0
    )
    chunked = data_count if fast else 0

    own = run_pack(triple_weight, outward_weight, widen_weight, narrow_t, bias_row, head_t)
    other = lax.ppermute(own, "tensor", [(0, 1), (1, 0)])
    keep_here = lax.dynamic_slice_in_dim(keep_mask, tensor_rank * images, images).astype(F32)
    kp = -(-patches // 16) * 16
    keep_cols = jnp.broadcast_to(
        jnp.pad(keep_here, ((0, 0), (0, kp - patches)))[:, :, None], (images, kp, 128)
    )
    result, grad_middle, first, q, k, v, kt, dm, lse, hp, *sums = run_forward(
        rank, tokens, cotangent, keep_cols, own, other, vectors, heads, patches, chunked
    )
    if fast:
        early_sent = sums[0]
    else:
        nar_g, wid_g, out_g, vec_g, hid_g = sums
        early_mine = jnp.sum(vec_g, axis=1).reshape(1, 1, -1)
        early_sent = plain_chunks(
            [
                wid_g.reshape(depth, 2, wide).transpose(1, 0, 2).reshape(2, -1),
                nar_g.reshape(2, -1),
                out_g.reshape(2, -1),
                jnp.broadcast_to(early_mine, (2, data_count, early_mine.size)).reshape(2, -1),
                jnp.broadcast_to(
                    jnp.sum(hid_g, axis=0).reshape(2, 1, wide), (2, data_count, wide)
                ).reshape(2, -1),
            ],
            tensor_rank,
            data_count,
            EARLY_ROWS,
        )
    early_got = lax.all_to_all(early_sent, axes, 0, 0, tiled=False)
    dp, head_row, late = run_backward(
        rank, hp, keep_cols, first, q, k, v, kt, dm, lse, heads, patches, chunked
    )
    if not fast:
        halves = late.reshape(3 * depth, 2, half).transpose(1, 0, 2).reshape(2, -1)
        late = plain_chunks([halves], tensor_rank, data_count, LATE_ROWS)
    late_got = lax.all_to_all(late, axes, 0, 0, tiled=False)
    grad_input, late_vec = run_input(tokens, grad_middle, dp, own, other, vectors, patches)
    if fast:
        wid_f, nar_f, out_f, wt_f, wo_f, ww_f, wn_f, early_vec, hid, sq = run_early(
            rank, early_got, triple_rows, outward_weight, widen_weight, narrow_t, data_count
        )
        tri_f, payload = run_late(late_got, late_vec, head_row, sq, 3 * depth // data_count // 4)
    else:
        early_sum = jnp.sum(early_got.astype(F32), axis=0).reshape(1, -1)
        masters = (widen_weight, narrow_weight, outward_weight)
        sizes = [member.size // data_count for member in masters] + [4 * depth, wide]
        cuts = [sum(sizes[:at]) for at in range(6)]
        wid_f, nar_f, out_f, early_vec, hid = (
            early_sum[:, cuts[at] : cuts[at + 1]] for at in range(5)
        )
        early_vec = early_vec.reshape(4, depth)
        share = triple_rows.size // data_count
        tri_f = jnp.sum(late_got.astype(F32), axis=0).reshape(1, -1)[:, :share]

        def weight_share(member):
            length = member.size // data_count
            return lax.dynamic_slice_in_dim(member.reshape(1, -1), data_rank * length, length, 1)

        ww_f, wn_f, wo_f = (weight_share(member) for member in masters)
        wt_f = weight_share(triple_rows)
        squares = sum(jnp.sum(member * member) for member in (wid_f, nar_f, out_f, tri_f))
        squares = squares + jnp.where(data_rank == 0, jnp.sum(hid * hid), 0.0)
        lane = lax.broadcasted_iota(jnp.int32, (1, 128), 1)
        payload = jnp.concatenate(
            [
                late_vec[:, :128],
                late_vec[:, 128:].reshape(1, 128),
                jnp.where(lane == 127, squares, head_row),
            ]
        )
        payload = jnp.broadcast_to(payload[None], (2 * data_count, 4, 128))
    last_got = lax.all_to_all(payload, axes, 0, 0, tiled=False)
    renewed = run_adam(
        rank,
        last_got,
        early_vec,
        hid,
        head_t,
        vectors,
        bias_row,
        (tri_f, out_f, wid_f, nar_f),
        (wt_f, wo_f, ww_f, wn_f),
        (
            triple_moment,
            triple_square,
            outward_moment,
            outward_square,
            widen_moment,
            widen_square,
            narrow_moment,
            narrow_square,
            vector_moment,
            vector_square,
            hidden_moment.reshape(1, wide),
            hidden_square.reshape(1, wide),
            head_moment.T,
            head_square.T,
        ),
    )
    hidden_new = [member.reshape(wide) for member in renewed[15:18]]
    head_new = [member.T for member in renewed[18:21]]
    return (result, grad_input, *renewed[:15], *hidden_new, *head_new, renewed[21].reshape(()))


def solution(mesh):
    return jax.shard_map(
        on_device,
        mesh=mesh,
        in_specs=(
            P(("dp", "tensor"), None),
            P(("dp", "tensor"), None),
            P("dp", None),
            P(None, None, "tensor"),
            P("tensor", None),
            P(None, "tensor"),
            P("tensor", None),
            P(),
            P("tensor"),
            P(None, "tensor"),
            P("tensor", "dp"),
            P("tensor", "dp"),
            P("tensor", "dp"),
            P("tensor", "dp"),
            P("tensor", "dp"),
            P("tensor", "dp"),
            P("tensor", "dp"),
            P("tensor", "dp"),
            P(),
            P(),
            P("tensor"),
            P("tensor"),
            P(None, "tensor"),
            P(None, "tensor"),
        ),
        out_specs=(
            P(("dp", "tensor"), None),
            P(("dp", "tensor"), None),
            P("tensor", "dp"),
            P("tensor", "dp"),
            P("tensor", "dp"),
            P("tensor", "dp"),
            P("tensor", "dp"),
            P("tensor", "dp"),
            P("tensor", "dp"),
            P("tensor", "dp"),
            P("tensor", "dp"),
            P("tensor", "dp"),
            P("tensor", "dp"),
            P("tensor", "dp"),
            P(),
            P(),
            P(),
            P("tensor"),
            P("tensor"),
            P("tensor"),
            P(None, "tensor"),
            P(None, "tensor"),
            P(None, "tensor"),
            P(),
        ),
        check_vma=False,
    )
```

time: 436 us -> 103 us (0.24); the launches traced: 429 us -> 103 us
  waiting for transfers between devices: 96.1 us -> 4.54 us
  blocking collectives: 82.6 us -> 0 us
  matrix products: 78.3 us -> 0 us
  local copies, waits for them, and re-layouts: 87 us -> 11.9 us
  Pallas kernels: 0 us -> 64.7 us
  other arithmetic: 62.5 us -> 4.36 us
  between operations: 21.6 us -> 0.75 us
  starting transfers between devices: 1.2 us -> 16.3 us
    psum x2 -> x0, blocking collectives: 82.6 us -> none  [the longest x1 41.9 us: on_device(): bias_here, head_here = lax.psum((hidden_grad, head_grads), 'dp')]
    dot_general x17 -> x0, matrix products: 65 us -> none  [the longest x1 14.3 us: layer_pass(): jnp.dot(second_in, widen_low, preferred_element_type=jnp.float32)]
    pallas_call x0 -> x7, Pallas kernels: none -> 64.7 us  [the longest x1 30.6 us: run_forward(): pl.pallas_call(functools.partial(forward_kernel, patches=patches, heads=h...]
    psum x1 -> x0, waiting for transfers between devices: 52 us -> none  [on_device(): summed = lax.psum(flattened, 'dp')]
    unnamed x13 -> x0, waiting for transfers between devices: 26.5 us -> none
    reduce_sum x18 -> x0, other arithmetic: 24.5 us -> none  [the longest x5 7.12 us: layer_norm(): return centred * lax.rsqrt(variance + EPS_NORM) * gains + shifts]
    unnamed x163 -> x24, local copies, waits for them, and re-layouts: 32.7 us -> 8.2 us
    all_gather x4 -> x0, waiting for transfers between devices: 17.5 us -> none  [the longest x1 8.32 us: layer_pass(): second_in = lax.all_gather(second_low, 'tensor', axis=0, tiled=True)]
  transfers between devices with their start and end apart: 9 -> 4, of which waited for: 7 -> 3; matrix products, arithmetic and copies ran while one was open for 20% -> 8% of each run, Pallas kernels for 0% -> 28%
where the time goes in v1:
time: 103 us
  Pallas kernels  64.7 us (63%)
  starting transfers between devices  16.3 us (16%)
  local copies, waits for them, and re-layouts  11.9 us (12%)
  waiting for transfers between devices  4.54 us (4%)
  other arithmetic  4.36 us (4%)
    pallas_call x1, Pallas kernels, run_forward(): pl.pallas_call(functools.partial(forward_kernel, patches=patches, heads=h...  30.6 us
    pallas_call x1, Pallas kernels, run_backward(): pl.pallas_call(functools.partial(backward_kernel, patches=patches, heads=...  18.7 us
    unnamed x24, local copies, waits for them, and re-layouts  8.2 us
    all_to_all x1, starting transfers between devices, on_device(): early_got = lax.all_to_all(early_sent, axes, 0, 0, tiled=False)  6.96 us
    pallas_call x1, Pallas kernels, run_input(): pl.pallas_call(functools.partial(input_kernel, patches=patches), out_shap...  6.38 us
    all_to_all x1, starting transfers between devices, on_device(): last_got = lax.all_to_all(payload, axes, 0, 0, tiled=False)  4.78 us
    all_to_all x1, starting transfers between devices, on_device(): late_got = lax.all_to_all(late, axes, 0, 0, tiled=False)  4.13 us
    pallas_call x3, other arithmetic, run_adam(): pl.pallas_call(adam_kernel, out_shape=(*shapes, sds(1, 1)), in_specs=[SM]...  3.76 us
  transfers between devices with their start and end apart: 4, of which 3 were waited for; matrix products, arithmetic and copies ran while one was open for 8% of the time, Pallas kernels for 28%

profile of v1, /device:TPU:0, one launch (start us, length us, event | category | flops | bytes accessed | tf_op | source)
XLA Modules:
  0.0 102.6 jit_solution(16940726978833938943)
XLA Ops:
  0.7 0.0 copy-start.4
  0.7 0.0 copy-start.5
  0.7 1.3 %reshape.73.hb_ref = f32[1,384]{1,0:T(1,128)} reshape(f32[384]{0:T(512)} %param.32) | data formatting | bytes 3072 | tf_op jit(solution)/shard_map/reshape | solution.py:817
  2.0 2.2 %pack_weights.1.refs_4_.own_ref = bf16[592,384]{1,0:T(8,128)(2,1)} custom-call(f32[3,192,96]{2,1,0:T(8,128)} %tri_ref.1, f32[96,192]{1,0:T(8,128)} %out_ref.3, f32[192,384]{1,0:T(8,128)} %wid_ref.3, f32[192,384]{1,0:T(8,128)} %bitcast.12, f32[1,384]{1,0:T(1,128)} %reshape.73.hb_ref, f32[2,4]{1,0:T(2,128)} %bitcast.14), custom_call_target="tpu_custom_call" | custom-call | tf_op jit(solution)/shard_map/pack_weights/pallas_call | solution.py:162
  4.2 0.0 copy-start.7
  4.2 0.5 collective-permute-start
  4.6 0.0 copy-done.4
  4.6 1.2 %copy.48.refs_1_.tok_ref = bf16[1568,192]{1,0:T(8,128)(2,1)} copy(bf16[1568,192]{0,1:T(8,128)(2,1)S(1)} %copy-done.4) | data formatting | bytes 1204224 | tf_op args[0]
  5.8 0.0 copy-done.5
  5.8 1.2 %copy.49.refs_2_ = bf16[1568,192]{1,0:T(8,128)(2,1)} copy(bf16[1568,192]{0,1:T(8,128)(2,1)S(1)} %copy-done.5) | data formatting | bytes 1204224 | tf_op args[1]
  7.0 0.0 copy-done.7
  7.0 0.6 pad_add_fusion.refs_0_.rank_ref
  7.6 0.0 collective-permute-done.refs_5_.oth_ref
  7.6 0.0 copy-start.1
  7.6 1.2 %broadcast_in_dim.2.refs_3_.refs_2_ = f32[8,208,128]{2,1,0:T(8,128)} broadcast(f32[8,208]{1,0:T(8,128)S(1)} %pad.4), dimensions={0,1} | broadcast | bytes 858624 | tf_op jit(solution)/shard_map/broadcast_in_dim | solution.py:834
  8.8 0.0 copy-done.1
  8.8 30.6 %forward.1 = (f32[1568,192]{1,0:T(8,128)}, f32[8,208,192]{2,1,0:T(8,128)}, bf16[8,208,192]{2,1,0:T(8,128)(2,1)}, bf16[8,256,192]{2,1,0:T(8,128)(2,1)}, bf16[8,20...) custom-call(s32[2]{0:T(128)} %pad_add_fusion.refs_0_.rank_ref, ...), custom_call_target="tpu_custom_call" | custom-call | tf_op jit(solution)/shard_map/forward/pallas_call | solution.py:381
  39.4 7.0 %all-to-all-start.1 = ((bf16[32,96,128]{2,1,0:T(8,128)(2,1)}), bf16[32,96,128]{2,1,0:T(8,128)(2,1)S(1)}, u32[]{:S(2)}, u32[]{:S(2)}) async-start(bf16[32,96,128]{2,1,0:T(8,128)(2,1)} %get-tuple-element.89), calls=%async_computation.1 | async-start | bytes 1572864 | tf_op jit(solution)/shard_map/all_to_all | solution.py:859
  46.4 18.7 %attention_backward.1 = (bf16[3,8,208,192]{3,2,1,0:T(8,128)(2,1)}, f32[1,128]{1,0:T(1,128)}, bf16[32,32,128]{2,1,0:T(8,128)(2,1)}) custom-call(s32[2]{0:T(128)} %pad_add_fusion.refs_0_.rank_ref, f32[8,128]{1,0:T(8,128)} %get-tuple-element.76.refs_1_, f32[8,208,128]{2,1,0:T(8,128)} %broadcast_in_dim.2.refs_3_.refs_2_, ...), custom_call_target="tpu_custom_call" | custom-call | tf_op jit(solution)/shard_map/attention_backward/pallas_call | solution.py:512
  65.1 1.9 %all-to-all-done.1.got_ref = bf16[32,96,128]{2,1,0:T(8,128)(2,1)S(1)} async-done(((bf16[32,96,128]{2,1,0:T(8,128)(2,1)}), bf16[32,96,128]{2,1,0:T(8,128)(2,1)S(1)}, u32[]{:S(2)}, u32[]{:S(2)}) %all-to-all-start.1) | async-done | bytes 786464 | tf_op jit(solution)/shard_map/all_to_all | solution.py:859
  67.0 0.0 copy-start
  67.0 4.1 %all-to-all-start = ((bf16[32,32,128]{2,1,0:T(8,128)(2,1)}), bf16[32,32,128]{2,1,0:T(8,128)(2,1)S(1)}, u32[]{:S(2)}, u32[]{:S(2)}) async-start(bf16[32,32,128]{2,1,0:T(8,128)(2,1)} %get-tuple-element.86), calls=%async_computation | async-start | bytes 524288 | tf_op jit(solution)/shard_map/all_to_all | solution.py:866
  71.1 6.4 %input_gradient.1 = (f32[1568,192]{1,0:T(8,128)}, f32[2,192]{1,0:T(2,128)}) custom-call(bf16[1568,192]{1,0:T(8,128)(2,1)} %copy.48.refs_1_.tok_ref, f32[8,208,192]{2,1,0:T(8,128)} %get-tuple-element.75.gm_ref, bf16[3,8,208,192]{3,2,1,0:T(8,128)(2,1)} %get-tuple-element.84.dp_ref, bf16[592,384]{1,0:T(8,128)(2,1)} %pack_weights.1.refs_4_.own_ref, ...), custom_call_target="tpu_custom_call" | custom-call | tf_op jit(solution)/shard_map/input_gradient/pallas_call | solution.py:559
  77.5 0.0 copy-done
  77.5 0.0 copy-start.8
  77.5 0.0 copy-start.9
  77.5 0.0 copy-start.2
  77.5 3.1 %early_sums.1 = (f32[1,4608]{1,0:T(1,128)}, f32[1,4608]{1,0:T(1,128)}, f32[1,1152]{1,0:T(1,128)}, f32[1,3456]{1,0:T(1,128)}, f32[1,1152]{1,0:T(1,128)}, /*index=...) custom-call(s32[2]{0:T(128)} %pad_add_fusion.refs_0_.rank_ref, ...), custom_call_target="tpu_custom_call" | custom-call | tf_op jit(solution)/shard_map/early_sums/pallas_call | solution.py:640
  80.6 0.9 all-to-all-done.got_ref
  81.5 0.0 copy-start.3
  81.5 0.7 copy-done.3
  82.2 1.8 %late_sums.1 = (f32[1,3456]{1,0:T(1,128)}, f32[32,4,128]{2,1,0:T(4,128)}) custom-call(bf16[32,32,128]{2,1,0:T(8,128)(2,1)} %copy-done.3, f32[2,192]{1,0:T(2,128)} %get-tuple-element.87.vec_ref, f32[1,128]{1,0:T(1,128)} %get-tuple-element.88.head_ref, f32[1,128]{1,0:T(1,128)} %get-tuple-element.90.sq_ref), custom_call_target="tpu_custom_call" | custom-call | tf_op jit(solution)/shard_map/late_sums/pallas_call | solution.py:678
  84.0 4.8 %all-to-all-start.2 = ((f32[32,4,128]{2,1,0:T(4,128)}), f32[32,4,128]{2,1,0:T(4,128)S(1)}, u32[]{:S(2)}, u32[]{:S(2)}) async-start(f32[32,4,128]{2,1,0:T(4,128)} %get-tuple-element.91), calls=%async_computation.2 | async-start | bytes 131072 | tf_op jit(solution)/shard_map/all_to_all | solution.py:902
  88.8 0.0 copy-done.8
  88.8 0.6 reshape.75.refs_18_
  89.4 0.0 copy-done.9
  89.4 0.6 reshape.76.refs_19_
  90.0 0.0 copy-done.2
  90.0 1.5 %copy.51 = f32[1568,192]{0,1:T(8,128)} copy(f32[1568,192]{1,0:T(8,128)S(1)} %copy-done.2) | data formatting | bytes 2408448
  91.5 3.0 %copy.52 = f32[1568,192]{0,1:T(8,128)} copy(f32[1568,192]{1,0:T(8,128)} %get-tuple-element.125) | data formatting | bytes 2408448
  94.4 1.7 %all-to-all-done.2.got_ref = f32[32,4,128]{2,1,0:T(4,128)S(1)} async-done(((f32[32,4,128]{2,1,0:T(4,128)}), f32[32,4,128]{2,1,0:T(4,128)S(1)}, u32[]{:S(2)}, u32[]{:S(2)}) %all-to-all-start.2) | async-done | bytes 65568 | tf_op jit(solution)/shard_map/all_to_all | solution.py:902
  96.2 0.0 copy-start.6
  96.2 0.6 copy-done.6
  96.8 2.0 %adam.1 = (f32[1,3456]{1,0:T(1,128)}, f32[1,3456]{1,0:T(1,128)}, f32[1,3456]{1,0:T(1,128)}, f32[1,1152]{1,0:T(1,128)}, f32[1,1152]{1,0:T(1,128)}, /*index=5*/f32...) custom-call(s32[2]{0:T(128)} %pad_add_fusion.refs_0_.rank_ref, ...), custom_call_target="tpu_custom_call" | custom-call | tf_op jit(solution)/shard_map/adam/pallas_call | solution.py:756
  98.8 1.3 %reduce = f32[384]{0:T(512)} reduce(f32[1,384]{1,0:T(1,128)} %get-tuple-element.117, f32[]{:T(128)} %constant.26), dimensions={0}, to_apply=%get-tuple-element.117.reduce_sub_computation | reduce | bytes 3076 | tf_op jit(solution)/shard_map/adam/pallas_call | solution.py:756
  100.1 1.3 %reduce.1 = f32[384]{0:T(512)} reduce(f32[1,384]{1,0:T(1,128)} %get-tuple-element.118, f32[]{:T(128)} %constant.26), dimensions={0}, to_apply=%get-tuple-element.118.reduce_sub_computation | reduce | bytes 3076 | tf_op jit(solution)/shard_map/adam/pallas_call | solution.py:756
  101.3 1.2 %reduce.2 = f32[384]{0:T(512)} reduce(f32[1,384]{1,0:T(1,128)} %get-tuple-element.119, f32[]{:T(128)} %constant.26), dimensions={0}, to_apply=%get-tuple-element.119.reduce_sub_computation | reduce | bytes 3076 | tf_op jit(solution)/shard_map/adam/pallas_call | solution.py:756
  (2 shorter events, 0.0 us)
Async XLA Ops:
  0.7 4.0 %copy-start.4 = (bf16[1568,192]{0,1:T(8,128)(2,1)S(1)}, bf16[1568,192]{0,1:T(8,128)(2,1)}, u32[]{:S(2)}) copy-start(bf16[1568,192]{0,1:T(8,128)(2,1)} %param.24) | copy-start | bytes 1806340
  0.7 5.1 %copy-start.5 = (bf16[1568,192]{0,1:T(8,128)(2,1)S(1)}, bf16[1568,192]{0,1:T(8,128)(2,1)}, u32[]{:S(2)}) copy-start(bf16[1568,192]{0,1:T(8,128)(2,1)} %param.25) | copy-start | bytes 1806340
  4.2 2.8 %copy-start.7 = (s32[16,196]{1,0:T(8,128)S(1)}, s32[16,196]{1,0:T(8,128)}, u32[]{:S(2)}) copy-start(s32[16,196]{1,0:T(8,128)} %param.26) | copy-start | bytes 37636
  4.2 3.4 %collective-permute-start = (bf16[592,384]{1,0:T(8,128)(2,1)}, bf16[592,384]{1,0:T(8,128)(2,1)S(1)}, u32[]{:S(2)}, u32[]{:S(2)}) collective-permute-start(bf16[592,384]{1,0:T(8,128)(2,1)} %pack_weights.1.refs_4_.own_ref), channel_id=1, source_target_pairs={{0,1},{1,0},{2,3},{3,2},{4,5},{5,4},{6,7},{7,6},{8,9},{9,8},{10,11... | collective-permute-start | bytes 1363976 | tf_op jit(solution)/shard_map/ppermute | solution.py:831
  7.6 1.2 %copy-start.1 = (bf16[592,384]{1,0:T(8,128)(2,1)}, bf16[592,384]{1,0:T(8,128)(2,1)S(1)}, u32[]{:S(2)}) copy-start(bf16[592,384]{1,0:T(8,128)(2,1)S(1)} %collective-permute-done.refs_5_.oth_ref) | copy-start | bytes 1363972
  39.4 27.6 %all-to-all-start.1 = ((bf16[32,96,128]{2,1,0:T(8,128)(2,1)}), bf16[32,96,128]{2,1,0:T(8,128)(2,1)S(1)}, u32[]{:S(2)}, u32[]{:S(2)}) async-start(bf16[32,96,128]{2,1,0:T(8,128)(2,1)} %get-tuple-element.89), calls=%async_computation.1 | async-start | bytes 1572864 | tf_op jit(solution)/shard_map/all_to_all | solution.py:859
  67.0 10.5 %copy-start = (bf16[32,96,128]{2,1,0:T(8,128)(2,1)}, bf16[32,96,128]{2,1,0:T(8,128)(2,1)S(1)}, u32[]{:S(2)}) copy-start(bf16[32,96,128]{2,1,0:T(8,128)(2,1)S(1)} %all-to-all-done.1.got_ref) | copy-start | bytes 2359300
  67.0 14.6 %all-to-all-start = ((bf16[32,32,128]{2,1,0:T(8,128)(2,1)}), bf16[32,32,128]{2,1,0:T(8,128)(2,1)S(1)}, u32[]{:S(2)}, u32[]{:S(2)}) async-start(bf16[32,32,128]{2,1,0:T(8,128)(2,1)} %get-tuple-element.86), calls=%async_computation | async-start | bytes 524288 | tf_op jit(solution)/shard_map/all_to_all | solution.py:866
  77.5 11.3 %copy-start.8 = (f32[384]{0:T(512)S(1)}, f32[384]{0:T(512)}, u32[]{:S(2)}) copy-start(f32[384]{0:T(512)} %param.44) | copy-start | bytes 4612
  77.5 11.9 %copy-start.9 = (f32[384]{0:T(512)S(1)}, f32[384]{0:T(512)}, u32[]{:S(2)}) copy-start(f32[384]{0:T(512)} %param.45) | copy-start | bytes 4612
  77.5 12.5 %copy-start.2 = (f32[1568,192]{1,0:T(8,128)S(1)}, f32[1568,192]{1,0:T(8,128)}, u32[]{:S(2)}) copy-start(f32[1568,192]{1,0:T(8,128)} %get-tuple-element.124) | copy-start | bytes 3612676
  81.5 0.7 copy-start.3
  84.0 12.2 %all-to-all-start.2 = ((f32[32,4,128]{2,1,0:T(4,128)}), f32[32,4,128]{2,1,0:T(4,128)S(1)}, u32[]{:S(2)}, u32[]{:S(2)}) async-start(f32[32,4,128]{2,1,0:T(4,128)} %get-tuple-element.91), calls=%async_computation.2 | async-start | bytes 131072 | tf_op jit(solution)/shard_map/all_to_all | solution.py:902
  96.2 0.6 copy-start.6

commit v2 on v1

v2 whole, which is shorter than its diff:
```python
import functools
import math

import jax
import jax.numpy as jnp
from jax import lax
from jax.experimental import pallas as pl
from jax.experimental.pallas import tpu as pltpu
from jax.sharding import PartitionSpec as P

GRID = 14
STEP = 10
EPS_NORM = 1e-06
CLIP_AT = 1.0
BETA_ONE = 0.9
BETA_TWO = 0.95
ADAM_EPS = 1e-08
RATES = (0.1, 0.5, 0.1, 0.05, 0.3, 0.1, 0.3)
DECAYS = (0.05, 0.05, 0.05, 0.05, 0.0, 0.0, 0.0)
LOG2E = 1.4426950408889634
BF = jnp.bfloat16
F32 = jnp.float32
VMEM_LIMIT = 56 * 1024 * 1024
EARLY_ROWS = 96
LATE_ROWS = 32
CHUNK_ROWS = EARLY_ROWS + LATE_ROWS
PAIR = 2
VM = pl.BlockSpec(memory_space=pltpu.VMEM)
SM = pl.BlockSpec(memory_space=pltpu.SMEM)
PARAMS = pltpu.CompilerParams(vmem_limit_bytes=VMEM_LIMIT)


def sds(*dims, dtype=F32):
    return jax.ShapeDtypeStruct(dims, dtype)


def nn(a, b):
    return lax.dot_general(a, b, (((1,), (0,)), ((), ())), preferred_element_type=F32)


def nt(a, b):
    return lax.dot_general(a, b, (((1,), (1,)), ((), ())), preferred_element_type=F32)


def norm_parts(v):
    width = v.shape[-1]
    average = jnp.sum(v, axis=-1, keepdims=True) * (1.0 / width)
    centred = v - average
    variance = jnp.sum(centred * centred, axis=-1, keepdims=True) * (1.0 / width)
    spread = lax.rsqrt(variance + EPS_NORM)
    return centred * spread, spread


def norm_back(e, n, spread):
    width = e.shape[-1]
    mean_e = jnp.sum(e, axis=-1, keepdims=True) * (1.0 / width)
    mean_en = jnp.sum(e * n, axis=-1, keepdims=True) * (1.0 / width)
    return spread * (e - mean_e - n * mean_en)


def fold(v):
    rows = v.shape[0]
    return jnp.sum(v.reshape(rows // 8, 8, v.shape[1]), axis=0)


def gelu_parts(x):
    phi = 0.5 + 0.5 * lax.erf(x * math.sqrt(0.5))
    density = jnp.exp2((x * x) * (-0.5 * LOG2E)) * (1.0 / math.sqrt(2.0 * math.pi))
    return x * phi, phi + x * density


def places(count, lanes, dim):
    at = lax.broadcasted_iota(jnp.int32, (count, lanes), dim).astype(F32)
    row = jnp.floor((at + 0.5) * (1.0 / GRID))
    return at - row * GRID, row


def offsets(kp, qp):
    kc, kr = places(kp, qp, 0)
    qc, qr = places(kp, qp, 1)
    a = kc - qc
    b = kr - qr
    return a, b, a * a + b * b


def head_mask(rows, width, hd, h):
    lane = lax.broadcasted_iota(jnp.int32, (rows, width), 1)
    return ((lane >= h * hd) & (lane < (h + 1) * hd)).astype(BF)


def gate_of(hp_ref, h, lanes):
    return 1.0 / (1.0 + jnp.exp(-jnp.broadcast_to(hp_ref[h : h + 1, 3:4], (1, lanes))))


def bf_parts(value, count=3):
    parts = []
    for _ in range(count):
        part = value.astype(BF).astype(F32)
        parts.append(part)
        value = value - part
    return parts


def key_operand(kp):
    kc, kr = places(kp, 128, 0)
    lane = lax.broadcasted_iota(jnp.int32, (kp, 128), 1)
    value = jnp.where(lane < 3, kc, jnp.where(lane < 6, kr, jnp.where(lane < 9, kc * kc, kr * kr)))
    return jnp.where(lane < 12, value, 0.0).astype(BF)


def query_operand(hp_ref, h, qp):
    p = [LOG2E * jnp.broadcast_to(hp_ref[h : h + 1, at : at + 1], (16, qp)) for at in range(3)]
    qc, qr = places(16, qp, 1)
    row = lax.broadcasted_iota(jnp.int32, (16, qp), 0)
    value = jnp.where(row < 3, p[0] - 2.0 * p[2] * qc, jnp.where(row < 6, p[1] - 2.0 * p[2] * qr, p[2]))
    parts = bf_parts(value)
    place = row - 3 * ((row >= 3).astype(jnp.int32) + (row >= 6) + (row >= 9))
    value = jnp.where(place == 0, parts[0], jnp.where(place == 1, parts[1], parts[2]))
    return jnp.where(row < 12, value, jnp.where(row == 12, 1.0, 0.0)).astype(BF)


STRIP = 16


def interleave(*streams):
    streams = [member for member in streams if member is not None]
    while streams:
        alive = []
        for member in streams:
            try:
                next(member)
                alive.append(member)
            except StopIteration:
                pass
        streams = alive


def slow(stream, count):
    for _ in range(count):
        yield
        try:
            next(stream)
        except StopIteration:
            return


def cut(value, r):
    return value[r * STRIP : (r + 1) * STRIP]


def rows_of(r):
    return pl.ds(r * STRIP, STRIP)


def put_planes(ref, value):
    width = value.shape[1]
    ref[0] = value[:, :128]
    ref[1, :, 0 : width - 128] = value[:, 128:]


def even_odd_tiles(ref, start, pairs):
    even = [ref[at, pl.ds(start, pairs, stride=2), :] for at in range(2)]
    odd = [ref[at, pl.ds(start + 1, pairs, stride=2), :] for at in range(2)]
    return (
        even[0],
        jnp.concatenate([even[1][:, :64], odd[0][:, :64]], axis=1),
        jnp.concatenate([odd[0][:, 64:], odd[1][:, :64]], axis=1),
    )


def four_row_tiles(ref, plane, start, groups):
    r = [ref[plane, pl.ds(start + at, groups, stride=4), :] for at in range(4)]
    return (
        jnp.concatenate([r[0][:, :96], r[1][:, :32]], axis=1),
        jnp.concatenate([r[1][:, 32:96], r[2][:, :64]], axis=1),
        jnp.concatenate([r[2][:, 64:96], r[3][:, :96]], axis=1),
    )


def pack_kernel(tri_ref, out_ref, wid_ref, nar_ref, hb_ref, hp_ref, pack_ref):
    depth, wide = wid_ref.shape
    pack_ref[0:depth, :] = wid_ref[...].astype(BF)
    pack_ref[depth : 2 * depth, :] = nar_ref[...].astype(BF)
    pack_ref[2 * depth : 3 * depth, :] = jnp.concatenate(
        [tri_ref[0], tri_ref[1], tri_ref[2], out_ref[...].T], axis=1
    ).astype(BF)
    heads_here = hp_ref.shape[0]
    hp = jnp.concatenate([hp_ref[...], jnp.zeros((heads_here, wide - 4), F32)], axis=1)
    left = jnp.concatenate([hb_ref[...].reshape(1, wide), hp], axis=0)
    parts = []
    for _ in range(3):
        part = left.astype(BF).astype(F32)
        parts.append(part)
        left = left - part
    parts.append(jnp.zeros((16 - 3 * (1 + heads_here), wide), F32))
    pack_ref[3 * depth : 3 * depth + 16, :] = jnp.concatenate(parts, axis=0).astype(BF)


def run_pack(tri, out, wid, nar_t, hb, hp_t):
    depth, wide = wid.shape
    return pl.pallas_call(
        pack_kernel,
        out_shape=sds(3 * depth + 16, wide, dtype=BF),
        in_specs=[VM] * 6,
        out_specs=VM,
        compiler_params=PARAMS,
        name="pack_weights",
    )(tri, out, wid, nar_t, hb, hp_t)


def prepare_kernel(rank_ref, tok_ref, cot_ref, keep_ref, x_ref, inc_ref, bias_ref, xs, cs):
    images, kp, width = x_ref.shape
    patches = keep_ref.shape[1]
    rows = images * patches
    qp = -(-patches // 128) * 128
    mine = keep_ref[pl.ds(pl.multiple_of(rank_ref[0] * images, 8), images), :].astype(F32)
    columns = jnp.concatenate([mine, jnp.zeros((images, qp - patches), F32)], axis=1).T
    xs[0:rows, :] = tok_ref[...].T.astype(F32)
    cs[0:rows, :] = cot_ref[...].T.astype(F32)
    xs[rows : rows + 16, :] = jnp.zeros((16, width), F32)
    cs[rows : rows + 16, :] = jnp.zeros((16, width), F32)
    for i in range(images):
        span = slice(i * patches, i * patches + kp)
        keep = jnp.broadcast_to(columns[:kp, i : i + 1], (kp, 128))
        keep_wide = jnp.concatenate([keep, keep[:, : width - 128]], axis=1)
        x_ref[i] = xs[span, :].astype(BF)
        inc_ref[i] = (cs[span, :] * keep_wide).astype(BF)
        bias_ref[i] = ((keep - 1.0) * 1e30).astype(BF)


def run_prepare(rank, tok_t, cot_t, keep_mask):
    images = keep_mask.shape[0] // 2
    kp = -(-keep_mask.shape[1] // 16) * 16
    width, rows_here = tok_t.shape
    rows = sds(images, kp, width, dtype=BF)
    return pl.pallas_call(
        prepare_kernel,
        out_shape=(rows, rows, sds(images, kp, 128, dtype=BF)),
        in_specs=[SM] + [VM] * 3,
        out_specs=(VM,) * 3,
        scratch_shapes=[pltpu.VMEM((rows_here + 16, width), F32)] * 2,
        compiler_params=PARAMS,
        name="prepare",
    )(rank, tok_t, cot_t, keep_mask)


def layer_kernel(*refs, patches, heads, data_count):
    (rank_ref, x_ref, inc_ref, bias_ref, own_ref, oth_ref, vec_ref) = refs[:7]
    (res_ref, gm_ref, dp_ref, head_ref) = refs[7:11]
    outs = refs[11:13] if data_count else refs[11:17]
    at = 11 + len(outs)
    (wq, wk, wv, wkt, wvt, wo, wi, wn, hb_s, hp_s, key_p, query_p) = refs[at : at + 12]
    at += 12
    (fst_s, keys_s, vt_s, qm_s, dmm_s, v_s, kt_s, soft_s, mix_s, mid_s, n2_s) = refs[at : at + 11]
    at += 11
    (first_t, left_t, right_s, res_s, gm_s, dp_s, s_buf, p_buf, att_buf) = refs[at : at + 9]
    at += 9
    (place_g, gate_g, da_buf, att_s, ds_s, wide_g, vec_g, hid_g, og, sems) = refs[at : at + 10]
    at += 10
    images, kp, width = x_ref.shape
    qp = soft_s.shape[4]
    hd = width // heads
    half = width // 2
    half_heads = heads // 2
    wide = own_ref.shape[1]
    hidden = 2 * wide
    strips = kp // STRIP
    c_scale = LOG2E / math.sqrt(hd)
    back_scale = 1.0 / math.sqrt(hd)
    v = [vec_ref[k : k + 1, :] for k in range(6)]

    wi[:, pl.ds(0, wide)] = own_ref[0:width, :]
    wi[:, pl.ds(wide, wide)] = oth_ref[0:width, :]
    wn[:, pl.ds(0, wide)] = own_ref[width : 2 * width, :]
    wn[:, pl.ds(wide, wide)] = oth_ref[width : 2 * width, :]
    own_tri = own_ref[2 * width : 3 * width, :]
    oth_tri = oth_ref[2 * width : 3 * width, :]
    for k, w in enumerate((wq, wk, wv, wo)):
        lanes = slice(k * half, (k + 1) * half)
        w[...] = jnp.concatenate([own_tri[:, lanes], oth_tri[:, lanes]], axis=1)
    wkt[...] = wk[...].T
    wvt[...] = wv[...].T
    small = []
    for ref in (own_ref, oth_ref):
        tail = ref[3 * width : 3 * width + 16, :].astype(F32)
        each = 1 + half_heads
        small.append(tail[0:each] + tail[each : 2 * each] + tail[2 * each : 3 * each])
    hb_s[0:1, :] = jnp.concatenate([member[0:1] for member in small], axis=1)
    hp_s[...] = jnp.concatenate(
        [member[1:, :128] for member in small] + [jnp.zeros((8 - heads, 128), F32)], axis=0
    )
    key_p[...] = key_operand(kp)
    query_p[...] = jnp.zeros_like(query_p)
    for h in range(heads):
        query_p[h, 0:16, :] = query_operand(hp_s, h, qp)
    for ref in (hid_g, vec_g, og, place_g, gate_g, mix_s, att_buf):
        ref[...] = jnp.zeros_like(ref)
    fst_s[kp:, :] = jnp.zeros((qp - kp, width), BF)
    for k in range(images):
        for side in range(2):
            right_s[side, k * qp + kp : (k + 1) * qp, :] = jnp.zeros((qp - kp, hidden), BF)
        for c in range(3):
            dp_s[c, k * qp + kp : (k + 1) * qp, :] = jnp.zeros((qp - kp, width), BF)
    gap = jnp.zeros((qp - kp, width), BF)
    one_lane = (lax.broadcasted_iota(jnp.int32, (qp, qp - width), 1) == 0).astype(BF)
    bias_lane = (lax.broadcasted_iota(jnp.int32, (kp, 128), 1) == 12).astype(BF)

    def columns_at(i):
        return pl.ds(pl.multiple_of(i * qp, 128), qp)


    def first_norm(i):
        for r in range(strips):
            n1, _ = norm_parts(x_ref[i, rows_of(r), :].astype(F32))
            fst_s[rows_of(r), :] = (n1 * v[0] + v[1]).astype(BF)
            yield

    def project(i):
        slot = i % 2
        first_q = fst_s[...]
        first = fst_s[0:kp, :]
        queries = nn(first_q, wq[...]).astype(BF)
        yield
        for h in range(heads):
            qm_s[i, h] = jnp.concatenate([queries * head_mask(qp, width, hd, h), one_lane], axis=1)
            yield
        keys_s[slot, :, 0:width] = nn(first, wk[...]).astype(BF)
        keys_s[slot, :, width:] = bias_ref[i, :, 0 : qp - width]
        yield
        vt_s[slot] = nt(wvt[...], first_q).astype(BF)
        yield
        v_s[i] = nn(first, wv[...]).astype(BF)
        yield
        kt_s[i] = nt(wkt[...], first_q).astype(BF)
        yield
        first_t[:, columns_at(i)] = first_q.T
        yield


    def forward_attention(i):
        held = {}
        slot_i = i % 2

        def scores(h):
            slot = h % 3
            s = nt(keys_s[slot_i], qm_s[i, h])
            p = nn(key_p[...] + bias_ref[i] * bias_lane, query_p[h])
            m, pm = cut(s, 0), cut(p, 0)
            for r in range(strips):
                yield
                s_buf[slot, rows_of(r), :] = cut(s, r)
                p_buf[slot, rows_of(r), :] = cut(p, r)
                m = jnp.maximum(m, cut(s, r))
                pm = jnp.maximum(pm, cut(p, r))
            held["m", h] = jnp.max(m, axis=0, keepdims=True)
            held["pm", h] = jnp.max(pm, axis=0, keepdims=True)

        def exponents(h):
            slot = h % 3
            m, pm = held["m", h], held["pm", h]
            z = jnp.zeros((STRIP, qp), F32)
            pz = jnp.zeros((STRIP, qp), F32)
            for r in range(strips):
                yield
                e = jnp.exp2((s_buf[slot, rows_of(r), :] - m) * c_scale)
                pe = jnp.exp2(p_buf[slot, rows_of(r), :] - pm)
                s_buf[slot, rows_of(r), :] = e
                p_buf[slot, rows_of(r), :] = pe
                z = z + e
                pz = pz + pe
            gate = gate_of(hp_s, h, qp)
            held["a", h] = (1.0 - gate) / jnp.sum(z, axis=0, keepdims=True)
            held["b", h] = gate / jnp.sum(pz, axis=0, keepdims=True)

        def mixing(h):
            slot = h % 3
            a, b = held["a", h], held["b", h]
            for r in range(strips):
                yield
                content = s_buf[slot, rows_of(r), :] * a
                located = p_buf[slot, rows_of(r), :] * b
                soft_s[i, h, 0, rows_of(r), :] = content
                soft_s[i, h, 1, rows_of(r), :] = located
                att_buf[h % 2, rows_of(r), :] = (content + located).astype(BF)
            yield
            mix_s[slot_i, h * hd : (h + 1) * hd, :] = nn(
                vt_s[slot_i, h * hd : (h + 1) * hd, :], att_buf[h % 2]
            ).astype(BF)

        return scores, exponents, mixing


    def feed_forward(i, slot, on):
        spreads = {}

        def strip_rows(r):
            return pl.ds(pl.multiple_of(i * qp + r * STRIP, 16), STRIP)

        rows = pl.ds(pl.multiple_of(i * qp, 16), kp)
        second = {}

        def start():
            attn = nt(mix_s[slot].T[:kp], wo[...])
            for r in range(strips):
                yield
                middle = x_ref[i, rows_of(r), :].astype(F32) + cut(attn, r) + v[4]
                n2, spread = norm_parts(middle)
                mid_s[rows_of(r), :] = middle
                n2_s[rows_of(r), :] = n2
                spreads[r] = spread
                second[r] = (n2 * v[2] + v[3]).astype(BF)
            inc_q = jnp.concatenate([inc_ref[i], gap], axis=0)
            left_t[0, :, columns_at(i)] = inc_q.T
            yield
            second["all"] = jnp.concatenate([second[r] for r in range(strips)], axis=0)
            left_t[1, :, columns_at(i)] = jnp.concatenate([second["all"], gap], axis=0).T

        def chunk(c):
            lanes = pl.ds(c * 256, 256)
            before = nn(second["all"], wi[:, lanes])
            back = nn(inc_ref[i] * on, wn[:, lanes])
            bias_row = hb_s[0:1, lanes]
            total = jnp.zeros((8, 256), F32)
            for r in range(strips):
                yield
                gelu, slope = gelu_parts(cut(before, r) + bias_row)
                right_s[0, strip_rows(r), lanes] = gelu.astype(BF)
                grad_before = cut(back, r) * slope
                right_s[1, strip_rows(r), lanes] = grad_before.astype(BF)
                total = total + fold(grad_before)
            hid_g[:, lanes] += total

        def end():
            grad_second = nt(right_s[1, rows, :], wi[...])
            product = nt(right_s[0, rows, :], wn[...])
            totals = [jnp.zeros((8, width), F32)] * 4
            mids = []
            for r in range(strips):
                yield
                n2 = n2_s[rows_of(r), :]
                res_s[i, rows_of(r), :] = mid_s[rows_of(r), :] + cut(product, r) + v[5]
                incoming = (inc_ref[i, rows_of(r), :] * on).astype(F32)
                g = cut(grad_second, r)
                grad_middle = incoming + norm_back(g * v[2], n2, spreads[r])
                gm_s[i, rows_of(r), :] = grad_middle
                mids.append(grad_middle.astype(BF))
                for k, term in enumerate((g * n2, g, grad_middle, incoming)):
                    totals[k] = totals[k] + fold(term)
            for k in range(4):
                vec_g[k] += totals[k]
            mid_low = jnp.concatenate([*mids, gap], axis=0)
            yield
            dm = nn(mid_low, wo[...]).astype(BF)
            for h in range(heads):
                yield
                dmm_s[i, h] = dm * head_mask(qp, width, hd, h)
            yield
            og[...] += nn(mix_s[slot], mid_low)

        return start, chunk, end

    def together(scores, exponents, mixing, feed, extra):
        for tick in range(heads + 2):
            interleave(
                scores(tick) if tick < heads else None,
                exponents(tick - 1) if 0 <= tick - 1 < heads else None,
                mixing(tick - 2) if 0 <= tick - 2 < heads else None,
                feed[tick] if tick < len(feed) else None,
                extra.get(tick),
            )

    blocks = hidden // 256

    def forward_step(i, carry):
        behind = jnp.maximum(i - 1, 0)
        after = jnp.minimum(i + 1, images - 1)
        start, chunk, end = feed_forward(behind, (i + 1) % 2, (i > 0).astype(BF))
        together(
            *forward_attention(i),
            [start(), *[chunk(c) for c in range(blocks)], end()],
            {heads: first_norm(after), heads + 1: project(after)},
        )
        return carry

    interleave(first_norm(0))
    interleave(project(0))
    lax.fori_loop(0, images, forward_step, 0)
    start, chunk, end = feed_forward(images - 1, (images - 1) % 2, jnp.ones((), BF))
    interleave(start())
    for c in range(blocks):
        interleave(chunk(c))
    interleave(end())
    sent = [
        pltpu.make_async_copy(res_s, res_ref, sems.at[0]),
        pltpu.make_async_copy(gm_s, gm_ref, sems.at[1]),
    ]
    for member in sent:
        member.start()


    def attention_back(i):
        held = {}
        here = i % 2

        def scores(h):
            slot = h % 2
            da = nt(v_s[i], dmm_s[i, h])
            rc = jnp.zeros((STRIP, qp), F32)
            rl = jnp.zeros((STRIP, qp), F32)
            for r in range(strips):
                yield
                part = cut(da, r)
                da_buf[slot, rows_of(r), :] = part
                rc = rc + soft_s[i, h, 0, rows_of(r), :] * part
                rl = rl + soft_s[i, h, 1, rows_of(r), :] * part
            gate = gate_of(hp_s, h, qp)
            held["c", h] = jnp.sum(rc, axis=0, keepdims=True) / (1.0 - gate)
            held["l", h] = jnp.sum(rl, axis=0, keepdims=True) / gate
            gate_g[h : h + 1, :] += held["l", h] - held["c", h]

        def spread(h):
            slot = h % 2
            rc, rl = held["c", h], held["l", h]
            lanes = pl.ds(h * qp, qp)
            for r in range(strips):
                yield
                rows = rows_of(r)
                c = soft_s[i, h, 0, rows, :]
                l = soft_s[i, h, 1, rows, :]
                part = da_buf[slot, rows, :]
                ds_s[here, rows, lanes] = (c * (part - rc)).astype(BF)
                att_s[here, rows, lanes] = (c + l).astype(BF)
                place_g[h, rows, :] += l * (part - rl)

        return scores, spread

    def products(i, there):
        rows = pl.ds(pl.multiple_of(i * qp, 16), kp)
        dq_t = []
        pad = jnp.zeros((qp - kp, qp), BF)
        for h in range(heads):
            yield
            ds = jnp.concatenate([ds_s[there, :, h * qp : (h + 1) * qp], pad], axis=0)
            dq_t.append(nn(kt_s[i, h * hd : (h + 1) * hd, :], ds))
        yield
        dq = (jnp.concatenate(dq_t, axis=0) * back_scale).astype(BF).T[:kp]
        yield
        dp_s[0, rows, :] = dq
        yield
        dk = nn(ds_s[there], qm_s[i].reshape(heads * qp, qp))[:, :width]
        dp_s[1, rows, :] = (dk * back_scale).astype(BF)
        yield
        dv = nn(att_s[there], dmm_s[i].reshape(heads * qp, width))
        dp_s[2, rows, :] = dv.astype(BF)

    def weight_gradient(unit):
        side = unit // blocks
        lanes = pl.ds(pl.multiple_of((unit % blocks) * 256, 128), 256)
        wide_g[side, :, lanes] = nn(left_t[side], right_s[side, :, lanes])
        yield

    def backward_step(i, carry):
        scores, spread = attention_back(i)
        work = products(jnp.maximum(i - 1, 0), (i + 1) % 2)
        for tick in range(heads + 1):
            interleave(
                scores(tick) if tick < heads else None,
                spread(tick - 1) if tick >= 1 else None,
                slow(work, 2),
                weight_gradient(jnp.minimum(i, 2 * blocks - 1)) if tick == 2 else None,
            )
        interleave(work)
        return carry

    lax.fori_loop(0, images, backward_step, 0)
    interleave(products(images - 1, (images - 1) % 2))
    for unit in range(images, 2 * blocks):
        interleave(weight_gradient(unit))
    sent.append(pltpu.make_async_copy(dp_s, dp_ref, sems.at[2]))
    sent[-1].start()

    triple = [nn(first_t[...], dp_s[c]) for c in range(3)]
    parts = offsets(kp, qp)
    rank = rank_ref[0]
    lane = lax.broadcasted_iota(jnp.int32, (1, 128), 1)
    row = jnp.zeros((1, 128), F32)
    for h in range(heads):
        base = ((rank + h // half_heads) % 2) * (4 * half_heads) + h % half_heads
        g = place_g[h]
        for k in range(3):
            total = jnp.sum(g * parts[k])
            row = row + jnp.where(lane == base + k * half_heads, total, 0.0)
        gate = gate_of(hp_s, h, 128)
        total = jnp.sum(gate_g[h : h + 1, :])
        row = row + jnp.where(lane == base + 3 * half_heads, total * gate * (1.0 - gate), 0.0)
    head_ref[...] = row
    if data_count:
        nar_p, out_p, tri_p, tmp = refs[at : at + 4]
        put_planes(nar_p, wide_g[0].T)
        put_planes(out_p, og[...])
        for c in range(3):
            tri_p[0, c * width : (c + 1) * width, 0:half] = triple[c][:, :half]
            tri_p[1, c * width : (c + 1) * width, 0:half] = triple[c][:, half:]
        early = jnp.sum(vec_g[...], axis=1)
        hidden_sum = jnp.sum(hid_g[...], axis=0, keepdims=True)
        rest = width - 128
        wp, np_, op = width // data_count, wide // data_count // 2, half // data_count // 2
        groups = 3 * width // data_count // 4
        small_at = 3 * (wp + np_ + op)
        for r in range(data_count):
            for side in range(2):
                piece = outs[0].at[r] if side == 0 else tmp.at[r % 4]
                for k in range(3):
                    lanes = slice(side * wide + 128 * k, side * wide + 128 * (k + 1))
                    piece[k * wp : (k + 1) * wp, :] = wide_g[1, r * wp : (r + 1) * wp, lanes]
                    piece[small_at + 8 + k : small_at + 9 + k, :] = hidden_sum[:, lanes]
                base = 3 * wp
                tiles = even_odd_tiles(nar_p, side * wide + 2 * np_ * r, np_)
                for k in range(3):
                    piece[base + k * np_ : base + (k + 1) * np_, :] = tiles[k]
                base += 3 * np_
                tiles = even_odd_tiles(out_p, side * half + 2 * op * r, op)
                for k in range(3):
                    piece[base + k * op : base + (k + 1) * op, :] = tiles[k]
                piece[small_at : small_at + 4, :] = early[:, :128]
                piece[small_at + 4 : small_at + 8, 0:rest] = early[:, 128:]
                piece[small_at + 4 : small_at + 8, rest:] = jnp.zeros((4, 128 - rest), F32)
                piece[small_at + 11 : EARLY_ROWS, :] = jnp.zeros(
                    (EARLY_ROWS - small_at - 11, 128), F32
                )
                tiles = four_row_tiles(tri_p, side, 4 * groups * r, groups)
                for k in range(3):
                    at_row = EARLY_ROWS + k * groups
                    piece[at_row : at_row + groups, :] = tiles[k]
                at_row = EARLY_ROWS + 3 * groups
                piece[at_row:CHUNK_ROWS, :] = jnp.zeros((CHUNK_ROWS - at_row, 128), F32)
                if side:
                    outs[1][r] = piece[...].astype(BF)
    else:
        outs[0][...] = wide_g[0].T
        outs[1][...] = wide_g[1]
        outs[2][...] = og[...]
        outs[3][...] = vec_g[...]
        outs[4][...] = hid_g[...]
        for c in range(3):
            outs[5][c * width : (c + 1) * width, :] = triple[c]
    for member in sent:
        member.wait()


def run_layer(rank, x, inc, bias, own, oth, vec, heads, patches, data_count):
    images, kp, width = x.shape
    qp = -(-patches // 128) * 128
    hidden = 2 * own.shape[1]
    full = images * qp
    if data_count:
        outs = [sds(data_count, CHUNK_ROWS, 128), sds(data_count, CHUNK_ROWS, 128, dtype=BF)]
    else:
        outs = [
            sds(hidden, width),
            sds(width, hidden),
            sds(width, width),
            sds(4, 8, width),
            sds(8, hidden),
            sds(3 * width, width),
        ]

    def bf(*dims):
        return pltpu.VMEM(dims, BF)

    def f32(*dims):
        return pltpu.VMEM(dims, F32)

    scratch = [
        *[bf(width, width)] * 6,
        bf(width, hidden),
        bf(width, hidden),
        f32(8, hidden),
        f32(8, 128),
        bf(kp, 128),
        bf(heads, 128, qp),
        bf(qp, width),
        bf(2, kp, qp),
        bf(2, width, qp),
        bf(images, heads, qp, qp),
        bf(images, heads, qp, width),
        bf(images, kp, width),
        bf(images, width, qp),
        f32(images, heads, 2, kp, qp),
        bf(2, width, qp),
        f32(kp, width),
        f32(kp, width),
        bf(width, full),
        bf(2, width, full),
        bf(2, full, hidden),
        f32(images, kp, width),
        f32(images, kp, width),
        bf(3, full, width),
        f32(3, kp, qp),
        f32(3, kp, qp),
        bf(2, qp, qp),
        f32(heads, kp, qp),
        f32(8, qp),
        f32(2, kp, qp),
        bf(2, kp, heads * qp),
        bf(2, kp, heads * qp),
        f32(2, width, hidden),
        f32(4, 8, width),
        f32(8, hidden),
        f32(width, width),
        pltpu.SemaphoreType.DMA((3,)),
    ]
    if data_count:
        scratch += [f32(2, hidden, 128), f32(2, width, 128), f32(2, 3 * width, 128)]
        scratch.append(f32(4, CHUNK_ROWS, 128))
    anywhere = pl.BlockSpec(memory_space=pl.ANY)
    return pl.pallas_call(
        functools.partial(layer_kernel, patches=patches, heads=heads, data_count=data_count),
        out_shape=(
            sds(images, kp, width),
            sds(images, kp, width),
            sds(3, full, width, dtype=BF),
            sds(1, 128),
            *outs,
        ),
        in_specs=[SM] + [VM] * 6,
        out_specs=(anywhere,) * 3 + (VM,) * (1 + len(outs)),
        scratch_shapes=scratch,
        compiler_params=PARAMS,
        name="layer",
    )(rank, x, inc, bias, own, oth, vec)


def whole(*dims):
    return pl.BlockSpec(dims, lambda i: (0,) * len(dims))


def paired(*dims):
    return pl.BlockSpec((PAIR, *dims), lambda i: (i,) + (0,) * len(dims))


def input_kernel(x_ref, gm_ref, dp_ref, own_ref, oth_ref, vec_ref, gi_ref, vec_out, w, vec_g, *, patches):
    step = pl.program_id(0)
    kp, width = gm_ref.shape[1:]
    qp = dp_ref.shape[1] // PAIR
    half = width // 2

    @pl.when(step == 0)
    def _():
        own_tri = own_ref[2 * width : 3 * width, :]
        oth_tri = oth_ref[2 * width : 3 * width, :]
        for at in range(3):
            span = slice(at * half, (at + 1) * half)
            w[at] = jnp.concatenate([own_tri[:, span], oth_tri[:, span]], axis=1)
        vec_g[...] = jnp.zeros_like(vec_g)

    gain = vec_ref[0:1, :]
    done = []
    for at in range(PAIR):
        n1, spread = norm_parts(x_ref[at].astype(F32))
        g = sum(nt(dp_ref[c, at * qp : at * qp + kp, :], w[c]) for c in range(3))
        vec_g[0] += fold(g * n1)
        vec_g[1] += fold(g)
        done.append(gm_ref[at] + norm_back(g * gain, n1, spread))
    gi_ref[...] = jnp.concatenate([member[:patches] for member in done], axis=0)

    @pl.when(step == pl.num_programs(0) - 1)
    def _():
        vec_out[...] = jnp.sum(vec_g[...], axis=1)


def run_input(x, gm, dp, own, oth, vec, patches):
    images, kp, width = gm.shape
    qp = dp.shape[1] // images
    return pl.pallas_call(
        functools.partial(input_kernel, patches=patches),
        grid=(images // PAIR,),
        out_shape=(sds(images * patches, width), sds(2, width)),
        in_specs=[
            paired(kp, width),
            paired(kp, width),
            pl.BlockSpec((3, PAIR * qp, width), lambda i: (0, i, 0)),
            whole(*own.shape),
            whole(*own.shape),
            whole(*vec.shape),
        ],
        out_specs=(
            pl.BlockSpec((PAIR * patches, width), lambda i: (i, 0)),
            whole(2, width),
        ),
        scratch_shapes=[pltpu.VMEM((3, width, width), BF), pltpu.VMEM((2, 8, width), F32)],
        compiler_params=PARAMS,
        name="input_gradient",
    )(x, gm, dp, own, oth, vec)


def combine_kernel(own_ref, got_ref, out_ref):
    out_ref[...] = (own_ref[...] + got_ref[...].astype(F32)).astype(BF)


def run_combine(own, got):
    return pl.pallas_call(
        combine_kernel,
        out_shape=sds(*own.shape, dtype=BF),
        in_specs=[VM] * 2,
        out_specs=VM,
        compiler_params=PARAMS,
        name="combine",
    )(own, got)


def pick_rows(ref, start, count, flip=False):
    total = ref.shape[1] if flip else ref.shape[0]
    row = lax.broadcasted_iota(jnp.int32, (count, total), 0) + start
    col = lax.broadcasted_iota(jnp.int32, (count, total), 1)
    chosen = (row == col).astype(F32)
    return lax.dot_general(
        chosen,
        ref[...],
        (((1,), (1 if flip else 0,)), ((), ())),
        preferred_element_type=F32,
        precision=lax.Precision.HIGHEST,
    )


def share_kernel(rank_ref, _, tri_ref, out_ref, wid_ref, nar_ref, *refs, data_count):
    (wt_f, wo_f, ww_f, wn_f, st, so, sw, sn) = refs
    width, wide = wid_ref.shape
    half = out_ref.shape[0]
    wp, np_, op = width // data_count, wide // data_count // 2, half // data_count // 2
    data_rank = rank_ref[1]
    groups = tri_ref.shape[0] // data_count // 4
    st[0, :, 0 : tri_ref.shape[1]] = pick_rows(tri_ref, data_rank * 4 * groups, 4 * groups)
    put_planes(so, pick_rows(out_ref, data_rank * 2 * op, 2 * op))
    sw[...] = pick_rows(wid_ref, data_rank * wp, wp)
    put_planes(sn, pick_rows(nar_ref, data_rank * 2 * np_, 2 * np_, flip=True))
    tiles = four_row_tiles(st, 0, 0, groups)
    for p in range(groups):
        for k in range(3):
            tile = 128 * (3 * p + k)
            wt_f[0:1, tile : tile + 128] = tiles[k][p : p + 1, :]
    for ref, flat, pairs in ((so, wo_f, op), (sn, wn_f, np_)):
        tiles = even_odd_tiles(ref, 0, pairs)
        for p in range(pairs):
            for k in range(3):
                tile = 128 * (3 * p + k)
                flat[0:1, tile : tile + 128] = tiles[k][p : p + 1, :]
    for p in range(wp):
        ww_f[0:1, wide * p : wide * (p + 1)] = sw[p : p + 1, :]


def run_shares(rank, after, tri, out, wid, nar_t, data_count):
    wide = wid.shape[1]
    share = [member.shape[0] // data_count for member in (tri, out, wid)]
    return pl.pallas_call(
        functools.partial(share_kernel, data_count=data_count),
        out_shape=tuple(sds(1, member.size // data_count) for member in (tri, out, wid, nar_t)),
        in_specs=[SM] + [VM] * 5,
        out_specs=(VM,) * 4,
        scratch_shapes=[
            pltpu.VMEM((1, share[0], 128), F32),
            pltpu.VMEM((2, share[1], 128), F32),
            pltpu.VMEM((share[2], wide), F32),
            pltpu.VMEM((2, wide // data_count, 128), F32),
        ],
        compiler_params=PARAMS,
        name="weight_shares",
    )(rank, after, tri, out, wid, nar_t)


def spread_rows(flat_ref, from_ref, base, blocks):
    for p in range(blocks):
        for k in range(3):
            at = base + k * blocks + p
            tile = 128 * (3 * p + k)
            flat_ref[0:1, tile : tile + 128] = from_ref[at : at + 1, :]


def sum_kernel(rank_ref, got_ref, late_ref, head_ref, _, *refs, blocks):
    (tri_f, out_f, wid_f, nar_f, vec_ref, hid_ref, pay_ref, tot) = refs
    width = late_ref.shape[1]
    tri_b, out_b, wid_b, nar_b = blocks
    tot[...] = jnp.sum(got_ref[...].astype(F32), axis=0)
    spread_rows(wid_f, tot, 0, wid_b)
    spread_rows(nar_f, tot, 3 * wid_b, nar_b)
    spread_rows(out_f, tot, 3 * (wid_b + nar_b), out_b)
    spread_rows(tri_f, tot, EARLY_ROWS, tri_b)
    at = 3 * (wid_b + nar_b + out_b)
    vec_ref[...] = jnp.concatenate(
        [tot[at : at + 4, :], tot[at + 4 : at + 8, : width - 128]], axis=1
    )
    hid = jnp.concatenate([tot[at + 8 + k : at + 9 + k, :] for k in range(3)], axis=1)
    hid_ref[...] = hid
    early = tot[0:at, :]
    late = tot[EARLY_ROWS : EARLY_ROWS + 3 * tri_b, :]
    squares = jnp.sum(early * early) + jnp.sum(late * late)
    squares = squares + jnp.where(rank_ref[1] == 0, jnp.sum(hid * hid), 0.0)
    lane = lax.broadcasted_iota(jnp.int32, (1, 128), 1)
    tails = jnp.concatenate([late_ref[0:1, 128:], late_ref[1:2, 128:]], axis=1)
    payload = jnp.concatenate(
        [late_ref[:, :128], tails, jnp.where(lane == 127, squares, head_ref[...])], axis=0
    )
    pay_ref[...] = jnp.broadcast_to(payload[None], pay_ref.shape)


def run_sums(rank, got, late_vec, head, after, blocks, wide):
    count = got.shape[0]
    width = late_vec.shape[1]
    return pl.pallas_call(
        functools.partial(sum_kernel, blocks=blocks),
        out_shape=(
            *[sds(1, 3 * 128 * member) for member in blocks],
            sds(4, width),
            sds(1, wide),
            sds(2 * count, 4, 128),
        ),
        in_specs=[SM] + [VM] * 4,
        out_specs=(VM,) * 7,
        scratch_shapes=[pltpu.VMEM((EARLY_ROWS + LATE_ROWS, 128), F32)],
        compiler_params=PARAMS,
        name="sums",
    )(rank, got, late_vec, head, after)


def adam_parts(weight, gradient, moment, squares, rate, decay):
    moment_new = BETA_ONE * moment + (1.0 - BETA_ONE) * gradient
    squares_new = BETA_TWO * squares + (1.0 - BETA_TWO) * gradient * gradient
    quotient = (moment_new / (1.0 - BETA_ONE**STEP)) / (
        jnp.sqrt(squares_new / (1.0 - BETA_TWO**STEP)) + ADAM_EPS
    )
    return moment_new, squares_new, weight - rate * (quotient + decay * weight)


def adam_kernel(rank_ref, got_ref, early_ref, hid_ref, hp_ref, vec_ref, hb_ref, *refs):
    grads = refs[0:4]
    weights = refs[4:8]
    states = refs[8:22]
    outs = refs[22:43]
    norm_ref = refs[43]
    width = vec_ref.shape[1]
    half_heads = hp_ref.shape[0]
    tail = width - 128
    total = jnp.sum(got_ref[...], axis=0)
    late = jnp.concatenate(
        [
            total[0:2, :],
            jnp.concatenate([total[2:3, :tail], total[2:3, tail : 2 * tail]], axis=0),
        ],
        axis=1,
    )
    vector = jnp.concatenate([late, early_ref[...]], axis=0)
    lane = lax.broadcasted_iota(jnp.int32, (1, 128), 1)
    heads_row = jnp.where(lane < 8 * half_heads, total[3:4, :], 0.0)
    squares = (
        jnp.sum(jnp.where(lane == 127, total[3:4, :], 0.0))
        + jnp.sum(vector * vector)
        + jnp.sum(heads_row * heads_row)
    )
    norm = jnp.sqrt(jnp.full((1, 128), squares))
    norm_ref[0] = jnp.sum(norm[:, 0:1])
    factor = (CLIP_AT / jnp.maximum(norm, CLIP_AT))[:, 0:1]
    span = 4 * half_heads
    mine = jnp.where(rank_ref[0] == 0, heads_row[:, :span], heads_row[:, span : 2 * span])
    head = jnp.concatenate(
        [
            jnp.concatenate(
                [mine[:, c * half_heads + h : c * half_heads + h + 1] for c in range(4)], axis=1
            )
            for h in range(half_heads)
        ],
        axis=0,
    )
    given = [ref[...] for ref in grads] + [vector, hid_ref[...], head]
    wide = hid_ref.shape[1]
    held = [ref[...] for ref in weights] + [vec_ref[...], hb_ref[...].reshape(1, wide), hp_ref[...]]
    for at in range(7):
        renewed = adam_parts(
            held[at],
            given[at] * factor,
            states[2 * at][...].reshape(held[at].shape),
            states[2 * at + 1][...].reshape(held[at].shape),
            RATES[at],
            DECAYS[at],
        )
        for step in range(3):
            out = outs[3 * at + step]
            out[...] = renewed[step].reshape(out.shape)


def run_adam(rank, got, early, hid, hp_t, vec, hb, grads, weights, states):
    shapes = []
    for at in range(7):
        shapes += [sds(*states[2 * at].shape)] * 3
    return pl.pallas_call(
        adam_kernel,
        out_shape=(*shapes, sds(1)),
        in_specs=[SM] + [VM] * (6 + 4 + 4 + 14),
        out_specs=(VM,) * 21 + (SM,),
        compiler_params=PARAMS,
        name="adam",
    )(rank, got, early, hid, hp_t, vec, hb, *grads, *weights, *states)


def plain_chunks(halves, data_count, rows):
    sides = []
    for side in range(2):
        flat = jnp.concatenate([own_first[side].reshape(data_count, -1) for own_first in halves], axis=1)
        flat = jnp.pad(flat, ((0, 0), (0, rows * 128 - flat.shape[1])))
        sides.append(flat.reshape(data_count, rows, 128))
    return sides[0], sides[1].astype(BF)


def on_device(
    tokens,
    cotangent,
    keep_mask,
    triple_weight,
    outward_weight,
    widen_weight,
    narrow_weight,
    vectors,
    hidden_bias,
    head_params,
    triple_moment,
    triple_square,
    outward_moment,
    outward_square,
    widen_moment,
    widen_square,
    narrow_moment,
    narrow_square,
    vector_moment,
    vector_square,
    hidden_moment,
    hidden_square,
    head_moment,
    head_square,
):
    tensor_rank = lax.axis_index("tensor")
    data_rank = lax.axis_index("dp")
    data_count = lax.axis_size("dp")
    images = keep_mask.shape[0] // 2
    patches = keep_mask.shape[1]
    heads = 2 * head_params.shape[1]
    depth = triple_weight.shape[1]
    half = triple_weight.shape[2]
    wide = widen_weight.shape[1]
    rank = jnp.stack([tensor_rank, data_rank]).astype(jnp.int32)
    triple_rows = triple_weight.reshape(3 * depth, half)
    narrow_t = narrow_weight.T
    head_t = head_params.T
    fast = (
        depth == 192
        and half == 96
        and wide == 384
        and depth % data_count == 0
        and wide % (2 * data_count) == 0
        and half % (2 * data_count) == 0
        and 3 * depth % (4 * data_count) == 0
    )
    chunked = data_count if fast else 0
    swap = [(0, 1), (1, 0)]

    own = run_pack(triple_weight, outward_weight, widen_weight, narrow_t, hidden_bias, head_t)
    other = lax.ppermute(own, "tensor", swap)
    x, inc, bias = run_prepare(rank, tokens.T, cotangent.T, keep_mask)
    result, grad_middle, dp, head_row, *sums = run_layer(
        rank, x, inc, bias, own, other, vectors, heads, patches, chunked
    )
    if fast:
        mine, theirs = sums
    else:
        nar_g, wid_g, out_g, vec_g, hid_g, tri_g = sums
        early_mine = jnp.sum(vec_g, axis=1).reshape(1, -1)
        early_both = jnp.broadcast_to(early_mine, (data_count, early_mine.size))
        hidden_both = jnp.broadcast_to(
            jnp.sum(hid_g, axis=0).reshape(2, 1, wide), (2, data_count, wide)
        )
        early = plain_chunks(
            [
                wid_g.reshape(depth, 2, wide).transpose(1, 0, 2),
                nar_g.reshape(2, -1),
                out_g.reshape(2, -1),
                (early_both, early_both),
                hidden_both,
            ],
            data_count,
            EARLY_ROWS,
        )
        late = plain_chunks(
            [tri_g.reshape(3 * depth, 2, half).transpose(1, 0, 2)], data_count, LATE_ROWS
        )
        mine, theirs = (jnp.concatenate(pair, axis=1) for pair in zip(early, late))
    chunks = run_combine(mine, lax.ppermute(theirs, "tensor", swap))
    got = lax.all_to_all(chunks, "dp", 0, 0, tiled=False)
    grad_input, late_vec = run_input(x, grad_middle, dp, own, other, vectors, patches)
    if fast:
        wt_f, wo_f, ww_f, wn_f = run_shares(
            rank, head_row, triple_rows, outward_weight, widen_weight, narrow_t, data_count
        )
        blocks = [
            member.size // data_count // 384
            for member in (triple_rows, outward_weight, widen_weight, narrow_t)
        ]
        tri_f, out_f, wid_f, nar_f, early_vec, hid, payload = run_sums(
            rank, got, late_vec, head_row, wo_f, blocks, wide
        )
    else:
        total = jnp.sum(got.astype(F32), axis=0)
        early_sum = total[:EARLY_ROWS].reshape(1, -1)
        masters = (widen_weight, narrow_weight, outward_weight)
        sizes = [member.size // data_count for member in masters] + [4 * depth, wide]
        cuts = [sum(sizes[:at]) for at in range(6)]
        wid_f, nar_f, out_f, early_vec, hid = (
            early_sum[:, cuts[at] : cuts[at + 1]] for at in range(5)
        )
        early_vec = early_vec.reshape(4, depth)
        share = triple_rows.size // data_count
        tri_f = total[EARLY_ROWS:].reshape(1, -1)[:, :share]

        def weight_share(member):
            length = member.size // data_count
            return lax.dynamic_slice_in_dim(member.reshape(1, -1), data_rank * length, length, 1)

        ww_f, wn_f, wo_f = (weight_share(member) for member in masters)
        wt_f = weight_share(triple_rows)
        squares = sum(jnp.sum(member * member) for member in (wid_f, nar_f, out_f, tri_f))
        squares = squares + jnp.where(data_rank == 0, jnp.sum(hid * hid), 0.0)
        lane = lax.broadcasted_iota(jnp.int32, (1, 128), 1)
        payload = jnp.concatenate(
            [
                late_vec[:, :128],
                late_vec[:, 128:].reshape(1, 128),
                jnp.where(lane == 127, squares, head_row),
            ]
        )
        payload = jnp.broadcast_to(payload[None], (2 * data_count, 4, 128))
    last_got = lax.all_to_all(payload, ("dp", "tensor"), 0, 0, tiled=False)
    renewed = run_adam(
        rank,
        last_got,
        early_vec,
        hid,
        head_t,
        vectors,
        hidden_bias,
        (tri_f, out_f, wid_f, nar_f),
        (wt_f, wo_f, ww_f, wn_f),
        (
            triple_moment,
            triple_square,
            outward_moment,
            outward_square,
            widen_moment,
            widen_square,
            narrow_moment,
            narrow_square,
            vector_moment,
            vector_square,
            hidden_moment,
            hidden_square,
            head_moment.T,
            head_square.T,
        ),
    )
    hidden_new = renewed[15:18]
    head_new = [member.T for member in renewed[18:21]]
    result = result[:, :patches].reshape(images * patches, depth)
    return (result, grad_input, *renewed[:15], *hidden_new, *head_new, renewed[21].reshape(()))


def solution(mesh):
    return jax.shard_map(
        on_device,
        mesh=mesh,
        in_specs=(
            P(("dp", "tensor"), None),
            P(("dp", "tensor"), None),
            P("dp", None),
            P(None, None, "tensor"),
            P("tensor", None),
            P(None, "tensor"),
            P("tensor", None),
            P(),
            P("tensor"),
            P(None, "tensor"),
            P("tensor", "dp"),
            P("tensor", "dp"),
            P("tensor", "dp"),
            P("tensor", "dp"),
            P("tensor", "dp"),
            P("tensor", "dp"),
            P("tensor", "dp"),
            P("tensor", "dp"),
            P(),
            P(),
            P("tensor"),
            P("tensor"),
            P(None, "tensor"),
            P(None, "tensor"),
        ),
        out_specs=(
            P(("dp", "tensor"), None),
            P(("dp", "tensor"), None),
            P("tensor", "dp"),
            P("tensor", "dp"),
            P("tensor", "dp"),
            P("tensor", "dp"),
            P("tensor", "dp"),
            P("tensor", "dp"),
            P("tensor", "dp"),
            P("tensor", "dp"),
            P("tensor", "dp"),
            P("tensor", "dp"),
            P("tensor", "dp"),
            P("tensor", "dp"),
            P(),
            P(),
            P(),
            P("tensor"),
            P("tensor"),
            P("tensor"),
            P(None, "tensor"),
            P(None, "tensor"),
            P(None, "tensor"),
            P(),
        ),
        check_vma=False,
    )
```

time: 103 us -> 86 us (0.83)
  Pallas kernels: 64.7 us -> 53.2 us
  waiting for transfers between devices: 4.54 us -> 12.8 us
  local copies, waits for them, and re-layouts: 11.9 us -> 6.37 us
  starting transfers between devices: 16.3 us -> 11.6 us
  other arithmetic: 4.36 us -> 0.66 us
    pallas_call x6 -> x7, Pallas kernels: 62.5 us -> 51 us  [the longest x1 32.8 us: run_layer(): pl.pallas_call(functools.partial(layer_kernel, patches=patches, heads=hea...]
    all_to_all x3 -> x2, waiting for transfers between devices: 4.53 us -> 10.8 us  [the longest x1 6.76 us: on_device(): got = lax.all_to_all(chunks, 'dp', 0, 0, tiled=False)]
    all_to_all x3 -> x2, starting transfers between devices: 15.9 us -> 11.1 us  [the longest x1 8.01 us: on_device(): got = lax.all_to_all(chunks, 'dp', 0, 0, tiled=False)]
    pallas_call x3 -> x0, other arithmetic: 3.76 us -> none  [run_adam(): pl.pallas_call(adam_kernel, out_shape=(*shapes, sds(1, 1)), in_specs=[SM]...]
    unnamed x24 -> x13, local copies, waits for them, and re-layouts: 8.2 us -> 4.55 us
    ppermute x1 -> x2, waiting for transfers between devices: 0.01 us -> 2.07 us  [the longest x1 2.07 us: on_device(): chunks = run_combine(mine, lax.ppermute(theirs, 'tensor', swap))]
    broadcast_in_dim x1 -> x0, local copies, waits for them, and re-layouts: 1.22 us -> none  [on_device(): jnp.broadcast_to(jnp.pad(keep_here, ((0, 0), (0, kp - patches)))[:, :, No...]
    reshape x3 -> x2, local copies, waits for them, and re-layouts: 2.5 us -> 1.69 us  [on_device(): result = result[:, :patches].reshape(images * patches, depth)]
  transfers between devices with their start and end apart: 4 -> 4, of which waited for: 3 -> 3; matrix products, arithmetic and copies ran while one was open for 8% -> 5% of each run, Pallas kernels for 28% -> 14%
where the time goes in v2:
time: 86 us; the launch traced here: 85.4 us
  Pallas kernels  53.2 us (62%)
  waiting for transfers between devices  12.8 us (15%)
  starting transfers between devices  11.6 us (13%)
  local copies, waits for them, and re-layouts  6.37 us (7%)
    pallas_call x1, Pallas kernels, run_layer(): pl.pallas_call(functools.partial(layer_kernel, patches=patches, heads=hea...  32.8 us
    all_to_all x1, starting transfers between devices, on_device(): got = lax.all_to_all(chunks, 'dp', 0, 0, tiled=False)  8.01 us
    all_to_all x1, waiting for transfers between devices, on_device(): got = lax.all_to_all(chunks, 'dp', 0, 0, tiled=False)  6.76 us
    pallas_call x1, Pallas kernels, run_input(): pl.pallas_call(functools.partial(input_kernel, patches=patches), grid=(im...  6.02 us
    unnamed x13, local copies, waits for them, and re-layouts  4.55 us
    all_to_all x1, waiting for transfers between devices, on_device(): last_got = lax.all_to_all(payload, ('dp', 'tensor'), 0, 0, tiled=False)  4.01 us
    pallas_call x1, Pallas kernels, run_prepare(): pl.pallas_call(prepare_kernel, out_shape=(rows, rows, sds(images, kp, 128...  3.27 us
    all_to_all x1, starting transfers between devices, on_device(): last_got = lax.all_to_all(payload, ('dp', 'tensor'), 0, 0, tiled=False)  3.06 us
  transfers between devices with their start and end apart: 4, of which 3 were waited for; matrix products, arithmetic and copies ran while one was open for 5% of the time, Pallas kernels for 14%

profile of v2, /device:TPU:0, one launch (start us, length us, event | category | flops | bytes accessed | tf_op | source)
XLA Modules:
  0.0 85.4 jit_solution(254491915826981074)
XLA Ops:
  0.7 2.2 %pack_weights.1.refs_4_.own_ref = bf16[592,384]{1,0:T(8,128)(2,1)} custom-call(f32[3,192,96]{2,1,0:T(8,128)} %tri_ref.1, f32[96,192]{1,0:T(8,128)} %out_ref.3, f32[192,384]{1,0:T(8,128)} %wid_ref.3, f32[192,384]{1,0:T(8,128)} %bitcast.14, f32[384]{0:T(512)} %hb_ref.3, f32[2,4]{1,0:T(2,128)} %bitcast.18), custom_call_target="tpu_custom_call" | custom-call | tf_op jit(solution)/shard_map/pack_weights/pallas_call | solution.py:201
  2.9 0.5 collective-permute-start
  3.3 0.7 pad_add_fusion.rank_ref.refs_0_
  4.0 3.3 %prepare.1 = (bf16[8,208,192]{2,1,0:T(8,128)(2,1)}, bf16[8,208,192]{2,1,0:T(8,128)(2,1)}, bf16[8,208,128]{2,1,0:T(8,128)(2,1)}) custom-call(s32[2]{0:T(128)} %pad_add_fusion.rank_ref.refs_0_, bf16[192,1568]{1,0:T(8,128)(2,1)} %bitcast.16, bf16[192,1568]{1,0:T(8,128)(2,1)} %bitcast.17, s32[16,196]{1,0:T(8,128)} %keep_ref.1), custom_call_target="tpu_custom_call" | custom-call | tf_op jit(solution)/shard_map/prepare/pallas_call | solution.py:236
  7.2 0.0 collective-permute-done.refs_5_.oth_ref
  7.2 0.0 copy-start.1
  7.2 0.8 copy-done.1
  8.0 32.8 %layer.1 = (f32[8,208,192]{2,1,0:T(8,128)}, f32[8,208,192]{2,1,0:T(8,128)}, bf16[3,2048,192]{2,1,0:T(8,128)(2,1)}, f32[1,128]{1,0:T(1,128)}, f32[16,128,128]{2,1,0:T(8,128)}, /*index=5*/bf16[16,128,128]{2,1,0:T(8,128)(2,1)}) custom-call(s32[2]{0:T(128)} %pad_add_fusion.rank_ref.refs_0_, bf16[8,208,192]{2,1,0:T(8,128)(2,1)} %get-tuple-element.68.refs_1_.x_ref, ...), custom_call_target="tpu_custom_call" | custom-call | tf_op jit(solution)/shard_map/layer/pallas_call | solution.py:717
  40.8 0.1 collective-permute-start.1
  40.9 2.1 %collective-permute-done.1.got_ref = bf16[16,128,128]{2,1,0:T(8,128)(2,1)S(1)} collective-permute-done((bf16[16,128,128]{2,1,0:T(8,128)(2,1)}, bf16[16,128,128]{2,1,0:T(8,128)(2,1)S(1)}, u32[]{:S(2)}, u32[]{:S(2)}) %collective-permute-start.1) | collective-permute-done | bytes 524320 | tf_op jit(solution)/shard_map/ppermute | solution.py:1094
  43.0 0.0 copy-start.4
  43.0 0.8 copy-done.4
  43.8 2.3 %combine.1 = bf16[16,128,128]{2,1,0:T(8,128)(2,1)} custom-call(f32[16,128,128]{2,1,0:T(8,128)} %get-tuple-element.75.own_ref, bf16[16,128,128]{2,1,0:T(8,128)(2,1)} %copy-done.4), custom_call_target="tpu_custom_call" | custom-call | tf_op jit(solution)/shard_map/combine/pallas_call | solution.py:802
  46.1 8.0 %all-to-all-start = ((bf16[16,128,128]{2,1,0:T(8,128)(2,1)}), bf16[16,128,128]{2,1,0:T(8,128)(2,1)S(1)}, u32[]{:S(2)}, u32[]{:S(2)}) async-start(bf16[16,128,128]{2,1,0:T(8,128)(2,1)} %combine.1), calls=%async_computation | async-start | bytes 1048576 | tf_op jit(solution)/shard_map/all_to_all | solution.py:1095
  54.1 2.7 %weight_shares.1 = (f32[1,3456]{1,0:T(1,128)}, f32[1,1152]{1,0:T(1,128)}, f32[1,4608]{1,0:T(1,128)}, f32[1,4608]{1,0:T(1,128)}) custom-call(s32[2]{0:T(128)} %pad_add_fusion.rank_ref.refs_0_, f32[1,128]{1,0:T(1,128)} %get-tuple-element.78._.head_ref, f32[576,96]{1,0:T(8,128)} %bitcast.13, f32[96,192]{1,0:T(8,128)} %out_ref.3, f32[192,384]{1,0:T(8,128)} %wid_ref.3, ...), custom_call_target="tpu_custom_call" | custom-call | tf_op jit(solution)/shard_map/weight_shares/pallas_call | solution.py:855
  56.8 0.0 copy-start.3
  56.8 6.0 %input_gradient.1 = (f32[1568,192]{1,0:T(8,128)}, f32[2,192]{1,0:T(2,128)}) custom-call(bf16[8,208,192]{2,1,0:T(8,128)(2,1)} %get-tuple-element.68.refs_1_.x_ref, f32[8,208,192]{2,1,0:T(8,128)} %get-tuple-element.72.gm_ref, bf16[3,2048,192]{2,1,0:T(8,128)(2,1)} %get-tuple-element.73.dp_ref, bf16[592,384]{1,0:T(8,128)(2,1)} %pack_weights.1.refs_4_.own_ref, ...), custom_call_target="tpu_custom_call" | custom-call | tf_op jit(solution)/shard_map/input_gradient/pallas_call | solution.py:775
  62.8 6.8 %all-to-all-done.got_ref = bf16[16,128,128]{2,1,0:T(8,128)(2,1)S(1)} async-done(((bf16[16,128,128]{2,1,0:T(8,128)(2,1)}), bf16[16,128,128]{2,1,0:T(8,128)(2,1)S(1)}, u32[]{:S(2)}, u32[]{:S(2)}) %all-to-all-start) | async-done | bytes 524320 | tf_op jit(solution)/shard_map/all_to_all | solution.py:1095
  69.6 0.0 copy-start
  69.6 0.8 copy-done
  70.4 1.9 %sums.1 = (f32[1,3456]{1,0:T(1,128)}, f32[1,1152]{1,0:T(1,128)}, f32[1,4608]{1,0:T(1,128)}, f32[1,4608]{1,0:T(1,128)}, f32[4,192]{1,0:T(4,128)}, /*index=5*/f32[1,384]{1,0:T(1,128)}, f32[32,4,128]{2,1,0:T(4,128)}) custom-call(s32[2]{0:T(128)} %pad_add_fusion.rank_ref.refs_0_, bf16[16,128,128]{2,1,0:T(8,128)(2,1)} %copy-done, ...), custom_call_target="tpu_custom_call" | custom-call | tf_op jit(solution)/shard_map/sums/pallas_call | solution.py:909
  72.3 3.1 %all-to-all-start.1 = ((f32[32,4,128]{2,1,0:T(4,128)}), f32[32,4,128]{2,1,0:T(4,128)S(1)}, u32[]{:S(2)}, u32[]{:S(2)}) async-start(f32[32,4,128]{2,1,0:T(4,128)} %get-tuple-element.80), calls=%async_computation.1 | async-start | bytes 131072 | tf_op jit(solution)/shard_map/all_to_all | solution.py:1138
  75.4 0.0 copy-done.3
  75.4 0.1 slice.3
  75.5 0.2 reshape.60
  75.7 0.0 copy-start.2
  75.7 1.5 %copy.52 = f32[1568,192]{0,1:T(8,128)} copy(f32[1568,192]{1,0:T(8,128)S(1)} %reshape.60) | data formatting | bytes 2408448 | tf_op jit(solution)/shard_map/reshape | solution.py:1168
  77.2 0.0 copy-done.2
  77.2 1.5 %copy.51 = f32[1568,192]{0,1:T(8,128)} copy(f32[1568,192]{1,0:T(8,128)S(1)} %copy-done.2) | data formatting | bytes 2408448
  78.8 4.0 %all-to-all-done.1.got_ref = f32[32,4,128]{2,1,0:T(4,128)S(1)} async-done(((f32[32,4,128]{2,1,0:T(4,128)}), f32[32,4,128]{2,1,0:T(4,128)S(1)}, u32[]{:S(2)}, u32[]{:S(2)}) %all-to-all-start.1) | async-done | bytes 65568 | tf_op jit(solution)/shard_map/all_to_all | solution.py:1138
  82.8 0.0 copy-start.5
  82.8 0.6 copy-done.5
  83.4 2.0 %adam.1 = (f32[1,3456]{1,0:T(1,128)}, f32[1,3456]{1,0:T(1,128)}, f32[1,3456]{1,0:T(1,128)}, f32[1,1152]{1,0:T(1,128)}, f32[1,1152]{1,0:T(1,128)}, /*index=5*/f32...) custom-call(s32[2]{0:T(128)} %pad_add_fusion.rank_ref.refs_0_, ...), custom_call_target="tpu_custom_call" | custom-call | tf_op jit(solution)/shard_map/adam/pallas_call | solution.py:994
Async XLA Ops:
  2.9 4.4 %collective-permute-start = (bf16[592,384]{1,0:T(8,128)(2,1)}, bf16[592,384]{1,0:T(8,128)(2,1)S(1)}, u32[]{:S(2)}, u32[]{:S(2)}) collective-permute-start(bf16[592,384]{1,0:T(8,128)(2,1)} %pack_weights.1.refs_4_.own_ref), channel_id=1, source_target_pairs={{0,1},{1,0},{2,3},{3,2},{4,5},{5,4},{6,7},{7,6},{8,9},{9,8},{10,11... | collective-permute-start | bytes 1363976 | tf_op jit(solution)/shard_map/ppermute | solution.py:1065
  7.2 0.8 copy-start.1
  40.8 2.2 %collective-permute-start.1 = (bf16[16,128,128]{2,1,0:T(8,128)(2,1)}, bf16[16,128,128]{2,1,0:T(8,128)(2,1)S(1)}, u32[]{:S(2)}, u32[]{:S(2)}) collective-permute-start(bf16[16,128,128]{2,1,0:T(8,128)(2,1)} %get-tuple-element.76), channel_id=1, source_target_pairs={{0,1},{1,0},{2,3},{3,2},{4,5},{5,4},{6,7},{7,6},{8,9},{9,8},{10,11... | collective-permute-start | bytes 1572872 | tf_op jit(solution)/shard_map/ppermute | solution.py:1094
  43.0 0.8 copy-start.4
  46.1 23.5 %all-to-all-start = ((bf16[16,128,128]{2,1,0:T(8,128)(2,1)}), bf16[16,128,128]{2,1,0:T(8,128)(2,1)S(1)}, u32[]{:S(2)}, u32[]{:S(2)}) async-start(bf16[16,128,128]{2,1,0:T(8,128)(2,1)} %combine.1), calls=%async_computation | async-start | bytes 1048576 | tf_op jit(solution)/shard_map/all_to_all | solution.py:1095
  56.8 18.6 %copy-start.3 = (f32[8,208,192]{2,1,0:T(8,128)S(1)}, f32[8,208,192]{2,1,0:T(8,128)}, u32[]{:S(2)}) copy-start(f32[8,208,192]{2,1,0:T(8,128)} %get-tuple-element.71) | copy-start | bytes 3833860
  69.6 0.8 copy-start
  72.3 10.5 %all-to-all-start.1 = ((f32[32,4,128]{2,1,0:T(4,128)}), f32[32,4,128]{2,1,0:T(4,128)S(1)}, u32[]{:S(2)}, u32[]{:S(2)}) async-start(f32[32,4,128]{2,1,0:T(4,128)} %get-tuple-element.80), calls=%async_computation.1 | async-start | bytes 131072 | tf_op jit(solution)/shard_map/all_to_all | solution.py:1138
  75.7 1.5 %copy-start.2 = (f32[1568,192]{1,0:T(8,128)S(1)}, f32[1568,192]{1,0:T(8,128)}, u32[]{:S(2)}) copy-start(f32[1568,192]{1,0:T(8,128)} %get-tuple-element.137) | copy-start | bytes 3612676
  82.8 0.6 copy-start.5

commit v3 on v2

v3 whole, which is shorter than its diff:
```python
import functools
import math

import jax
import jax.numpy as jnp
from jax import lax
from jax.experimental import pallas as pl
from jax.experimental.pallas import tpu as pltpu
from jax.sharding import PartitionSpec as P

GRID = 14
STEP = 10
EPS_NORM = 1e-06
CLIP_AT = 1.0
BETA_ONE = 0.9
BETA_TWO = 0.95
ADAM_EPS = 1e-08
RATES = (0.1, 0.5, 0.1, 0.05, 0.3, 0.1, 0.3)
DECAYS = (0.05, 0.05, 0.05, 0.05, 0.0, 0.0, 0.0)
LOG2E = 1.4426950408889634
BF = jnp.bfloat16
F32 = jnp.float32
LAYER_VMEM = 55 * 1024 * 1024
SMALL_VMEM = 16 * 1024 * 1024
EARLY_ROWS = 96
LATE_ROWS = 32
CHUNK_ROWS = EARLY_ROWS + LATE_ROWS
PAIR = 2
VM = pl.BlockSpec(memory_space=pltpu.VMEM)
ANYWHERE = pl.BlockSpec(memory_space=pl.ANY)
SM = pl.BlockSpec(memory_space=pltpu.SMEM)
PARAMS = pltpu.CompilerParams(vmem_limit_bytes=SMALL_VMEM)


def sds(*dims, dtype=F32):
    return jax.ShapeDtypeStruct(dims, dtype)


def near(*arrays):
    return [pltpu.with_memory_space_constraint(member, pltpu.VMEM) for member in arrays]


def far(*arrays):
    return [pltpu.with_memory_space_constraint(member, pltpu.HBM) for member in arrays]


def nn(a, b):
    return lax.dot_general(a, b, (((1,), (0,)), ((), ())), preferred_element_type=F32)


def nt(a, b):
    return lax.dot_general(a, b, (((1,), (1,)), ((), ())), preferred_element_type=F32)


def norm_parts(v):
    width = v.shape[-1]
    average = jnp.sum(v, axis=-1, keepdims=True) * (1.0 / width)
    centred = v - average
    variance = jnp.sum(centred * centred, axis=-1, keepdims=True) * (1.0 / width)
    spread = lax.rsqrt(variance + EPS_NORM)
    return centred * spread, spread


def norm_back(e, n, spread):
    width = e.shape[-1]
    mean_e = jnp.sum(e, axis=-1, keepdims=True) * (1.0 / width)
    mean_en = jnp.sum(e * n, axis=-1, keepdims=True) * (1.0 / width)
    return spread * (e - mean_e - n * mean_en)


def fold(v):
    rows = v.shape[0]
    return jnp.sum(v.reshape(rows // 8, 8, v.shape[1]), axis=0)


def gelu_parts(x):
    phi = 0.5 + 0.5 * lax.erf(x * math.sqrt(0.5))
    density = jnp.exp2((x * x) * (-0.5 * LOG2E)) * (1.0 / math.sqrt(2.0 * math.pi))
    return x * phi, phi + x * density


def places(count, lanes, dim):
    at = lax.broadcasted_iota(jnp.int32, (count, lanes), dim).astype(F32)
    row = jnp.floor((at + 0.5) * (1.0 / GRID))
    return at - row * GRID, row


def offsets(kp, qp):
    kc, kr = places(kp, qp, 0)
    qc, qr = places(kp, qp, 1)
    a = kc - qc
    b = kr - qr
    return a, b, a * a + b * b


def head_mask(width, hd, h):
    lane = lax.broadcasted_iota(jnp.int32, (STRIP, width), 1)
    return ((lane >= h * hd) & (lane < (h + 1) * hd)).astype(BF)


def gate_of(hp_ref, h, lanes):
    return 1.0 / (1.0 + jnp.exp(-jnp.broadcast_to(hp_ref[h : h + 1, 3:4], (1, lanes))))


def bf_parts(value, count=3):
    parts = []
    for _ in range(count):
        part = value.astype(BF).astype(F32)
        parts.append(part)
        value = value - part
    return parts


def key_operand(kp):
    kc, kr = places(kp, 128, 0)
    lane = lax.broadcasted_iota(jnp.int32, (kp, 128), 1)
    value = jnp.where(lane < 3, kc, jnp.where(lane < 6, kr, jnp.where(lane < 9, kc * kc, kr * kr)))
    return jnp.where(lane < 12, value, 0.0).astype(BF)


def query_operand(hp_ref, h, qp):
    p = [LOG2E * jnp.broadcast_to(hp_ref[h : h + 1, at : at + 1], (16, qp)) for at in range(3)]
    qc, qr = places(16, qp, 1)
    row = lax.broadcasted_iota(jnp.int32, (16, qp), 0)
    value = jnp.where(row < 3, p[0] - 2.0 * p[2] * qc, jnp.where(row < 6, p[1] - 2.0 * p[2] * qr, p[2]))
    parts = bf_parts(value)
    place = row - 3 * ((row >= 3).astype(jnp.int32) + (row >= 6) + (row >= 9))
    value = jnp.where(place == 0, parts[0], jnp.where(place == 1, parts[1], parts[2]))
    return jnp.where(row < 12, value, jnp.where(row == 12, 1.0, 0.0)).astype(BF)


STRIP = 16
LAG = 3
WAIT = 3


def interleave(*streams):
    streams = [member for member in streams if member is not None]
    while streams:
        alive = []
        for member in streams:
            try:
                next(member)
                alive.append(member)
            except StopIteration:
                pass
        streams = alive


def staged(count, lag, *stages):
    for t in range(count + lag * (len(stages) - 1)):
        for k, stage in enumerate(stages):
            if 0 <= t - k * lag < count:
                stage(t - k * lag)
        yield


def slow(stream, count):
    for _ in range(count):
        yield
        try:
            next(stream)
        except StopIteration:
            return


def cut(value, r):
    return value[r * STRIP : (r + 1) * STRIP]


def rows_of(r):
    return pl.ds(r * STRIP, STRIP)


def put_planes(ref, value):
    width = value.shape[1]
    ref[0] = value[:, :128]
    ref[1, :, 0 : width - 128] = value[:, 128:]


def even_odd_tiles(ref, start, pairs):
    even = [ref[at, pl.ds(start, pairs, stride=2), :] for at in range(2)]
    odd = [ref[at, pl.ds(start + 1, pairs, stride=2), :] for at in range(2)]
    return (
        even[0],
        jnp.concatenate([even[1][:, :64], odd[0][:, :64]], axis=1),
        jnp.concatenate([odd[0][:, 64:], odd[1][:, :64]], axis=1),
    )


def four_row_tiles(ref, plane, start, groups):
    r = [ref[plane, pl.ds(start + at, groups, stride=4), :] for at in range(4)]
    return (
        jnp.concatenate([r[0][:, :96], r[1][:, :32]], axis=1),
        jnp.concatenate([r[1][:, 32:96], r[2][:, :64]], axis=1),
        jnp.concatenate([r[2][:, 64:96], r[3][:, :96]], axis=1),
    )


def pack_kernel(*refs):
    given, pack_ref, passed, held, sems = refs[:9], refs[9], refs[10:13], refs[13:19], refs[19]
    copies = [
        pltpu.make_async_copy(source, target, sems.at[at])
        for at, (source, target) in enumerate(zip(given, [*held, *passed]))
    ]
    for member in copies:
        member.start()
    for member in copies[:6]:
        member.wait()
    tri_ref, out_ref, wid_ref, nar_ref, hb_ref, hp_ref = held
    depth, wide = wid_ref.shape
    pack_ref[0:depth, :] = wid_ref[...].astype(BF)
    pack_ref[depth : 2 * depth, :] = nar_ref[...].astype(BF)
    pack_ref[2 * depth : 3 * depth, :] = jnp.concatenate(
        [tri_ref[0], tri_ref[1], tri_ref[2], out_ref[...].T], axis=1
    ).astype(BF)
    heads_here = hp_ref.shape[0]
    hp = jnp.concatenate([hp_ref[...], jnp.zeros((heads_here, wide - 4), F32)], axis=1)
    left = jnp.concatenate([hb_ref[...].reshape(1, wide), hp], axis=0)
    parts = []
    for _ in range(3):
        part = left.astype(BF).astype(F32)
        parts.append(part)
        left = left - part
    parts.append(jnp.zeros((16 - 3 * (1 + heads_here), wide), F32))
    pack_ref[3 * depth : 3 * depth + 16, :] = jnp.concatenate(parts, axis=0).astype(BF)
    for member in copies[6:]:
        member.wait()


def run_pack(tri, out, wid, nar_t, hb, hp_t, *passed):
    depth, wide = wid.shape
    given = (tri, out, wid, nar_t, hb, hp_t)
    return pl.pallas_call(
        pack_kernel,
        out_shape=(
            pltpu.VMEM((3 * depth + 16, wide), BF),
            *[pltpu.VMEM(member.shape, member.dtype) for member in passed],
        ),
        in_specs=[pl.BlockSpec(memory_space=pltpu.HBM)] * 9,
        out_specs=(VM,) * 4,
        scratch_shapes=[
            *[pltpu.VMEM(member.shape, member.dtype) for member in given],
            pltpu.SemaphoreType.DMA((9,)),
        ],
        compiler_params=PARAMS,
        name="pack_weights",
    )(*far(*given, *passed))


def prepare_kernel(tok_ref, cot_ref, keep_ref, x_ref, inc_ref, bias_ref, xs, cs):
    images, kp, width = x_ref.shape
    patches = keep_ref.shape[1]
    rows = images * patches
    qp = -(-patches // 128) * 128
    mine = keep_ref[pl.ds(pl.multiple_of(lax.axis_index("tensor") * images, 8), images), :].astype(F32)
    columns = jnp.concatenate([mine, jnp.zeros((images, qp - patches), F32)], axis=1).T
    xs[0:rows, :] = tok_ref[...].T.astype(F32)
    cs[0:rows, :] = cot_ref[...].T.astype(F32)
    xs[rows : rows + 16, :] = jnp.zeros((16, width), F32)
    cs[rows : rows + 16, :] = jnp.zeros((16, width), F32)
    for i in range(images):
        span = slice(i * patches, i * patches + kp)
        keep = jnp.broadcast_to(columns[:kp, i : i + 1], (kp, 128))
        keep_wide = jnp.concatenate([keep, keep[:, : width - 128]], axis=1)
        x_ref[i] = xs[span, :].astype(BF)
        inc_ref[i] = (cs[span, :] * keep_wide).astype(BF)
        bias_ref[i] = ((keep - 1.0) * 1e30).astype(BF)


def run_prepare(tok_t, cot_t, keep_mask):
    images = keep_mask.shape[0] // 2
    kp = -(-keep_mask.shape[1] // 16) * 16
    width, rows_here = tok_t.shape
    rows = pltpu.VMEM((images, kp, width), BF)
    return pl.pallas_call(
        prepare_kernel,
        out_shape=(rows, rows, pltpu.VMEM((images, kp, 128), BF)),
        in_specs=[VM] * 3,
        out_specs=(VM,) * 3,
        scratch_shapes=[pltpu.VMEM((rows_here + 16, width), F32)] * 2,
        compiler_params=PARAMS,
        name="prepare",
    )(*near(tok_t, cot_t, keep_mask))


def layer_kernel(*refs, patches, heads, data_count):
    (x_ref, inc_ref, bias_ref, own_ref, oth_ref, vec_ref) = refs[:6]
    (res_ref, gm_ref, dp_ref, head_ref) = refs[6:10]
    outs = refs[10:12] if data_count else refs[10:16]
    at = 10 + len(outs)
    (wq, wk, wv, wo, wi, wn, hb_s, hp_s, key_p, query_p) = refs[at : at + 10]
    at += 10
    (fst_s, keys_s, vt_s, qm_s, dmm_s, v_s, kt_s, soft_s, mid_s, n2_s) = refs[at : at + 10]
    at += 10
    (sec_s, spr_s, low_s, stat_s, back_s) = refs[at : at + 5]
    at += 5
    (first_t, left_t, right_s, res_s, gm_s, dp_s, s_buf, p_buf, att_buf) = refs[at : at + 9]
    at += 9
    (place_g, gate_g, da_buf, att_s, ds_s, wide_g, vec_g, hid_g, sems) = refs[at : at + 9]
    at += 9
    images, kp, width = x_ref.shape
    qp = soft_s.shape[4]
    hd = width // heads
    half = width // 2
    half_heads = heads // 2
    wide = own_ref.shape[1]
    hidden = 2 * wide
    strips = kp // STRIP
    c_scale = LOG2E / math.sqrt(hd)
    back_scale = 1.0 / math.sqrt(hd)
    v = [vec_ref[k : k + 1, :] for k in range(6)]

    key_p[...] = key_operand(kp)
    query_p[...] = jnp.zeros_like(query_p)
    for ref in (hid_g, vec_g, place_g, gate_g, att_buf, mid_s, n2_s, sec_s, spr_s, stat_s):
        ref[...] = jnp.zeros_like(ref)
    s_buf[heads - 2 :] = jnp.zeros((2, kp, qp), F32)
    p_buf[heads - 2 :] = jnp.zeros((2, kp, qp), F32)
    left_t[2, :, 0:qp] = jnp.zeros((width, qp), BF)
    right_s[1, 0:qp, :] = jnp.zeros((qp, hidden), BF)
    vt_s[...] = jnp.zeros((width, qp), BF)
    for k in range(2):
        fst_s[k, kp:, :] = jnp.zeros((qp - kp, width), BF)
    for k in range(images):
        for side in range(2):
            right_s[side, k * qp + kp : (k + 1) * qp, :] = jnp.zeros((qp - kp, hidden), BF)
        for c in range(3):
            dp_s[c, k * qp + kp : (k + 1) * qp, :] = jnp.zeros((qp - kp, width), BF)
    gap = jnp.zeros((qp - kp, width), BF)
    one_lane = (lax.broadcasted_iota(jnp.int32, (STRIP, qp - width), 1) == 0).astype(BF)
    masks = [head_mask(width, hd, h) for h in range(heads)]
    bias_lane = (lax.broadcasted_iota(jnp.int32, (kp, 128), 1) == 12).astype(BF)

    def columns_at(i):
        return pl.ds(pl.multiple_of(i * qp, 128), qp)


    def first_norm(i):
        kept = {}

        def mean(r):
            x = x_ref[i, rows_of(r), :].astype(F32)
            kept[r] = x - jnp.sum(x, axis=-1, keepdims=True) * (1.0 / width)

        def spread(r):
            kept[r] = (kept[r], jnp.sum(kept[r] * kept[r], axis=-1, keepdims=True) * (1.0 / width))

        def put(r):
            centred, variance = kept[r]
            fst_s[i % 2, rows_of(r), :] = (centred * lax.rsqrt(variance + EPS_NORM) * v[0] + v[1]).astype(BF)

        yield from staged(strips, LAG, mean, spread, put)

    def project(i, part):
        first_q = fst_s[i % 2]
        if part == 0:
            queries = nn(first_q, wq[...]).astype(BF)
            yield
            for r in range(qp // STRIP):
                for h in range(heads):
                    qm_s[i, h, rows_of(r), 0:width] = cut(queries, r) * masks[h]
                    qm_s[i, h, rows_of(r), width:] = one_lane
                yield
        elif part == 1:
            keys = nn(first_q, wk[...]).astype(BF)
            yield
            keys_s[:, 0:width] = keys[:kp]
            keys_s[:, width:] = bias_ref[i, :, 0 : qp - width]
            yield
            kt_s[i] = keys.T
            yield
        else:
            values = nn(first_q, wv[...]).astype(BF)
            yield
            v_s[i] = values[:kp]
            vt_s[...] = values.T
            yield
            yield
            first_t[:, columns_at(i)] = first_q.T
            yield


    def scores(i, h):
        s = nt(keys_s[...], qm_s[i, h])
        p = nn(key_p[...] + bias_ref[i] * bias_lane, query_p[h])
        m, pm = cut(s, 0), cut(p, 0)
        for r in range(strips):
            yield
            s_buf[h, rows_of(r), :] = cut(s, r)
            p_buf[h, rows_of(r), :] = cut(p, r)
            m = jnp.maximum(m, cut(s, r))
            pm = jnp.maximum(pm, cut(p, r))
        stat_s[4 * h : 4 * h + 1, :] = jnp.max(m, axis=0, keepdims=True)
        stat_s[4 * h + 1 : 4 * h + 2, :] = jnp.max(pm, axis=0, keepdims=True)

    def exponents(h):
        m, pm = stat_s[4 * h : 4 * h + 1, :], stat_s[4 * h + 1 : 4 * h + 2, :]
        z = jnp.zeros((STRIP, qp), F32)
        pz = jnp.zeros((STRIP, qp), F32)
        for r in range(strips):
            yield
            e = jnp.exp2((s_buf[h, rows_of(r), :] - m) * c_scale)
            pe = jnp.exp2(p_buf[h, rows_of(r), :] - pm)
            s_buf[h, rows_of(r), :] = e
            p_buf[h, rows_of(r), :] = pe
            z = z + e
            pz = pz + pe
        gate = gate_of(hp_s, h, qp)
        stat_s[4 * h + 2 : 4 * h + 3, :] = (1.0 - gate) / jnp.sum(z, axis=0, keepdims=True)
        stat_s[4 * h + 3 : 4 * h + 4, :] = gate / jnp.sum(pz, axis=0, keepdims=True)

    def mixing(i, h):
        a, b = stat_s[4 * h + 2 : 4 * h + 3, :], stat_s[4 * h + 3 : 4 * h + 4, :]
        for r in range(strips):
            yield
            content = s_buf[h, rows_of(r), :] * a
            located = p_buf[h, rows_of(r), :] * b
            soft_s[i, h, 0, rows_of(r), :] = content
            soft_s[i, h, 1, rows_of(r), :] = located
            att_buf[h % 2, rows_of(r), :] = (content + located).astype(BF)
        yield
        left_t[2, h * hd : (h + 1) * hd, columns_at(i)] = nn(
            vt_s[h * hd : (h + 1) * hd, :], att_buf[h % 2]
        ).astype(BF)


    def strip_rows(i, r):
        return pl.ds(pl.multiple_of(i * qp + r * STRIP, 16), STRIP)

    def image_rows(i):
        return pl.ds(pl.multiple_of(i * qp, 16), kp)

    def start(i):
        attn = nt(left_t[2, :, columns_at(i)].T[:kp], wo[...])
        for _ in range(WAIT + 2):
            yield
        kept = {}

        def mean(r):
            middle = x_ref[i, rows_of(r), :].astype(F32) + cut(attn, r) + v[4]
            mid_s[rows_of(r), :] = middle
            kept[r] = middle - jnp.sum(middle, axis=-1, keepdims=True) * (1.0 / width)

        def vary(r):
            kept[r] = (kept[r], jnp.sum(kept[r] * kept[r], axis=-1, keepdims=True) * (1.0 / width))

        def put(r):
            centred, variance = kept[r]
            spread = lax.rsqrt(variance + EPS_NORM)
            n2 = centred * spread
            n2_s[rows_of(r), :] = n2
            spr_s[rows_of(r), :] = spread
            sec_s[rows_of(r), :] = (n2 * v[2] + v[3]).astype(BF)

        yield from staged(strips, LAG, mean, vary, put)
        left_t[0, :, columns_at(i)] = jnp.concatenate([inc_ref[i], gap], axis=0).T
        yield
        left_t[1, :, columns_at(i)] = jnp.concatenate([sec_s[...], gap], axis=0).T

    def chunk(i, c, on):
        lanes = pl.ds(c * 256, 256)
        before = nn(sec_s[...], wi[:, lanes])
        back = nn(inc_ref[i] * on, wn[:, lanes])
        bias_row = hb_s[0:1, lanes]
        total = jnp.zeros((8, 256), F32)
        for r in range(strips):
            yield
            gelu, slope = gelu_parts(cut(before, r) + bias_row)
            right_s[0, strip_rows(i, r), lanes] = gelu.astype(BF)
            grad_before = cut(back, r) * slope
            right_s[1, strip_rows(i, r), lanes] = grad_before.astype(BF)
            total = total + fold(grad_before)
        hid_g[:, lanes] += total

    def end(i, on):
        grad_second = nt(right_s[1, image_rows(i), :], wi[...])
        totals = [jnp.zeros((8, width), F32)] * 4
        mids = []
        for _ in range(WAIT):
            yield
        kept = {}

        def means(r):
            n2 = n2_s[rows_of(r), :]
            g = cut(grad_second, r)
            e = g * v[2]
            mean_e = jnp.sum(e, axis=-1, keepdims=True) * (1.0 / width)
            mean_en = jnp.sum(e * n2, axis=-1, keepdims=True) * (1.0 / width)
            kept[r] = (e, mean_e, mean_en)
            for k, term in enumerate((g * n2, g)):
                totals[k] = totals[k] + fold(term)

        def put(r):
            e, mean_e, mean_en = kept[r]
            n2 = n2_s[rows_of(r), :]
            incoming = (inc_ref[i, rows_of(r), :] * on).astype(F32)
            spread = spr_s[rows_of(r), :]
            grad_middle = incoming + spread * (e - mean_e - n2 * mean_en)
            gm_s[i, rows_of(r), :] = grad_middle
            mids.append(grad_middle.astype(BF))
            for k, term in enumerate((grad_middle, incoming)):
                totals[2 + k] = totals[2 + k] + fold(term)

        yield from staged(strips, LAG, means, put)
        for k in range(4):
            vec_g[k] += totals[k]
        mid_low = jnp.concatenate([*mids, gap], axis=0)
        yield
        dm = nn(mid_low, wo[...]).astype(BF)
        for r in range(qp // STRIP):
            yield
            for h in range(heads):
                dmm_s[i, h, rows_of(r), :] = cut(dm, r) * masks[h]
        yield
        low_s[pl.ds(pl.multiple_of(i * qp, 16), qp), :] = mid_low

    def outcome(i):
        product = nt(right_s[0, image_rows(i), :], wn[...])
        for _ in range(WAIT):
            yield
        for r in range(strips):
            res_s[i, rows_of(r), :] = mid_s[rows_of(r), :] + cut(product, r) + v[5]
            yield

    blocks = hidden // 256

    def forward_step(i, carry):
        one, two = jnp.maximum(i - 1, 0), jnp.maximum(i - 2, 0)
        after = jnp.minimum(i + 1, images - 1)
        on_one, on_two = (i > 0).astype(BF), (i > 1).astype(BF)
        interleave(scores(i, 0), exponents(3), mixing(one, 2), chunk(two, 1, on_two), first_norm(after))
        interleave(scores(i, 1), exponents(0), mixing(one, 3), chunk(two, 2, on_two))
        interleave(
            scores(i, 2),
            exponents(1),
            mixing(i, 0),
            end(two, on_two),
            outcome(two),
            start(one),
            project(i, 2),
        )
        interleave(
            scores(i, 3),
            exponents(2),
            mixing(i, 1),
            chunk(one, 0, on_one),
            project(after, 0),
            project(after, 1),
        )
        return carry

    interleave(first_norm(0))
    wi[:, pl.ds(0, wide)] = own_ref[0:width, :]
    wi[:, pl.ds(wide, wide)] = oth_ref[0:width, :]
    wn[:, pl.ds(0, wide)] = own_ref[width : 2 * width, :]
    wn[:, pl.ds(wide, wide)] = oth_ref[width : 2 * width, :]
    own_tri = own_ref[2 * width : 3 * width, :]
    oth_tri = oth_ref[2 * width : 3 * width, :]
    for k, w in enumerate((wq, wk, wv, wo)):
        lanes = slice(k * half, (k + 1) * half)
        w[...] = jnp.concatenate([own_tri[:, lanes], oth_tri[:, lanes]], axis=1)
    small = []
    for ref in (own_ref, oth_ref):
        tail = ref[3 * width : 3 * width + 16, :].astype(F32)
        each = 1 + half_heads
        small.append(tail[0:each] + tail[each : 2 * each] + tail[2 * each : 3 * each])
    hb_s[0:1, :] = jnp.concatenate([member[0:1] for member in small], axis=1)
    hp_s[...] = jnp.concatenate(
        [member[1:, :128] for member in small] + [jnp.zeros((8 - heads, 128), F32)], axis=0
    )
    for h in range(heads):
        query_p[h, 0:16, :] = query_operand(hp_s, h, qp)
    for part in range(2):
        interleave(project(0, part))
    lax.fori_loop(0, images, forward_step, 0)


    def back_scores(i, h):
        da = nt(v_s[i], dmm_s[i, h])
        rc = jnp.zeros((STRIP, qp), F32)
        rl = jnp.zeros((STRIP, qp), F32)
        for r in range(strips):
            yield
            part = cut(da, r)
            da_buf[h % 2, rows_of(r), :] = part
            rc = rc + soft_s[i, h, 0, rows_of(r), :] * part
            rl = rl + soft_s[i, h, 1, rows_of(r), :] * part
        gate = gate_of(hp_s, h, qp)
        rc = jnp.sum(rc, axis=0, keepdims=True) / (1.0 - gate)
        rl = jnp.sum(rl, axis=0, keepdims=True) / gate
        back_s[2 * h : 2 * h + 1, :] = rc
        back_s[2 * h + 1 : 2 * h + 2, :] = rl
        gate_g[h : h + 1, :] += rl - rc

    def back_spread(i, h):
        rc, rl = back_s[2 * h : 2 * h + 1, :], back_s[2 * h + 1 : 2 * h + 2, :]
        lanes = pl.ds(h * qp, qp)
        for r in range(strips):
            yield
            rows = rows_of(r)
            c = soft_s[i, h, 0, rows, :]
            l = soft_s[i, h, 1, rows, :]
            part = da_buf[h % 2, rows, :]
            ds_s[i % 2, rows, lanes] = (c * (part - rc)).astype(BF)
            att_s[i % 2, rows, lanes] = (c + l).astype(BF)
            place_g[h, rows, :] += l * (part - rl)

    def keys_back(i):
        dk = nn(ds_s[i % 2], qm_s[i].reshape(heads * qp, qp))[:, :width]
        yield
        dp_s[1, image_rows(i), :] = (dk * back_scale).astype(BF)

    def values_back(i):
        dv = nn(att_s[i % 2], dmm_s[i].reshape(heads * qp, width))
        yield
        dp_s[2, image_rows(i), :] = dv.astype(BF)

    def queries_back(i):
        pad = jnp.zeros((qp - kp, qp), BF)
        dq_t = []
        for h in range(heads):
            ds = jnp.concatenate([ds_s[i % 2, :, h * qp : (h + 1) * qp], pad], axis=0)
            dq_t.append(nn(kt_s[i, h * hd : (h + 1) * hd, :], ds))
            yield
        dp_s[0, image_rows(i), :] = (jnp.concatenate(dq_t, axis=0) * back_scale).astype(BF).T[:kp]

    def weight_gradient(unit):
        side = unit // blocks
        lanes = pl.ds(pl.multiple_of((unit % blocks) * 256, 128), 256)
        wide_g[side, :, lanes] = nn(left_t[side], right_s[side, :, lanes])
        yield

    def backward_step(i, carry):
        unit = jnp.minimum(i - 1, 2 * blocks - 1)
        interleave(back_scores(i, 0), back_spread(i - 1, 3), weight_gradient(unit))
        interleave(back_scores(i, 1), back_spread(i, 0), keys_back(i - 1))
        interleave(back_scores(i, 2), back_spread(i, 1), values_back(i - 1))
        interleave(back_scores(i, 3), back_spread(i, 2), queries_back(i - 1))
        return carry

    last = images - 1
    on = jnp.ones((), BF)
    interleave(exponents(3), mixing(last, 2), chunk(last - 1, 1, on), back_scores(0, 0))
    interleave(mixing(last, 3), chunk(last - 1, 2, on), back_scores(0, 1), back_spread(0, 0))
    interleave(end(last - 1, on), outcome(last - 1), start(last), back_scores(0, 2), back_spread(0, 1))
    interleave(chunk(last, 0, on), back_scores(0, 3), back_spread(0, 2))
    interleave(chunk(last, 1, on))
    interleave(chunk(last, 2, on))
    interleave(end(last, on), outcome(last))
    sent = [
        pltpu.make_async_copy(res_s, res_ref, sems.at[0]),
        pltpu.make_async_copy(gm_s, gm_ref, sems.at[1]),
    ]
    for member in sent:
        member.start()

    lax.fori_loop(1, images, backward_step, 0)
    interleave(back_spread(last, 3))
    interleave(keys_back(last), values_back(last), queries_back(last))
    for unit in range(images - 1, 2 * blocks):
        interleave(weight_gradient(unit))
    sent.append(pltpu.make_async_copy(dp_s, dp_ref, sems.at[2]))
    sent[-1].start()

    triple = [nn(first_t[...], dp_s[c]) for c in range(3)]
    parts = offsets(kp, qp)
    rank = lax.axis_index("tensor")
    lane = lax.broadcasted_iota(jnp.int32, (1, 128), 1)
    row = jnp.zeros((1, 128), F32)
    for h in range(heads):
        base = ((rank + h // half_heads) % 2) * (4 * half_heads) + h % half_heads
        g = place_g[h]
        for k in range(3):
            total = jnp.sum(g * parts[k])
            row = row + jnp.where(lane == base + k * half_heads, total, 0.0)
        gate = gate_of(hp_s, h, 128)
        total = jnp.sum(gate_g[h : h + 1, :])
        row = row + jnp.where(lane == base + 3 * half_heads, total * gate * (1.0 - gate), 0.0)
    head_ref[...] = row
    if data_count:
        nar_p, out_p, tri_p, tmp = refs[at : at + 4]
        put_planes(nar_p, wide_g[0].T)
        put_planes(out_p, nn(left_t[2], low_s[...]))
        for c in range(3):
            tri_p[0, c * width : (c + 1) * width, 0:half] = triple[c][:, :half]
            tri_p[1, c * width : (c + 1) * width, 0:half] = triple[c][:, half:]
        early = jnp.sum(vec_g[...], axis=1)
        hidden_sum = jnp.sum(hid_g[...], axis=0, keepdims=True)
        rest = width - 128
        wp, np_, op = width // data_count, wide // data_count // 2, half // data_count // 2
        groups = 3 * width // data_count // 4
        small_at = 3 * (wp + np_ + op)
        for r in range(data_count):
            for side in range(2):
                piece = outs[0].at[r] if side == 0 else tmp.at[r % 4]
                for k in range(3):
                    lanes = slice(side * wide + 128 * k, side * wide + 128 * (k + 1))
                    piece[k * wp : (k + 1) * wp, :] = wide_g[1, r * wp : (r + 1) * wp, lanes]
                    piece[small_at + 8 + k : small_at + 9 + k, :] = hidden_sum[:, lanes]
                base = 3 * wp
                tiles = even_odd_tiles(nar_p, side * wide + 2 * np_ * r, np_)
                for k in range(3):
                    piece[base + k * np_ : base + (k + 1) * np_, :] = tiles[k]
                base += 3 * np_
                tiles = even_odd_tiles(out_p, side * half + 2 * op * r, op)
                for k in range(3):
                    piece[base + k * op : base + (k + 1) * op, :] = tiles[k]
                piece[small_at : small_at + 4, :] = early[:, :128]
                piece[small_at + 4 : small_at + 8, 0:rest] = early[:, 128:]
                piece[small_at + 4 : small_at + 8, rest:] = jnp.zeros((4, 128 - rest), F32)
                piece[small_at + 11 : EARLY_ROWS, :] = jnp.zeros(
                    (EARLY_ROWS - small_at - 11, 128), F32
                )
                tiles = four_row_tiles(tri_p, side, 4 * groups * r, groups)
                for k in range(3):
                    at_row = EARLY_ROWS + k * groups
                    piece[at_row : at_row + groups, :] = tiles[k]
                at_row = EARLY_ROWS + 3 * groups
                piece[at_row:CHUNK_ROWS, :] = jnp.zeros((CHUNK_ROWS - at_row, 128), F32)
                if side:
                    outs[1][r] = piece[...].astype(BF)
    else:
        outs[0][...] = wide_g[0].T
        outs[1][...] = wide_g[1]
        outs[2][...] = nn(left_t[2], low_s[...])
        outs[3][...] = vec_g[...]
        outs[4][...] = hid_g[...]
        for c in range(3):
            outs[5][c * width : (c + 1) * width, :] = triple[c]
    for member in sent:
        member.wait()


def run_layer(x, inc, bias, own, oth, vec, heads, patches, data_count):
    images, kp, width = x.shape
    qp = -(-patches // 128) * 128
    hidden = 2 * own.shape[1]
    full = images * qp
    if data_count:
        outs = [
            pltpu.VMEM((data_count, CHUNK_ROWS, 128), F32),
            pltpu.VMEM((data_count, CHUNK_ROWS, 128), BF),
        ]
    else:
        outs = [
            sds(hidden, width),
            sds(width, hidden),
            sds(width, width),
            sds(4, 8, width),
            sds(8, hidden),
            sds(3 * width, width),
        ]

    def bf(*dims):
        return pltpu.VMEM(dims, BF)

    def f32(*dims):
        return pltpu.VMEM(dims, F32)

    scratch = [
        *[bf(width, width)] * 4,
        bf(width, hidden),
        bf(width, hidden),
        f32(8, hidden),
        f32(8, 128),
        bf(kp, 128),
        bf(heads, 128, qp),
        bf(2, qp, width),
        bf(kp, qp),
        bf(width, qp),
        bf(images, heads, qp, qp),
        bf(images, heads, qp, width),
        bf(images, kp, width),
        bf(images, width, qp),
        f32(images, heads, 2, kp, qp),
        f32(kp, width),
        f32(kp, width),
        bf(kp, width),
        f32(kp, 1),
        bf(full, width),
        f32(4 * heads, qp),
        f32(2 * heads, qp),
        bf(width, full),
        bf(3, width, full),
        bf(2, full, hidden),
        f32(images, kp, width),
        f32(images, kp, width),
        bf(3, full, width),
        f32(heads, kp, qp),
        f32(heads, kp, qp),
        bf(2, qp, qp),
        f32(heads, kp, qp),
        f32(8, qp),
        f32(2, kp, qp),
        bf(2, kp, heads * qp),
        bf(2, kp, heads * qp),
        f32(2, width, hidden),
        f32(4, 8, width),
        f32(8, hidden),
        pltpu.SemaphoreType.DMA((3,)),
    ]
    if data_count:
        scratch += [f32(2, hidden, 128), f32(2, width, 128), f32(2, 3 * width, 128)]
        scratch.append(f32(4, CHUNK_ROWS, 128))
    return pl.pallas_call(
        functools.partial(layer_kernel, patches=patches, heads=heads, data_count=data_count),
        out_shape=(
            sds(images, kp, width),
            sds(images, kp, width),
            sds(3, full, width, dtype=BF),
            sds(1, 128),
            *outs,
        ),
        in_specs=[VM] * 6,
        out_specs=(ANYWHERE,) * 3 + (VM,) * (1 + len(outs)),
        scratch_shapes=scratch,
        compiler_params=pltpu.CompilerParams(vmem_limit_bytes=LAYER_VMEM),
        name="layer",
    )(*near(x, inc, bias, own, oth), vec)


def finish_kernel(
    x_ref, own_ref, oth_ref, vec_ref, res_hbm, gm_hbm, dp_hbm, res_out, gi_out, vec_out,
    res_s, gm_s, dp_s, w, vec_g, rows_s, sems, *, patches,
):
    images, kp, width = x_ref.shape
    qp = dp_s.shape[1] // images
    half = width // 2
    copies = [
        pltpu.make_async_copy(source, target, sems.at[at])
        for at, (source, target) in enumerate(
            ((res_hbm, res_s), (gm_hbm, gm_s), (dp_hbm, dp_s))
        )
    ]
    for member in copies:
        member.start()
    own_tri = own_ref[2 * width : 3 * width, :]
    oth_tri = oth_ref[2 * width : 3 * width, :]
    for at in range(3):
        span = slice(at * half, (at + 1) * half)
        w[at] = jnp.concatenate([own_tri[:, span], oth_tri[:, span]], axis=1)
    vec_g[...] = jnp.zeros_like(vec_g)
    gain = vec_ref[0:1, :]
    copies[0].wait()
    for i in range(images):
        rows_s[i * patches : (i + 1) * patches, :] = res_s[i, 0:patches, :]
    res_out[...] = rows_s[...].T
    copies[1].wait()
    copies[2].wait()
    for i in range(images):
        n1, spread = norm_parts(x_ref[i].astype(F32))
        g = sum(nt(dp_s[c, i * qp : i * qp + kp, :], w[c]) for c in range(3))
        vec_g[0] += fold(g * n1)
        vec_g[1] += fold(g)
        rows = gm_s[i] + norm_back(g * gain, n1, spread)
        rows_s[i * patches : (i + 1) * patches, :] = rows[0:patches]
    gi_out[...] = rows_s[...].T
    vec_out[...] = jnp.sum(vec_g[...], axis=1)


def run_finish(x, own, oth, vec, res, gm, dp, patches):
    images, kp, width = x.shape
    rows = images * patches
    return pl.pallas_call(
        functools.partial(finish_kernel, patches=patches),
        out_shape=(sds(width, rows), sds(width, rows), sds(2, width)),
        in_specs=[VM] * 4 + [ANYWHERE] * 3,
        out_specs=(VM,) * 3,
        scratch_shapes=[
            pltpu.VMEM(res.shape, F32),
            pltpu.VMEM(gm.shape, F32),
            pltpu.VMEM(dp.shape, BF),
            pltpu.VMEM((3, width, width), BF),
            pltpu.VMEM((2, 8, width), F32),
            pltpu.VMEM((rows, width), F32),
            pltpu.SemaphoreType.DMA((3,)),
        ],
        compiler_params=pltpu.CompilerParams(vmem_limit_bytes=32 * 1024 * 1024),
        name="finish",
    )(*near(x, own, oth), vec, *far(res, gm, dp))


def combine_kernel(own_ref, got_ref, out_ref):
    out_ref[...] = (own_ref[...] + got_ref[...].astype(F32)).astype(BF)


def run_combine(own, got):
    return pl.pallas_call(
        combine_kernel,
        out_shape=pltpu.VMEM(own.shape, BF),
        in_specs=[VM] * 2,
        out_specs=VM,
        compiler_params=PARAMS,
        name="combine",
    )(*near(own, got))


def pick_rows(ref, start, count, flip=False):
    total = ref.shape[1] if flip else ref.shape[0]
    row = lax.broadcasted_iota(jnp.int32, (count, total), 0) + start
    col = lax.broadcasted_iota(jnp.int32, (count, total), 1)
    chosen = (row == col).astype(F32)
    return lax.dot_general(
        chosen,
        ref[...],
        (((1,), (1 if flip else 0,)), ((), ())),
        preferred_element_type=F32,
        precision=lax.Precision.HIGHEST,
    )


def share_kernel(_, tri_ref, out_ref, wid_ref, nar_ref, *refs, data_count):
    (wt_f, wo_f, ww_f, wn_f, st, so, sw, sn) = refs
    width, wide = wid_ref.shape
    half = out_ref.shape[0]
    wp, np_, op = width // data_count, wide // data_count // 2, half // data_count // 2
    data_rank = lax.axis_index("dp")
    groups = tri_ref.shape[0] // data_count // 4
    st[0, :, 0 : tri_ref.shape[1]] = pick_rows(tri_ref, data_rank * 4 * groups, 4 * groups)
    put_planes(so, pick_rows(out_ref, data_rank * 2 * op, 2 * op))
    sw[...] = pick_rows(wid_ref, data_rank * wp, wp)
    put_planes(sn, pick_rows(nar_ref, data_rank * 2 * np_, 2 * np_, flip=True))
    tiles = four_row_tiles(st, 0, 0, groups)
    for p in range(groups):
        for k in range(3):
            tile = 128 * (3 * p + k)
            wt_f[0:1, tile : tile + 128] = tiles[k][p : p + 1, :]
    for ref, flat, pairs in ((so, wo_f, op), (sn, wn_f, np_)):
        tiles = even_odd_tiles(ref, 0, pairs)
        for p in range(pairs):
            for k in range(3):
                tile = 128 * (3 * p + k)
                flat[0:1, tile : tile + 128] = tiles[k][p : p + 1, :]
    for p in range(wp):
        ww_f[0:1, wide * p : wide * (p + 1)] = sw[p : p + 1, :]


def run_shares(after, tri, out, wid, nar_t, data_count):
    wide = wid.shape[1]
    share = [member.shape[0] // data_count for member in (tri, out, wid)]
    return pl.pallas_call(
        functools.partial(share_kernel, data_count=data_count),
        out_shape=tuple(sds(1, member.size // data_count) for member in (tri, out, wid, nar_t)),
        in_specs=[VM] * 5,
        out_specs=(VM,) * 4,
        scratch_shapes=[
            pltpu.VMEM((1, share[0], 128), F32),
            pltpu.VMEM((2, share[1], 128), F32),
            pltpu.VMEM((share[2], wide), F32),
            pltpu.VMEM((2, wide // data_count, 128), F32),
        ],
        compiler_params=PARAMS,
        name="weight_shares",
    )(after, tri, out, wid, nar_t)


def spread_rows(flat_ref, from_ref, base, blocks):
    for p in range(blocks):
        for k in range(3):
            at = base + k * blocks + p
            tile = 128 * (3 * p + k)
            flat_ref[0:1, tile : tile + 128] = from_ref[at : at + 1, :]


def sum_kernel(got_ref, late_ref, head_ref, _, *refs, blocks):
    (tri_f, out_f, wid_f, nar_f, vec_ref, hid_ref, pay_ref, tot) = refs
    width = late_ref.shape[1]
    tri_b, out_b, wid_b, nar_b = blocks
    tot[...] = jnp.sum(got_ref[...].astype(F32), axis=0)
    spread_rows(wid_f, tot, 0, wid_b)
    spread_rows(nar_f, tot, 3 * wid_b, nar_b)
    spread_rows(out_f, tot, 3 * (wid_b + nar_b), out_b)
    spread_rows(tri_f, tot, EARLY_ROWS, tri_b)
    at = 3 * (wid_b + nar_b + out_b)
    vec_ref[...] = jnp.concatenate(
        [tot[at : at + 4, :], tot[at + 4 : at + 8, : width - 128]], axis=1
    )
    hid = jnp.concatenate([tot[at + 8 + k : at + 9 + k, :] for k in range(3)], axis=1)
    hid_ref[...] = hid
    early = tot[0:at, :]
    late = tot[EARLY_ROWS : EARLY_ROWS + 3 * tri_b, :]
    squares = jnp.sum(early * early) + jnp.sum(late * late)
    squares = squares + jnp.where(lax.axis_index("dp") == 0, jnp.sum(hid * hid), 0.0)
    lane = lax.broadcasted_iota(jnp.int32, (1, 128), 1)
    tails = jnp.concatenate([late_ref[0:1, 128:], late_ref[1:2, 128:]], axis=1)
    payload = jnp.concatenate(
        [late_ref[:, :128], tails, jnp.where(lane == 127, squares, head_ref[...])], axis=0
    )
    pay_ref[...] = jnp.broadcast_to(payload[None], pay_ref.shape)


def run_sums(got, late_vec, head, after, blocks, wide):
    count = got.shape[0]
    width = late_vec.shape[1]
    return pl.pallas_call(
        functools.partial(sum_kernel, blocks=blocks),
        out_shape=(
            *[sds(1, 3 * 128 * member) for member in blocks],
            sds(4, width),
            sds(1, wide),
            sds(2 * count, 4, 128),
        ),
        in_specs=[VM] * 4,
        out_specs=(VM,) * 7,
        scratch_shapes=[pltpu.VMEM((CHUNK_ROWS, 128), F32)],
        compiler_params=PARAMS,
        name="sums",
    )(got, late_vec, head, after)


def adam_parts(weight, gradient, moment, squares, rate, decay):
    moment_new = BETA_ONE * moment + (1.0 - BETA_ONE) * gradient
    squares_new = BETA_TWO * squares + (1.0 - BETA_TWO) * gradient * gradient
    quotient = (moment_new / (1.0 - BETA_ONE**STEP)) / (
        jnp.sqrt(squares_new / (1.0 - BETA_TWO**STEP)) + ADAM_EPS
    )
    return moment_new, squares_new, weight - rate * (quotient + decay * weight)


def adam_kernel(got_ref, early_ref, hid_ref, hp_ref, vec_ref, hb_ref, *refs):
    grads = refs[0:4]
    weights = refs[4:8]
    states = refs[8:22]
    outs = refs[22:43]
    norm_ref = refs[43]
    width = vec_ref.shape[1]
    half_heads = hp_ref.shape[0]
    tail = width - 128
    total = jnp.sum(got_ref[...], axis=0)
    late = jnp.concatenate(
        [
            total[0:2, :],
            jnp.concatenate([total[2:3, :tail], total[2:3, tail : 2 * tail]], axis=0),
        ],
        axis=1,
    )
    vector = jnp.concatenate([late, early_ref[...]], axis=0)
    lane = lax.broadcasted_iota(jnp.int32, (1, 128), 1)
    heads_row = jnp.where(lane < 8 * half_heads, total[3:4, :], 0.0)
    squares = (
        jnp.sum(jnp.where(lane == 127, total[3:4, :], 0.0))
        + jnp.sum(vector * vector)
        + jnp.sum(heads_row * heads_row)
    )
    norm = jnp.sqrt(jnp.full((1, 128), squares))
    norm_ref[0] = jnp.sum(norm[:, 0:1])
    factor = (CLIP_AT / jnp.maximum(norm, CLIP_AT))[:, 0:1]
    span = 4 * half_heads
    mine = jnp.where(lax.axis_index("tensor") == 0, heads_row[:, :span], heads_row[:, span : 2 * span])
    head = jnp.concatenate(
        [
            jnp.concatenate(
                [mine[:, c * half_heads + h : c * half_heads + h + 1] for c in range(4)], axis=1
            )
            for h in range(half_heads)
        ],
        axis=0,
    )
    given = [ref[...] for ref in grads] + [vector, hid_ref[...], head]
    wide = hid_ref.shape[1]
    held = [ref[...] for ref in weights] + [vec_ref[...], hb_ref[...].reshape(1, wide), hp_ref[...]]
    for at in range(7):
        renewed = adam_parts(
            held[at],
            given[at] * factor,
            states[2 * at][...].reshape(held[at].shape),
            states[2 * at + 1][...].reshape(held[at].shape),
            RATES[at],
            DECAYS[at],
        )
        for step in range(3):
            out = outs[3 * at + step]
            out[...] = renewed[step].reshape(out.shape)


def run_adam(got, early, hid, hp_t, vec, hb, grads, weights, states):
    shapes = []
    for at in range(7):
        shapes += [sds(*states[2 * at].shape)] * 3
    return pl.pallas_call(
        adam_kernel,
        out_shape=(*shapes, sds(1)),
        in_specs=[VM] * (6 + 4 + 4 + 14),
        out_specs=(VM,) * 21 + (SM,),
        compiler_params=PARAMS,
        name="adam",
    )(got, early, hid, hp_t, vec, hb, *grads, *weights, *states)


def plain_chunks(halves, data_count, rows):
    sides = []
    for side in range(2):
        flat = jnp.concatenate([own_first[side].reshape(data_count, -1) for own_first in halves], axis=1)
        flat = jnp.pad(flat, ((0, 0), (0, rows * 128 - flat.shape[1])))
        sides.append(flat.reshape(data_count, rows, 128))
    return sides[0], sides[1].astype(BF)


def on_device(
    tokens,
    cotangent,
    keep_mask,
    triple_weight,
    outward_weight,
    widen_weight,
    narrow_weight,
    vectors,
    hidden_bias,
    head_params,
    triple_moment,
    triple_square,
    outward_moment,
    outward_square,
    widen_moment,
    widen_square,
    narrow_moment,
    narrow_square,
    vector_moment,
    vector_square,
    hidden_moment,
    hidden_square,
    head_moment,
    head_square,
):
    tensor_rank = lax.axis_index("tensor")
    data_rank = lax.axis_index("dp")
    data_count = lax.axis_size("dp")
    images = keep_mask.shape[0] // 2
    patches = keep_mask.shape[1]
    heads = 2 * head_params.shape[1]
    depth = triple_weight.shape[1]
    half = triple_weight.shape[2]
    wide = widen_weight.shape[1]
    triple_rows = triple_weight.reshape(3 * depth, half)
    narrow_t = narrow_weight.T
    head_t = head_params.T
    fast = (
        depth == 192
        and half == 96
        and wide == 384
        and depth % data_count == 0
        and wide % (2 * data_count) == 0
        and half % (2 * data_count) == 0
        and 3 * depth % (4 * data_count) == 0
    )
    chunked = data_count if fast else 0
    swap = [(0, 1), (1, 0)]

    own, *rows_near = run_pack(
        triple_weight,
        outward_weight,
        widen_weight,
        narrow_t,
        hidden_bias,
        head_t,
        tokens.T,
        cotangent.T,
        keep_mask,
    )
    other = lax.ppermute(own, "tensor", swap)
    x, inc, bias = run_prepare(*rows_near)
    result, grad_middle, dp, head_row, *sums = run_layer(
        x, inc, bias, own, other, vectors, heads, patches, chunked
    )
    if fast:
        mine, theirs = sums
    else:
        nar_g, wid_g, out_g, vec_g, hid_g, tri_g = sums
        early_mine = jnp.sum(vec_g, axis=1).reshape(1, -1)
        early_both = jnp.broadcast_to(early_mine, (data_count, early_mine.size))
        hidden_both = jnp.broadcast_to(
            jnp.sum(hid_g, axis=0).reshape(2, 1, wide), (2, data_count, wide)
        )
        early = plain_chunks(
            [
                wid_g.reshape(depth, 2, wide).transpose(1, 0, 2),
                nar_g.reshape(2, -1),
                out_g.reshape(2, -1),
                (early_both, early_both),
                hidden_both,
            ],
            data_count,
            EARLY_ROWS,
        )
        late = plain_chunks(
            [tri_g.reshape(3 * depth, 2, half).transpose(1, 0, 2)], data_count, LATE_ROWS
        )
        mine, theirs = (jnp.concatenate(pair, axis=1) for pair in zip(early, late))
    received = lax.ppermute(theirs, "tensor", swap)
    chunks = run_combine(mine, received)
    got = lax.all_to_all(chunks, "dp", 0, 0, tiled=False)
    result_t, grad_input_t, late_vec = run_finish(
        x, own, other, vectors, result, grad_middle, dp, patches
    )
    if fast:
        wt_f, wo_f, ww_f, wn_f = run_shares(
            head_row, triple_rows, outward_weight, widen_weight, narrow_t, data_count
        )
        blocks = [
            member.size // data_count // 384
            for member in (triple_rows, outward_weight, widen_weight, narrow_t)
        ]
        tri_f, out_f, wid_f, nar_f, early_vec, hid, payload = run_sums(
            got, late_vec, head_row, wo_f, blocks, wide
        )
    else:
        total = jnp.sum(got.astype(F32), axis=0)
        early_sum = total[:EARLY_ROWS].reshape(1, -1)
        masters = (widen_weight, narrow_weight, outward_weight)
        sizes = [member.size // data_count for member in masters] + [4 * depth, wide]
        cuts = [sum(sizes[:at]) for at in range(6)]
        wid_f, nar_f, out_f, early_vec, hid = (
            early_sum[:, cuts[at] : cuts[at + 1]] for at in range(5)
        )
        early_vec = early_vec.reshape(4, depth)
        share = triple_rows.size // data_count
        tri_f = total[EARLY_ROWS:].reshape(1, -1)[:, :share]

        def weight_share(member):
            length = member.size // data_count
            return lax.dynamic_slice_in_dim(member.reshape(1, -1), data_rank * length, length, 1)

        ww_f, wn_f, wo_f = (weight_share(member) for member in masters)
        wt_f = weight_share(triple_rows)
        squares = sum(jnp.sum(member * member) for member in (wid_f, nar_f, out_f, tri_f))
        squares = squares + jnp.where(data_rank == 0, jnp.sum(hid * hid), 0.0)
        lane = lax.broadcasted_iota(jnp.int32, (1, 128), 1)
        payload = jnp.concatenate(
            [
                late_vec[:, :128],
                late_vec[:, 128:].reshape(1, 128),
                jnp.where(lane == 127, squares, head_row),
            ]
        )
        payload = jnp.broadcast_to(payload[None], (2 * data_count, 4, 128))
    last_got = lax.all_to_all(payload, ("dp", "tensor"), 0, 0, tiled=False)
    renewed = run_adam(
        last_got,
        early_vec,
        hid,
        head_t,
        vectors,
        hidden_bias,
        (tri_f, out_f, wid_f, nar_f),
        (wt_f, wo_f, ww_f, wn_f),
        (
            triple_moment,
            triple_square,
            outward_moment,
            outward_square,
            widen_moment,
            widen_square,
            narrow_moment,
            narrow_square,
            vector_moment,
            vector_square,
            hidden_moment,
            hidden_square,
            head_moment.T,
            head_square.T,
        ),
    )
    hidden_new = renewed[15:18]
    head_new = [member.T for member in renewed[18:21]]
    return (result_t.T, grad_input_t.T, *renewed[:15], *hidden_new, *head_new, renewed[21].reshape(()))


def solution(mesh):
    return jax.shard_map(
        on_device,
        mesh=mesh,
        in_specs=(
            P(("dp", "tensor"), None),
            P(("dp", "tensor"), None),
            P("dp", None),
            P(None, None, "tensor"),
            P("tensor", None),
            P(None, "tensor"),
            P("tensor", None),
            P(),
            P("tensor"),
            P(None, "tensor"),
            P("tensor", "dp"),
            P("tensor", "dp"),
            P("tensor", "dp"),
            P("tensor", "dp"),
            P("tensor", "dp"),
            P("tensor", "dp"),
            P("tensor", "dp"),
            P("tensor", "dp"),
            P(),
            P(),
            P("tensor"),
            P("tensor"),
            P(None, "tensor"),
            P(None, "tensor"),
        ),
        out_specs=(
            P(("dp", "tensor"), None),
            P(("dp", "tensor"), None),
            P("tensor", "dp"),
            P("tensor", "dp"),
            P("tensor", "dp"),
            P("tensor", "dp"),
            P("tensor", "dp"),
            P("tensor", "dp"),
            P("tensor", "dp"),
            P("tensor", "dp"),
            P("tensor", "dp"),
            P("tensor", "dp"),
            P("tensor", "dp"),
            P("tensor", "dp"),
            P(),
            P(),
            P(),
            P("tensor"),
            P("tensor"),
            P("tensor"),
            P(None, "tensor"),
            P(None, "tensor"),
            P(None, "tensor"),
            P(),
        ),
        check_vma=False,
    )
```

time: 86 us -> 74.2 us (0.86)
  Pallas kernels: 53.2 us -> 43.1 us
  blocking collectives: 0 us -> 10.1 us
  local copies, waits for them, and re-layouts: 6.37 us -> 0.14 us
  waiting for transfers between devices: 12.8 us -> 10.1 us
  starting transfers between devices: 11.6 us -> 9.2 us
    all_to_all x0 -> x1, blocking collectives: none -> 10.1 us  [on_device(): last_got = lax.all_to_all(payload, ('dp', 'tensor'), 0, 0, tiled=False)]
    pallas_call x5, Pallas kernels: 15.8 us -> 10.7 us  [the longest x1 6.17 us: run_finish(): pl.pallas_call(functools.partial(finish_kernel, patches=patches), out_sha...]
    unnamed x13 -> x44, local copies, waits for them, and re-layouts: 4.55 us -> 0.14 us
    all_to_all x1 -> x0, waiting for transfers between devices: 4.01 us -> none  [on_device(): last_got = lax.all_to_all(payload, ('dp', 'tensor'), 0, 0, tiled=False)]
    all_to_all x1 -> x0, starting transfers between devices: 3.06 us -> none  [on_device(): last_got = lax.all_to_all(payload, ('dp', 'tensor'), 0, 0, tiled=False)]
    pallas_call x1, Pallas kernels: 2.7 us -> 0.89 us  [run_shares(): pl.pallas_call(functools.partial(share_kernel, data_count=data_count), ou...]
    pallas_call x1, Pallas kernels: 1.94 us -> 0.23 us  [run_sums(): pl.pallas_call(functools.partial(sum_kernel, blocks=blocks), out_shape=(*...]
    reshape x2 -> x0, local copies, waits for them, and re-layouts: 1.69 us -> none  [on_device(): result = result[:, :patches].reshape(images * patches, depth)]
  transfers between devices with their start and end apart: 4 -> 3, of which waited for: 3 -> 3; matrix products, arithmetic and copies ran while one was open for 5% -> 0% of each run, Pallas kernels for 14% -> 11%
where the time goes in v3:
time: 74.2 us; the launch traced here: 73.9 us
  Pallas kernels  43.1 us (58%)
  waiting for transfers between devices  10.1 us (14%)
  blocking collectives  10.1 us (14%)
  starting transfers between devices  9.2 us (12%)
  between operations  1.2 us (2%)
    pallas_call x1, Pallas kernels, run_layer(): pl.pallas_call(functools.partial(layer_kernel, patches=patches, heads=hea...  31.3 us
    all_to_all x1, blocking collectives, on_device(): last_got = lax.all_to_all(payload, ('dp', 'tensor'), 0, 0, tiled=False)  10.1 us
    all_to_all x1, starting transfers between devices, on_device(): got = lax.all_to_all(chunks, 'dp', 0, 0, tiled=False)  8.24 us
    all_to_all x1, waiting for transfers between devices, on_device(): got = lax.all_to_all(chunks, 'dp', 0, 0, tiled=False)  8.06 us
    pallas_call x1, Pallas kernels, run_finish(): pl.pallas_call(functools.partial(finish_kernel, patches=patches), out_sha...  6.17 us
    pallas_call x1, Pallas kernels, run_pack(): pl.pallas_call(pack_kernel, out_shape=(pltpu.VMEM((3 * depth + 16, wide),...  1.71 us
    ppermute x1, waiting for transfers between devices, on_device(): received = lax.ppermute(theirs, 'tensor', swap)  1.54 us
  transfers between devices with their start and end apart: 3, of which 3 were waited for; matrix products, arithmetic and copies ran while one was open for 0% of the time, Pallas kernels for 11%

profile of v3, /device:TPU:0, one launch (start us, length us, event | category | flops | bytes accessed | tf_op | source)
XLA Modules:
  0.0 73.9 jit_solution(3438972212710137638)
XLA Ops:
  0.7 1.7 %pack_weights.1 = (bf16[592,384]{1,0:T(8,128)(2,1)S(1)}, bf16[192,1568]{1,0:T(8,128)(2,1)S(1)}, bf16[192,1568]{1,0:T(8,128)(2,1)S(1)}, s32[16,196]{1,0:T(8,128)S(1)}) custom-call(f32[3,192,96]{2,1,0:T(8,128)} %refs_0_.1, f32[96,192]{1,0:T(8,128)} %out_ref.1, f32[192,384]{1,0:T(8,128)} %wid_ref.1, f32[192,384]{1,0:T(8,128)} %bitcast.14, f32[384]{0:T(512)} %hb_ref.1, ...), custom_call_target="tpu_custom_call" | custom-call | tf_op jit(solution)/shard_map/pack_weights/pallas_call | solution.py:234
  2.4 0.5 collective-permute-start
  2.9 0.9 %prepare.1 = (bf16[8,208,192]{2,1,0:T(8,128)(2,1)S(1)}, bf16[8,208,192]{2,1,0:T(8,128)(2,1)S(1)}, bf16[8,208,128]{2,1,0:T(8,128)(2,1)S(1)}) custom-call(bf16[192,1568]{1,0:T(8,128)(2,1)S(1)} %get-tuple-element.73.tok_ref, bf16[192,1568]{1,0:T(8,128)(2,1)S(1)} %get-tuple-element.74.cot_ref, s32[16,196]{1,0:T(8,128)S(1)} %get-tuple-element.75.keep_ref), custom_call_target="tpu_custom_call" | custom-call | tf_op jit(solution)/shard_map/prepare/pallas_call | solution.py:276
  3.8 0.5 collective-permute-done.refs_4_.oth_ref
  4.3 31.3 %layer.1 = (f32[8,208,192]{2,1,0:T(8,128)}, f32[8,208,192]{2,1,0:T(8,128)}, bf16[3,2048,192]{2,1,0:T(8,128)(2,1)}, f32[1,128]{1,0:T(1,128)}, f32[16,128,128]{2,1...) custom-call(bf16[8,208,192]{2,1,0:T(8,128)(2,1)S(1)} %get-tuple-element.76.refs_0_.x_ref, ...), custom_call_target="tpu_custom_call" | custom-call | tf_op jit(solution)/shard_map/layer/pallas_call | solution.py:806
  35.6 0.0 copy-start
  35.6 0.0 copy-start.1
  35.6 0.0 copy-start.2
  35.6 0.0 copy-start.3
  35.6 0.0 copy-start.17
  35.7 0.4 collective-permute-start.1
  36.1 1.5 %collective-permute-done.1.got_ref = bf16[16,128,128]{2,1,0:T(8,128)(2,1)S(1)} collective-permute-done((bf16[16,128,128]{2,1,0:T(8,128)(2,1)S(1)}, bf16[16,128,128]{2,1,0:T(8,128)(2,1)S(1)}, u32[]{:S(2)}, u32[]{:S(2)}) %collective-permute-start.1) | collective-permute-done | bytes 524320 | tf_op jit(solution)/shard_map/ppermute | solution.py:1190
  37.6 0.9 %combine.1 = bf16[16,128,128]{2,1,0:T(8,128)(2,1)} custom-call(f32[16,128,128]{2,1,0:T(8,128)S(1)} %get-tuple-element.85.own_ref, bf16[16,128,128]{2,1,0:T(8,128)(2,1)S(1)} %collective-permute-done.1.got_ref), custom_call_target="tpu_custom_call" | custom-call | tf_op jit(solution)/shard_map/combine/pallas_call | solution.py:889
  38.5 8.2 %all-to-all-start = ((bf16[16,128,128]{2,1,0:T(8,128)(2,1)}), bf16[16,128,128]{2,1,0:T(8,128)(2,1)S(1)}, u32[]{:S(2)}, u32[]{:S(2)}) async-start(bf16[16,128,128]{2,1,0:T(8,128)(2,1)} %combine.1), calls=%async_computation | async-start | bytes 1048576 | tf_op jit(solution)/shard_map/all_to_all | solution.py:1192
  46.8 0.0 copy-done
  46.8 0.0 copy-done.1
  46.8 0.0 copy-done.2
  46.8 0.0 copy-done.3
  46.8 0.0 copy-done.17
  46.8 0.9 %weight_shares.1 = (f32[1,3456]{1,0:T(1,128)S(1)}, f32[1,1152]{1,0:T(1,128)S(1)}, f32[1,4608]{1,0:T(1,128)S(1)}, f32[1,4608]{1,0:T(1,128)S(1)}) custom-call(f32[1,128]{1,0:T(1,128)S(1)} %copy-done.17, f32[576,96]{1,0:T(8,128)S(1)} %bitcast.13, f32[96,192]{1,0:T(8,128)S(1)} %copy-done.3, f32[192,384]{1,0:T(8,128)S(1)} %copy-done.1, f32[192,384]{1,0:T(8,128)S(1)} %bitcast.15), custom_call_target="tpu_custom_call" | custom-call | tf_op jit(solution)/shard_map/weight_shares/pallas_call | solution.py:942
  47.7 0.0 copy-done.4
  47.7 0.0 copy-start.5
  47.8 0.0 copy-start.6
  47.8 0.0 copy-start.7
  47.8 0.0 copy-start.8
  47.8 0.0 copy-start.9
  47.8 0.0 copy-start.10
  47.8 0.0 copy-start.11
  47.8 0.0 copy-start.12
  47.8 0.0 copy-start.13
  47.9 0.0 copy-start.14
  47.9 0.0 copy-start.15
  47.9 0.0 copy-start.16
  47.9 0.0 copy-start.18
  47.9 0.0 copy-start.19
  47.9 0.0 copy-start.20
  47.9 0.0 copy-start.21
  47.9 6.2 %finish.1 = (f32[192,1568]{1,0:T(8,128)}, f32[192,1568]{1,0:T(8,128)}, f32[2,192]{1,0:T(2,128)S(1)}) custom-call(bf16[8,208,192]{2,1,0:T(8,128)(2,1)S(1)} %get-tuple-element.76.refs_0_.x_ref, bf16[592,384]{1,0:T(8,128)(2,1)S(1)} %get-tuple-element.77.refs_3_.own_ref, bf16[592,384]{1,0:T(8,128)(2,1)S(1)} %collective-permute-done.refs_4_.oth_ref, ...), custom_call_target="tpu_custom_call" | custom-call | tf_op jit(solution)/shard_map/finish/pallas_call | solution.py:865
  54.1 8.1 %all-to-all-done.got_ref = bf16[16,128,128]{2,1,0:T(8,128)(2,1)S(1)} async-done(((bf16[16,128,128]{2,1,0:T(8,128)(2,1)}), bf16[16,128,128]{2,1,0:T(8,128)(2,1)S(1)}, u32[]{:S(2)}, u32[]{:S(2)}) %all-to-all-start) | async-done | bytes 524320 | tf_op jit(solution)/shard_map/all_to_all | solution.py:1192
  62.2 0.2 sums.1
  62.4 10.1 %all_to_all.10.got_ref = f32[32,4,128]{2,1,0:T(4,128)S(1)} all-to-all(f32[32,4,128]{2,1,0:T(4,128)S(1)} %get-tuple-element.90), channel_id=1, replica_groups=mesh['dp'=16,'tensor'=2] {'dp','tensor'}, dimensions={0} | all-to-all | bytes 131072 | tf_op jit(solution)/shard_map/all_to_all | solution.py:1237
  72.6 0.0 copy-done.5
  72.6 0.0 copy-done.6
  72.6 0.0 copy-done.7
  72.6 0.0 copy-done.8
  72.6 0.0 copy-done.9
  72.6 0.0 copy-done.10
  72.7 1.1 %adam.1 = (f32[1,3456]{1,0:T(1,128)}, f32[1,3456]{1,0:T(1,128)}, f32[1,3456]{1,0:T(1,128)}, f32[1,1152]{1,0:T(1,128)}, f32[1,1152]{1,0:T(1,128)}, /*index=5*/f32...) custom-call(f32[32,4,128]{2,1,0:T(4,128)S(1)} %all_to_all.10.got_ref, ...), custom_call_target="tpu_custom_call" | custom-call | tf_op jit(solution)/shard_map/adam/pallas_call | solution.py:1081
  (11 shorter events, 0.0 us)
Async XLA Ops:
  2.4 2.0 %collective-permute-start = (bf16[592,384]{1,0:T(8,128)(2,1)S(1)}, bf16[592,384]{1,0:T(8,128)(2,1)S(1)}, u32[]{:S(2)}, u32[]{:S(2)}) collective-permute-start(bf16[592,384]{1,0:T(8,128)(2,1)S(1)} %get-tuple-element.77.refs_3_.own_ref), channel_id=1, source_target_pairs={{0,1},{1,0},{2,3},{3,2},{4,5},{5,4},{6,7},{7,6},{8,9},{9,8},{10,11... | collective-permute-start | bytes 1363976 | tf_op jit(solution)/shard_map/ppermute | solution.py:1161
  35.6 11.2 %copy-start = (f32[3,192,96]{2,1,0:T(8,128)S(1)}, f32[3,192,96]{2,1,0:T(8,128)}, u32[]{:S(2)}) copy-start(f32[3,192,96]{2,1,0:T(8,128)} %refs_0_.1) | copy-start | bytes 663556
  35.6 11.2 %copy-start.1 = (f32[192,384]{1,0:T(8,128)S(1)}, f32[192,384]{1,0:T(8,128)}, u32[]{:S(2)}) copy-start(f32[192,384]{1,0:T(8,128)} %wid_ref.1) | copy-start | bytes 884740
  35.6 11.2 %copy-start.2 = (f32[384,192]{0,1:T(8,128)S(1)}, f32[384,192]{0,1:T(8,128)}, u32[]{:S(2)}) copy-start(f32[384,192]{0,1:T(8,128)} %param.30) | copy-start | bytes 884740
  35.6 11.2 %copy-start.3 = (f32[96,192]{1,0:T(8,128)S(1)}, f32[96,192]{1,0:T(8,128)}, u32[]{:S(2)}) copy-start(f32[96,192]{1,0:T(8,128)} %out_ref.1) | copy-start | bytes 221188
  35.6 11.2 %copy-start.17 = (f32[1,128]{1,0:T(1,128)S(1)}, f32[1,128]{1,0:T(1,128)}, u32[]{:S(2)}) copy-start(f32[1,128]{1,0:T(1,128)} %get-tuple-element.88._.head_ref) | copy-start | bytes 1540
  35.7 2.0 %collective-permute-start.1 = (bf16[16,128,128]{2,1,0:T(8,128)(2,1)S(1)}, bf16[16,128,128]{2,1,0:T(8,128)(2,1)S(1)}, u32[]{:S(2)}, u32[]{:S(2)}) collective-permute-start(bf16[16,128,128]{2,1,0:T(8,128)(2,1)S(1)} %get-tuple-element.86), channel_id=1, source_target_pairs={{0,1},{1,0},{2,3},{3,2},{4,5},{5,4},{6,7},{7,6},{8,9},{9,8},{10,11... | collective-permute-start | bytes 1572872 | tf_op jit(solution)/shard_map/ppermute | solution.py:1190
  37.6 10.1 %copy-start.4 = (f32[6,192]{1,0:T(8,128)S(1)}, f32[6,192]{1,0:T(8,128)}, u32[]{:S(2)}) copy-start(f32[6,192]{1,0:T(8,128)} %vec_ref.3) | copy-start | bytes 13828
  38.5 23.6 %all-to-all-start = ((bf16[16,128,128]{2,1,0:T(8,128)(2,1)}), bf16[16,128,128]{2,1,0:T(8,128)(2,1)S(1)}, u32[]{:S(2)}, u32[]{:S(2)}) async-start(bf16[16,128,128]{2,1,0:T(8,128)(2,1)} %combine.1), calls=%async_computation | async-start | bytes 1048576 | tf_op jit(solution)/shard_map/all_to_all | solution.py:1192
  47.7 24.8 %copy-start.5 = (f32[1,4608]{1,0:T(1,128)S(1)}, f32[1,4608]{1,0:T(1,128)}, u32[]{:S(2)}) copy-start(f32[1,4608]{1,0:T(1,128)} %refs_12_.1) | copy-start | bytes 55300
  47.8 24.8 %copy-start.6 = (f32[1,4608]{1,0:T(1,128)S(1)}, f32[1,4608]{1,0:T(1,128)}, u32[]{:S(2)}) copy-start(f32[1,4608]{1,0:T(1,128)} %refs_13_.1) | copy-start | bytes 55300
  47.8 24.8 %copy-start.7 = (f32[1,4608]{1,0:T(1,128)S(1)}, f32[1,4608]{1,0:T(1,128)}, u32[]{:S(2)}) copy-start(f32[1,4608]{1,0:T(1,128)} %refs_14_.1) | copy-start | bytes 55300
  47.8 24.8 %copy-start.8 = (f32[1,4608]{1,0:T(1,128)S(1)}, f32[1,4608]{1,0:T(1,128)}, u32[]{:S(2)}) copy-start(f32[1,4608]{1,0:T(1,128)} %refs_15_.1) | copy-start | bytes 55300
  47.8 24.8 %copy-start.9 = (f32[1,3456]{1,0:T(1,128)S(1)}, f32[1,3456]{1,0:T(1,128)}, u32[]{:S(2)}) copy-start(f32[1,3456]{1,0:T(1,128)} %refs_8_.3) | copy-start | bytes 41476
  47.8 24.8 %copy-start.10 = (f32[1,3456]{1,0:T(1,128)S(1)}, f32[1,3456]{1,0:T(1,128)}, u32[]{:S(2)}) copy-start(f32[1,3456]{1,0:T(1,128)} %refs_9_.1) | copy-start | bytes 41476
  47.8 24.8 %copy-start.11 = (f32[384]{0:T(512)S(1)}, f32[384]{0:T(512)}, u32[]{:S(2)}) copy-start(f32[384]{0:T(512)} %hb_ref.1) | copy-start | bytes 4612
  47.8 24.8 %copy-start.12 = (f32[6,192]{1,0:T(8,128)S(1)}, f32[6,192]{1,0:T(8,128)}, u32[]{:S(2)}) copy-start(f32[6,192]{1,0:T(8,128)} %refs_16_.1) | copy-start | bytes 13828
  47.8 24.8 %copy-start.13 = (f32[6,192]{1,0:T(8,128)S(1)}, f32[6,192]{1,0:T(8,128)}, u32[]{:S(2)}) copy-start(f32[6,192]{1,0:T(8,128)} %refs_17_.1) | copy-start | bytes 13828
  47.9 24.8 %copy-start.14 = (f32[1,1152]{1,0:T(1,128)S(1)}, f32[1,1152]{1,0:T(1,128)}, u32[]{:S(2)}) copy-start(f32[1,1152]{1,0:T(1,128)} %refs_10_.1) | copy-start | bytes 13828
  47.9 24.8 %copy-start.15 = (f32[1,1152]{1,0:T(1,128)S(1)}, f32[1,1152]{1,0:T(1,128)}, u32[]{:S(2)}) copy-start(f32[1,1152]{1,0:T(1,128)} %refs_11_.1) | copy-start | bytes 13828
  47.9 24.8 %copy-start.16 = (f32[4,2]{0,1:T(2,128)S(1)}, f32[4,2]{0,1:T(2,128)}, u32[]{:S(2)}) copy-start(f32[4,2]{0,1:T(2,128)} %param.33) | copy-start | bytes 100
  47.9 24.8 %copy-start.18 = (f32[384]{0:T(512)S(1)}, f32[384]{0:T(512)}, u32[]{:S(2)}) copy-start(f32[384]{0:T(512)} %refs_18_.1) | copy-start | bytes 4612
  47.9 24.8 %copy-start.19 = (f32[384]{0:T(512)S(1)}, f32[384]{0:T(512)}, u32[]{:S(2)}) copy-start(f32[384]{0:T(512)} %refs_19_.1) | copy-start | bytes 4612
  47.9 24.8 %copy-start.20 = (f32[4,2]{0,1:T(2,128)S(1)}, f32[4,2]{0,1:T(2,128)}, u32[]{:S(2)}) copy-start(f32[4,2]{0,1:T(2,128)} %param.46) | copy-start | bytes 100
  47.9 24.8 %copy-start.21 = (f32[4,2]{0,1:T(2,128)S(1)}, f32[4,2]{0,1:T(2,128)}, u32[]{:S(2)}) copy-start(f32[4,2]{0,1:T(2,128)} %param.47) | copy-start | bytes 100

commit v4 on v3

--- a/solution.py
+++ b/solution.py
@@ -20,7 +20,7 @@
 LOG2E = 1.4426950408889634
 BF = jnp.bfloat16
 F32 = jnp.float32
-LAYER_VMEM = 55 * 1024 * 1024
+LAYER_VMEM = 52 * 1024 * 1024
 SMALL_VMEM = 16 * 1024 * 1024
 EARLY_ROWS = 96
 LATE_ROWS = 32
@@ -93,9 +93,14 @@
     return a, b, a * a + b * b
 
 
-def head_mask(width, hd, h):
-    lane = lax.broadcasted_iota(jnp.int32, (STRIP, width), 1)
+def head_mask(hd, h):
+    lane = lax.broadcasted_iota(jnp.int32, (STRIP, 128), 1)
     return ((lane >= h * hd) & (lane < (h + 1) * hd)).astype(BF)
+
+
+def in_tiles(own, oth):
+    gap = jnp.zeros((own.shape[0], 128 - own.shape[1]), own.dtype)
+    return jnp.concatenate([own, gap, oth, gap], axis=1)
 
 
 def gate_of(hp_ref, h, lanes):
@@ -286,19 +291,22 @@
 
 def layer_kernel(*refs, patches, heads, data_count):
     (x_ref, inc_ref, bias_ref, own_ref, oth_ref, vec_ref) = refs[:6]
-    (res_ref, gm_ref, dp_ref, head_ref) = refs[6:10]
-    outs = refs[10:12] if data_count else refs[10:16]
-    at = 10 + len(outs)
-    (wq, wk, wv, wo, wi, wn, hb_s, hp_s, key_p, query_p) = refs[at : at + 10]
-    at += 10
+    far_refs = refs[6:11]
+    gate_ref, hp_ref = refs[11:13]
+    outs = refs[13:15] if data_count else refs[13:19]
+    at = 13 + len(outs)
+    (wq, wk, wv, wo, wop, wi, wn, hb_s, hp_s, key_p, key_i, query_p) = refs[at : at + 12]
+    at += 12
     (fst_s, keys_s, vt_s, qm_s, dmm_s, v_s, kt_s, soft_s, mid_s, n2_s) = refs[at : at + 10]
     at += 10
     (sec_s, spr_s, low_s, stat_s, back_s) = refs[at : at + 5]
     at += 5
-    (first_t, left_t, right_s, res_s, gm_s, dp_s, s_buf, p_buf, att_buf) = refs[at : at + 9]
+    (first_t, mix_t, left_t, right_s, gm_s, dp_s, s_buf, p_buf, att_buf) = refs[at : at + 9]
     at += 9
-    (place_g, gate_g, da_buf, att_s, ds_s, wide_g, vec_g, hid_g, sems) = refs[at : at + 9]
-    at += 9
+    (place_g, gate_g, da_buf, att_s, ds_s, wide_g, out_g, vec_g, hid_g, tri_p, sems) = refs[at : at + 11]
+    at += 11
+    if data_count:
+        nar_p, out_p, tmp = refs[at : at + 3]
     images, kp, width = x_ref.shape
     qp = soft_s.shape[4]
     hd = width // heads
@@ -313,23 +321,21 @@
 
     key_p[...] = key_operand(kp)
     query_p[...] = jnp.zeros_like(query_p)
-    for ref in (hid_g, vec_g, place_g, gate_g, att_buf, mid_s, n2_s, sec_s, spr_s, stat_s):
+    for ref in (hid_g, vec_g, place_g, gate_g):
         ref[...] = jnp.zeros_like(ref)
-    s_buf[heads - 2 :] = jnp.zeros((2, kp, qp), F32)
-    p_buf[heads - 2 :] = jnp.zeros((2, kp, qp), F32)
-    left_t[2, :, 0:qp] = jnp.zeros((width, qp), BF)
-    right_s[1, 0:qp, :] = jnp.zeros((qp, hidden), BF)
-    vt_s[...] = jnp.zeros((width, qp), BF)
+    for k in range(2):
+        att_buf[k, kp:, :] = jnp.zeros((qp - kp, qp), BF)
     for k in range(2):
         fst_s[k, kp:, :] = jnp.zeros((qp - kp, width), BF)
     for k in range(images):
         for side in range(2):
             right_s[side, k * qp + kp : (k + 1) * qp, :] = jnp.zeros((qp - kp, hidden), BF)
         for c in range(3):
-            dp_s[c, k * qp + kp : (k + 1) * qp, :] = jnp.zeros((qp - kp, width), BF)
+            dp_s[c, k * qp + kp : (k + 1) * qp, :] = jnp.zeros((qp - kp, 256), BF)
     gap = jnp.zeros((qp - kp, width), BF)
-    one_lane = (lax.broadcasted_iota(jnp.int32, (STRIP, qp - width), 1) == 0).astype(BF)
-    masks = [head_mask(width, hd, h) for h in range(heads)]
+    one_lane = (lax.broadcasted_iota(jnp.int32, (STRIP, 128), 1) == half).astype(BF)
+    masks = [head_mask(hd, h) for h in range(half_heads)]
+    tiles = [slice(128 * t, 128 * (t + 1)) for t in range(2)]
     bias_lane = (lax.broadcasted_iota(jnp.int32, (kp, 128), 1) == 12).astype(BF)
 
     def columns_at(i):
@@ -359,15 +365,18 @@
             yield
             for r in range(qp // STRIP):
                 for h in range(heads):
-                    qm_s[i, h, rows_of(r), 0:width] = cut(queries, r) * masks[h]
-                    qm_s[i, h, rows_of(r), width:] = one_lane
+                    tile = cut(queries[:, tiles[h // half_heads]], r)
+                    qm_s[i, h, rows_of(r), :] = tile * masks[h % half_heads] + one_lane
                 yield
         elif part == 1:
             keys = nn(first_q, wk[...]).astype(BF)
             yield
-            keys_s[:, 0:width] = keys[:kp]
-            keys_s[:, width:] = bias_ref[i, :, 0 : qp - width]
-            yield
+            for r in range(strips):
+                bias = bias_ref[i, rows_of(r), :]
+                key_i[rows_of(r), :] = key_p[rows_of(r), :] + bias * cut(bias_lane, r)
+                for t in range(2):
+                    keys_s[rows_of(r), tiles[t]] = cut(keys[:, tiles[t]], r) + bias * one_lane
+                yield
             kt_s[i] = keys.T
             yield
         else:
@@ -380,10 +389,14 @@
             first_t[:, columns_at(i)] = first_q.T
             yield
 
+    def head_rows(h):
+        first_row = 128 * (h // half_heads) + hd * (h % half_heads)
+        return slice(first_row, first_row + hd)
+
 
     def scores(i, h):
-        s = nt(keys_s[...], qm_s[i, h])
-        p = nn(key_p[...] + bias_ref[i] * bias_lane, query_p[h])
+        s = nt(keys_s[:, tiles[h // half_heads]], qm_s[i, h])
+        p = nn(key_i[...], query_p[h])
         m, pm = cut(s, 0), cut(p, 0)
         for r in range(strips):
             yield
@@ -420,8 +433,8 @@
             soft_s[i, h, 1, rows_of(r), :] = located
             att_buf[h % 2, rows_of(r), :] = (content + located).astype(BF)
         yield
-        left_t[2, h * hd : (h + 1) * hd, columns_at(i)] = nn(
-            vt_s[h * hd : (h + 1) * hd, :], att_buf[h % 2]
+        mix_t[h * hd : (h + 1) * hd, columns_at(i)] = nn(
+            vt_s[head_rows(h), :], att_buf[h % 2]
         ).astype(BF)
 
 
@@ -432,14 +445,14 @@
         return pl.ds(pl.multiple_of(i * qp, 16), kp)
 
     def start(i):
-        attn = nt(left_t[2, :, columns_at(i)].T[:kp], wo[...])
+        attn = nt(mix_t[:, columns_at(i)].T[:kp], wo[...])
         for _ in range(WAIT + 2):
             yield
         kept = {}
 
         def mean(r):
             middle = x_ref[i, rows_of(r), :].astype(F32) + cut(attn, r) + v[4]
-            mid_s[rows_of(r), :] = middle
+            mid_s[i, rows_of(r), :] = middle
             kept[r] = middle - jnp.sum(middle, axis=-1, keepdims=True) * (1.0 / width)
 
         def vary(r):
@@ -461,7 +474,7 @@
     def chunk(i, c, on):
         lanes = pl.ds(c * 256, 256)
         before = nn(sec_s[...], wi[:, lanes])
-        back = nn(inc_ref[i] * on, wn[:, lanes])
+        back = nn(inc_ref[i], wn[:, lanes])
         bias_row = hb_s[0:1, lanes]
         total = jnp.zeros((8, 256), F32)
         for r in range(strips):
@@ -471,7 +484,7 @@
             grad_before = cut(back, r) * slope
             right_s[1, strip_rows(i, r), lanes] = grad_before.astype(BF)
             total = total + fold(grad_before)
-        hid_g[:, lanes] += total
+        hid_g[:, lanes] += jnp.where(on, total, 0.0)
 
     def end(i, on):
         grad_second = nt(right_s[1, image_rows(i), :], wi[...])
@@ -494,7 +507,7 @@
         def put(r):
             e, mean_e, mean_en = kept[r]
             n2 = n2_s[rows_of(r), :]
-            incoming = (inc_ref[i, rows_of(r), :] * on).astype(F32)
+            incoming = inc_ref[i, rows_of(r), :].astype(F32)
             spread = spr_s[rows_of(r), :]
             grad_middle = incoming + spread * (e - mean_e - n2 * mean_en)
             gm_s[i, rows_of(r), :] = grad_middle
@@ -504,31 +517,24 @@
 
         yield from staged(strips, LAG, means, put)
         for k in range(4):
-            vec_g[k] += totals[k]
+            vec_g[k] += jnp.where(on, totals[k], 0.0)
         mid_low = jnp.concatenate([*mids, gap], axis=0)
         yield
-        dm = nn(mid_low, wo[...]).astype(BF)
+        dm = nn(mid_low, wop[...]).astype(BF)
         for r in range(qp // STRIP):
             yield
             for h in range(heads):
-                dmm_s[i, h, rows_of(r), :] = cut(dm, r) * masks[h]
+                tile = cut(dm[:, tiles[h // half_heads]], r)
+                dmm_s[i, h, rows_of(r), :] = tile * masks[h % half_heads]
         yield
         low_s[pl.ds(pl.multiple_of(i * qp, 16), qp), :] = mid_low
-
-    def outcome(i):
-        product = nt(right_s[0, image_rows(i), :], wn[...])
-        for _ in range(WAIT):
-            yield
-        for r in range(strips):
-            res_s[i, rows_of(r), :] = mid_s[rows_of(r), :] + cut(product, r) + v[5]
-            yield
 
     blocks = hidden // 256
 
     def forward_step(i, carry):
         one, two = jnp.maximum(i - 1, 0), jnp.maximum(i - 2, 0)
         after = jnp.minimum(i + 1, images - 1)
-        on_one, on_two = (i > 0).astype(BF), (i > 1).astype(BF)
+        on_one, on_two = i > 0, i > 1
         interleave(scores(i, 0), exponents(3), mixing(one, 2), chunk(two, 1, on_two), first_norm(after))
         interleave(scores(i, 1), exponents(0), mixing(one, 3), chunk(two, 2, on_two))
         interleave(
@@ -536,7 +542,6 @@
             exponents(1),
             mixing(i, 0),
             end(two, on_two),
-            outcome(two),
             start(one),
             project(i, 2),
         )
@@ -557,9 +562,10 @@
     wn[:, pl.ds(wide, wide)] = oth_ref[width : 2 * width, :]
     own_tri = own_ref[2 * width : 3 * width, :]
     oth_tri = oth_ref[2 * width : 3 * width, :]
-    for k, w in enumerate((wq, wk, wv, wo)):
+    for k, w in enumerate((wq, wk, wv, wop)):
         lanes = slice(k * half, (k + 1) * half)
-        w[...] = jnp.concatenate([own_tri[:, lanes], oth_tri[:, lanes]], axis=1)
+        w[...] = in_tiles(own_tri[:, lanes], oth_tri[:, lanes])
+    wo[...] = jnp.concatenate([own_tri[:, 3 * half :], oth_tri[:, 3 * half :]], axis=1)
     small = []
     for ref in (own_ref, oth_ref):
         tail = ref[3 * width : 3 * width + 16, :].astype(F32)
@@ -573,11 +579,14 @@
         query_p[h, 0:16, :] = query_operand(hp_s, h, qp)
     for part in range(2):
         interleave(project(0, part))
-    lax.fori_loop(0, images, forward_step, 0)
+    def forward_pair(j, carry):
+        return forward_step(2 * j + 1, forward_step(2 * j, carry))
+
+    lax.fori_loop(0, images // 2, forward_pair, 0)
 
 
     def back_scores(i, h):
-        da = nt(v_s[i], dmm_s[i, h])
+        da = nt(v_s[i, :, tiles[h // half_heads]], dmm_s[i, h])
         rc = jnp.zeros((STRIP, qp), F32)
         rl = jnp.zeros((STRIP, qp), F32)
         for r in range(strips):
@@ -602,132 +611,193 @@
             c = soft_s[i, h, 0, rows, :]
             l = soft_s[i, h, 1, rows, :]
             part = da_buf[h % 2, rows, :]
-            ds_s[i % 2, rows, lanes] = (c * (part - rc)).astype(BF)
-            att_s[i % 2, rows, lanes] = (c + l).astype(BF)
+            ds_s[rows, lanes] = (c * (part - rc)).astype(BF)
+            att_s[rows, lanes] = (c + l).astype(BF)
             place_g[h, rows, :] += l * (part - rl)
 
-    def keys_back(i):
-        dk = nn(ds_s[i % 2], qm_s[i].reshape(heads * qp, qp))[:, :width]
+    def products(i, t):
+        lanes = slice(t * half_heads * qp, (t + 1) * half_heads * qp)
+        heads_in = slice(t * half_heads, (t + 1) * half_heads)
+        dk = nn(ds_s[:, lanes], qm_s[i, heads_in].reshape(half_heads * qp, 128))
+        dv = nn(att_s[:, lanes], dmm_s[i, heads_in].reshape(half_heads * qp, 128))
         yield
-        dp_s[1, image_rows(i), :] = (dk * back_scale).astype(BF)
-
-    def values_back(i):
-        dv = nn(att_s[i % 2], dmm_s[i].reshape(heads * qp, width))
-        yield
-        dp_s[2, image_rows(i), :] = dv.astype(BF)
-
-    def queries_back(i):
         pad = jnp.zeros((qp - kp, qp), BF)
         dq_t = []
-        for h in range(heads):
-            ds = jnp.concatenate([ds_s[i % 2, :, h * qp : (h + 1) * qp], pad], axis=0)
-            dq_t.append(nn(kt_s[i, h * hd : (h + 1) * hd, :], ds))
-            yield
-        dp_s[0, image_rows(i), :] = (jnp.concatenate(dq_t, axis=0) * back_scale).astype(BF).T[:kp]
-
-    def weight_gradient(unit):
+        for h in range(t * half_heads, (t + 1) * half_heads):
+            ds = jnp.concatenate([ds_s[:, h * qp : (h + 1) * qp], pad], axis=0)
+            dq_t.append(nn(kt_s[i, head_rows(h), :], ds))
+        yield
+        dp_s[1, image_rows(i), tiles[t]] = (dk * back_scale).astype(BF)
+        yield
+        dp_s[2, image_rows(i), tiles[t]] = dv.astype(BF)
+        yield
+        dq_t.append(jnp.zeros((128 - half, qp), F32))
+        dq = (jnp.concatenate(dq_t, axis=0) * back_scale).astype(BF)
+        dp_s[0, image_rows(i), tiles[t]] = dq.T[:kp]
+
+    cut_at = (images - 2) * qp
+    spans = (slice(0, cut_at), slice(cut_at, images * qp))
+
+    def weight_gradient(unit, part):
         side = unit // blocks
-        lanes = pl.ds(pl.multiple_of((unit % blocks) * 256, 128), 256)
-        wide_g[side, :, lanes] = nn(left_t[side], right_s[side, :, lanes])
+        lanes = slice((unit % blocks) * 256, (unit % blocks) * 256 + 256)
+        value = nn(left_t[side, :, spans[part]], right_s[side, spans[part], lanes])
         yield
-
-    def backward_step(i, carry):
-        unit = jnp.minimum(i - 1, 2 * blocks - 1)
-        interleave(back_scores(i, 0), back_spread(i - 1, 3), weight_gradient(unit))
-        interleave(back_scores(i, 1), back_spread(i, 0), keys_back(i - 1))
-        interleave(back_scores(i, 2), back_spread(i, 1), values_back(i - 1))
-        interleave(back_scores(i, 3), back_spread(i, 2), queries_back(i - 1))
-        return carry
+        if part:
+            wide_g[side, :, lanes] += value
+        else:
+            wide_g[side, :, lanes] = value
+
+    def outward_gradient(part):
+        value = nn(mix_t[:, spans[part]], low_s[spans[part], :])
+        yield
+        if part:
+            out_g[...] += value
+        else:
+            out_g[...] = value
+
+    def triple_gradient(c, part):
+        value = nn(first_t[:, spans[part]], dp_s[c, spans[part], :])
+        yield
+        rows = pl.ds(c * width, width)
+        for t in range(2):
+            if part:
+                tri_p[t, rows, :] += value[:, tiles[t]]
+            else:
+                tri_p[t, rows, :] = value[:, tiles[t]]
 
     last = images - 1
-    on = jnp.ones((), BF)
-    interleave(exponents(3), mixing(last, 2), chunk(last - 1, 1, on), back_scores(0, 0))
-    interleave(mixing(last, 3), chunk(last - 1, 2, on), back_scores(0, 1), back_spread(0, 0))
-    interleave(end(last - 1, on), outcome(last - 1), start(last), back_scores(0, 2), back_spread(0, 1))
-    interleave(chunk(last, 0, on), back_scores(0, 3), back_spread(0, 2))
-    interleave(chunk(last, 1, on))
-    interleave(chunk(last, 2, on))
-    interleave(end(last, on), outcome(last))
-    sent = [
-        pltpu.make_async_copy(res_s, res_ref, sems.at[0]),
-        pltpu.make_async_copy(gm_s, gm_ref, sems.at[1]),
-    ]
-    for member in sent:
-        member.start()
-
-    lax.fori_loop(1, images, backward_step, 0)
-    interleave(back_spread(last, 3))
-    interleave(keys_back(last), values_back(last), queries_back(last))
-    for unit in range(images - 1, 2 * blocks):
-        interleave(weight_gradient(unit))
-    sent.append(pltpu.make_async_copy(dp_s, dp_ref, sems.at[2]))
-    sent[-1].start()
-
-    triple = [nn(first_t[...], dp_s[c]) for c in range(3)]
-    parts = offsets(kp, qp)
-    rank = lax.axis_index("tensor")
-    lane = lax.broadcasted_iota(jnp.int32, (1, 128), 1)
-    row = jnp.zeros((1, 128), F32)
-    for h in range(heads):
-        base = ((rank + h // half_heads) % 2) * (4 * half_heads) + h % half_heads
-        g = place_g[h]
-        for k in range(3):
-            total = jnp.sum(g * parts[k])
-            row = row + jnp.where(lane == base + k * half_heads, total, 0.0)
-        gate = gate_of(hp_s, h, 128)
-        total = jnp.sum(gate_g[h : h + 1, :])
-        row = row + jnp.where(lane == base + 3 * half_heads, total * gate * (1.0 - gate), 0.0)
-    head_ref[...] = row
-    if data_count:
-        nar_p, out_p, tri_p, tmp = refs[at : at + 4]
+    on = True
+    partial = [weight_gradient(unit, 0) for unit in range(2 * blocks)] + [outward_gradient(0)]
+    interleave(
+        exponents(3), mixing(last, 2), chunk(last - 1, 1, on), back_scores(0, 0), partial[0]
+    )
+    interleave(
+        mixing(last, 3),
+        chunk(last - 1, 2, on),
+        back_scores(0, 1),
+        back_spread(0, 0),
+        partial[1],
+    )
+    interleave(
+        end(last - 1, on), start(last), back_scores(0, 2), back_spread(0, 1), partial[2]
+    )
+    interleave(chunk(last, 0, on), back_scores(0, 3), back_spread(0, 2), partial[3])
+    interleave(chunk(last, 1, on), back_spread(0, 3), partial[4])
+    interleave(chunk(last, 2, on), products(0, 0), partial[5])
+    interleave(end(last, on), products(0, 1), *partial[6:])
+
+    def send(slots, *sources):
+        copies = [
+            pltpu.make_async_copy(source, far_refs[k], sems.at[k])
+            for k, source in zip(slots, sources)
+        ]
+        for member in copies:
+            member.start()
+        return copies
+
+    sent = send((0, 1, 2), right_s.at[0], mid_s, gm_s)
+
+
+    def piece_of(r, side):
+        return outs[0].at[r] if side == 0 else tmp.at[r % 4]
+
+    def early_chunks():
         put_planes(nar_p, wide_g[0].T)
-        put_planes(out_p, nn(left_t[2], low_s[...]))
-        for c in range(3):
-            tri_p[0, c * width : (c + 1) * width, 0:half] = triple[c][:, :half]
-            tri_p[1, c * width : (c + 1) * width, 0:half] = triple[c][:, half:]
+        yield
+        put_planes(out_p, out_g[...])
         early = jnp.sum(vec_g[...], axis=1)
         hidden_sum = jnp.sum(hid_g[...], axis=0, keepdims=True)
         rest = width - 128
         wp, np_, op = width // data_count, wide // data_count // 2, half // data_count // 2
-        groups = 3 * width // data_count // 4
         small_at = 3 * (wp + np_ + op)
         for r in range(data_count):
             for side in range(2):
-                piece = outs[0].at[r] if side == 0 else tmp.at[r % 4]
+                yield
+                piece = piece_of(r, side)
                 for k in range(3):
                     lanes = slice(side * wide + 128 * k, side * wide + 128 * (k + 1))
                     piece[k * wp : (k + 1) * wp, :] = wide_g[1, r * wp : (r + 1) * wp, lanes]
                     piece[small_at + 8 + k : small_at + 9 + k, :] = hidden_sum[:, lanes]
                 base = 3 * wp
-                tiles = even_odd_tiles(nar_p, side * wide + 2 * np_ * r, np_)
+                parts = even_odd_tiles(nar_p, side * wide + 2 * np_ * r, np_)
                 for k in range(3):
-                    piece[base + k * np_ : base + (k + 1) * np_, :] = tiles[k]
+                    piece[base + k * np_ : base + (k + 1) * np_, :] = parts[k]
                 base += 3 * np_
-                tiles = even_odd_tiles(out_p, side * half + 2 * op * r, op)
+                parts = even_odd_tiles(out_p, side * half + 2 * op * r, op)
                 for k in range(3):
-                    piece[base + k * op : base + (k + 1) * op, :] = tiles[k]
+                    piece[base + k * op : base + (k + 1) * op, :] = parts[k]
                 piece[small_at : small_at + 4, :] = early[:, :128]
                 piece[small_at + 4 : small_at + 8, 0:rest] = early[:, 128:]
                 piece[small_at + 4 : small_at + 8, rest:] = jnp.zeros((4, 128 - rest), F32)
                 piece[small_at + 11 : EARLY_ROWS, :] = jnp.zeros(
                     (EARLY_ROWS - small_at - 11, 128), F32
                 )
-                tiles = four_row_tiles(tri_p, side, 4 * groups * r, groups)
+                if side:
+                    outs[1][r, 0:EARLY_ROWS, :] = piece[0:EARLY_ROWS, :].astype(BF)
+
+    def late_chunks():
+        groups = 3 * width // data_count // 4
+        for r in range(data_count):
+            for side in range(2):
+                yield
+                piece = piece_of(r, side)
+                parts = four_row_tiles(tri_p, side, 4 * groups * r, groups)
                 for k in range(3):
-                    at_row = EARLY_ROWS + k * groups
-                    piece[at_row : at_row + groups, :] = tiles[k]
-                at_row = EARLY_ROWS + 3 * groups
-                piece[at_row:CHUNK_ROWS, :] = jnp.zeros((CHUNK_ROWS - at_row, 128), F32)
+                    row = EARLY_ROWS + k * groups
+                    piece[row : row + groups, :] = parts[k]
+                row = EARLY_ROWS + 3 * groups
+                piece[row:CHUNK_ROWS, :] = jnp.zeros((CHUNK_ROWS - row, 128), F32)
                 if side:
-                    outs[1][r] = piece[...].astype(BF)
+                    outs[1][r, EARLY_ROWS:, :] = piece[EARLY_ROWS:, :].astype(BF)
+
+    chunking = early_chunks() if data_count else iter(())
+    for i in range(1, images):
+        before = i > 1
+        done = i == last
+        interleave(
+            back_scores(i, 0),
+            back_spread(i - 1, 3) if before else None,
+            outward_gradient(1) if i == 1 else None,
+        )
+        interleave(
+            back_scores(i, 1),
+            products(i - 1, 0) if before else None,
+            back_spread(i, 0),
+        )
+        interleave(
+            back_scores(i, 2),
+            products(i - 1, 1) if before else None,
+            back_spread(i, 1),
+        )
+        interleave(
+            back_scores(i, 3),
+            back_spread(i, 2),
+            weight_gradient(i - 1, 1) if i <= 2 * blocks else None,
+        )
+    for unit in range(last, 2 * blocks):
+        interleave(weight_gradient(unit, 1))
+    interleave(back_spread(last, 3), *[triple_gradient(c, 0) for c in range(3)])
+    interleave(products(last, 0), products(last, 1))
+    interleave(chunking)
+    sent += send((3, 4), dp_s, place_g)
+    gate_ref[...] = gate_g[...]
+    hp_ref[...] = hp_s[...]
+    for c in range(3):
+        interleave(triple_gradient(c, 1))
+    if data_count:
+        interleave(late_chunks())
     else:
         outs[0][...] = wide_g[0].T
         outs[1][...] = wide_g[1]
-        outs[2][...] = nn(left_t[2], low_s[...])
+        outs[2][...] = out_g[...]
         outs[3][...] = vec_g[...]
         outs[4][...] = hid_g[...]
         for c in range(3):
-            outs[5][c * width : (c + 1) * width, :] = triple[c]
+            rows = pl.ds(c * width, width)
+            outs[5][rows, :] = jnp.concatenate(
+                [tri_p[0, rows, 0:half], tri_p[1, rows, 0:half]], axis=1
+            )
     for member in sent:
         member.wait()
 
@@ -759,22 +829,25 @@
         return pltpu.VMEM(dims, F32)
 
     scratch = [
-        *[bf(width, width)] * 4,
+        *[bf(width, 256)] * 3,
+        bf(width, width),
+        bf(width, 256),
         bf(width, hidden),
         bf(width, hidden),
         f32(8, hidden),
         f32(8, 128),
         bf(kp, 128),
+        bf(kp, 128),
         bf(heads, 128, qp),
         bf(2, qp, width),
-        bf(kp, qp),
-        bf(width, qp),
-        bf(images, heads, qp, qp),
-        bf(images, heads, qp, width),
-        bf(images, kp, width),
-        bf(images, width, qp),
+        bf(kp, 256),
+        bf(256, qp),
+        bf(images, heads, qp, 128),
+        bf(images, heads, qp, 128),
+        bf(images, kp, 256),
+        bf(images, 256, qp),
         f32(images, heads, 2, kp, qp),
-        f32(kp, width),
+        f32(images, kp, width),
         f32(kp, width),
         bf(kp, width),
         f32(kp, 1),
@@ -782,55 +855,61 @@
         f32(4 * heads, qp),
         f32(2 * heads, qp),
         bf(width, full),
-        bf(3, width, full),
+        bf(width, full),
+        bf(2, width, full),
         bf(2, full, hidden),
         f32(images, kp, width),
-        f32(images, kp, width),
-        bf(3, full, width),
+        bf(3, full, 256),
         f32(heads, kp, qp),
         f32(heads, kp, qp),
         bf(2, qp, qp),
         f32(heads, kp, qp),
         f32(8, qp),
         f32(2, kp, qp),
-        bf(2, kp, heads * qp),
-        bf(2, kp, heads * qp),
+        bf(kp, heads * qp),
+        bf(kp, heads * qp),
         f32(2, width, hidden),
+        f32(width, width),
         f32(4, 8, width),
         f32(8, hidden),
-        pltpu.SemaphoreType.DMA((3,)),
+        f32(2, 3 * width, 128),
+        pltpu.SemaphoreType.DMA((5,)),
     ]
     if data_count:
-        scratch += [f32(2, hidden, 128), f32(2, width, 128), f32(2, 3 * width, 128)]
+        scratch += [f32(2, hidden, 128), f32(2, width, 128)]
         scratch.append(f32(4, CHUNK_ROWS, 128))
     return pl.pallas_call(
         functools.partial(layer_kernel, patches=patches, heads=heads, data_count=data_count),
         out_shape=(
+            sds(full, hidden, dtype=BF),
             sds(images, kp, width),
             sds(images, kp, width),
-            sds(3, full, width, dtype=BF),
-            sds(1, 128),
+            sds(3, full, 256, dtype=BF),
+            sds(heads, kp, qp),
+            pltpu.VMEM((8, qp), F32),
+            pltpu.VMEM((8, 128), F32),
             *outs,
         ),
         in_specs=[VM] * 6,
-        out_specs=(ANYWHERE,) * 3 + (VM,) * (1 + len(outs)),
+        out_specs=(ANYWHERE,) * 5 + (VM,) * (2 + len(outs)),
         scratch_shapes=scratch,
         compiler_params=pltpu.CompilerParams(vmem_limit_bytes=LAYER_VMEM),
         name="layer",
     )(*near(x, inc, bias, own, oth), vec)
 
 
-def finish_kernel(
-    x_ref, own_ref, oth_ref, vec_ref, res_hbm, gm_hbm, dp_hbm, res_out, gi_out, vec_out,
-    res_s, gm_s, dp_s, w, vec_g, rows_s, sems, *, patches,
-):
+def finish_kernel(*refs, patches, heads):
+    (x_ref, own_ref, oth_ref, vec_ref, gate_ref, hp_ref), far_refs = refs[:6], refs[6:11]
+    (res_out, gi_out, vec_out, head_ref) = refs[11:15]
+    (act_s, mid_s, gm_s, dp_s, place_s), (w, wn, vec_g, rows_s, sems) = refs[15:20], refs[20:]
     images, kp, width = x_ref.shape
     qp = dp_s.shape[1] // images
     half = width // 2
+    wide = own_ref.shape[1]
     copies = [
         pltpu.make_async_copy(source, target, sems.at[at])
         for at, (source, target) in enumerate(
-            ((res_hbm, res_s), (gm_hbm, gm_s), (dp_hbm, dp_s))
+            zip(far_refs, (act_s, mid_s, gm_s, dp_s, place_s))
         )
     ]
     for member in copies:
@@ -839,15 +918,20 @@
     oth_tri = oth_ref[2 * width : 3 * width, :]
     for at in range(3):
         span = slice(at * half, (at + 1) * half)
-        w[at] = jnp.concatenate([own_tri[:, span], oth_tri[:, span]], axis=1)
+        w[at] = in_tiles(own_tri[:, span], oth_tri[:, span])
+    wn[:, 0:wide] = own_ref[width : 2 * width, :]
+    wn[:, wide : 2 * wide] = oth_ref[width : 2 * width, :]
     vec_g[...] = jnp.zeros_like(vec_g)
     gain = vec_ref[0:1, :]
-    copies[0].wait()
+    shift = vec_ref[5:6, :]
+    for member in copies[:2]:
+        member.wait()
     for i in range(images):
-        rows_s[i * patches : (i + 1) * patches, :] = res_s[i, 0:patches, :]
+        rows = mid_s[i] + nt(act_s[i * qp : i * qp + kp, :], wn[...]) + shift
+        rows_s[i * patches : (i + 1) * patches, :] = rows[0:patches]
     res_out[...] = rows_s[...].T
-    copies[1].wait()
-    copies[2].wait()
+    for member in copies[2:]:
+        member.wait()
     for i in range(images):
         n1, spread = norm_parts(x_ref[i].astype(F32))
         g = sum(nt(dp_s[c, i * qp : i * qp + kp, :], w[c]) for c in range(3))
@@ -857,28 +941,43 @@
         rows_s[i * patches : (i + 1) * patches, :] = rows[0:patches]
     gi_out[...] = rows_s[...].T
     vec_out[...] = jnp.sum(vec_g[...], axis=1)
-
-
-def run_finish(x, own, oth, vec, res, gm, dp, patches):
+    parts = offsets(kp, qp)
+    rank = lax.axis_index("tensor")
+    lane = lax.broadcasted_iota(jnp.int32, (1, 128), 1)
+    row = jnp.zeros((1, 128), F32)
+    half_heads = heads // 2
+    for h in range(heads):
+        base = ((rank + h // half_heads) % 2) * (4 * half_heads) + h % half_heads
+        g = place_s[h]
+        for k in range(3):
+            total = jnp.sum(g * parts[k])
+            row = row + jnp.where(lane == base + k * half_heads, total, 0.0)
+        gate = gate_of(hp_ref, h, 128)
+        total = jnp.sum(gate_ref[h : h + 1, :])
+        row = row + jnp.where(lane == base + 3 * half_heads, total * gate * (1.0 - gate), 0.0)
+    head_ref[...] = row
+
+
+def run_finish(x, own, oth, vec, gate, hp, act, mid, gm, dp, place, patches):
     images, kp, width = x.shape
     rows = images * patches
+    fetched = (act, mid, gm, dp, place)
     return pl.pallas_call(
-        functools.partial(finish_kernel, patches=patches),
-        out_shape=(sds(width, rows), sds(width, rows), sds(2, width)),
-        in_specs=[VM] * 4 + [ANYWHERE] * 3,
-        out_specs=(VM,) * 3,
+        functools.partial(finish_kernel, patches=patches, heads=place.shape[0]),
+        out_shape=(sds(width, rows), sds(width, rows), sds(2, width), sds(1, 128)),
+        in_specs=[VM] * 6 + [ANYWHERE] * 5,
+        out_specs=(VM,) * 4,
         scratch_shapes=[
-            pltpu.VMEM(res.shape, F32),
-            pltpu.VMEM(gm.shape, F32),
-            pltpu.VMEM(dp.shape, BF),
-            pltpu.VMEM((3, width, width), BF),
+            *[pltpu.VMEM(member.shape, member.dtype) for member in fetched],
+            pltpu.VMEM((3, width, 256), BF),
+            pltpu.VMEM((width, 2 * own.shape[1]), BF),
             pltpu.VMEM((2, 8, width), F32),
             pltpu.VMEM((rows, width), F32),
-            pltpu.SemaphoreType.DMA((3,)),
+            pltpu.SemaphoreType.DMA((5,)),
         ],
         compiler_params=pltpu.CompilerParams(vmem_limit_bytes=32 * 1024 * 1024),
         name="finish",
-    )(*near(x, own, oth), vec, *far(res, gm, dp))
+    )(*near(x, own, oth), vec, gate, hp, *far(*fetched))
 
 
 def combine_kernel(own_ref, got_ref, out_ref):
@@ -1160,7 +1259,7 @@
     )
     other = lax.ppermute(own, "tensor", swap)
     x, inc, bias = run_prepare(*rows_near)
-    result, grad_middle, dp, head_row, *sums = run_layer(
+    act, middle, grad_middle, dp, place, gate, hp, *sums = run_layer(
         x, inc, bias, own, other, vectors, heads, patches, chunked
     )
     if fast:
@@ -1190,12 +1289,12 @@
     received = lax.ppermute(theirs, "tensor", swap)
     chunks = run_combine(mine, received)
     got = lax.all_to_all(chunks, "dp", 0, 0, tiled=False)
-    result_t, grad_input_t, late_vec = run_finish(
-        x, own, other, vectors, result, grad_middle, dp, patches
+    result_t, grad_input_t, late_vec, head_row = run_finish(
+        x, own, other, vectors, gate, hp, act, middle, grad_middle, dp, place, patches
     )
     if fast:
         wt_f, wo_f, ww_f, wn_f = run_shares(
-            head_row, triple_rows, outward_weight, widen_weight, narrow_t, data_count
+            gate, triple_rows, outward_weight, widen_weight, narrow_t, data_count
         )
         blocks = [
             member.size // data_count // 384

time: 74.2 us -> 67.9 us (0.915)
  Pallas kernels: 43.1 us -> 38.4 us
  waiting for transfers between devices: 10.1 us -> 8.54 us
    pallas_call x1, Pallas kernels: 31.3 us -> 25 us  [run_layer(): pl.pallas_call(functools.partial(layer_kernel, patches=patches, heads=hea...]
    pallas_call x1, Pallas kernels: 6.17 us -> 7.79 us  [run_finish(): pl.pallas_call(functools.partial(finish_kernel, patches=patches, heads=pl...]
    all_to_all x1, waiting for transfers between devices: 8.06 us -> 6.46 us  [on_device(): got = lax.all_to_all(chunks, 'dp', 0, 0, tiled=False)]
  transfers between devices with their start and end apart: 3 -> 3, of which waited for: 3 -> 3; matrix products, arithmetic and copies ran while one was open for 0% -> 0% of each run, Pallas kernels for 11% -> 14%
where the time goes in v4:
time: 67.9 us; the launch traced here: 67.6 us
  Pallas kernels  38.4 us (57%)
  blocking collectives  10.1 us (15%)
  starting transfers between devices  9.18 us (14%)
  waiting for transfers between devices  8.54 us (13%)
  between operations  1.18 us (2%)
    pallas_call x1, Pallas kernels, run_layer(): pl.pallas_call(functools.partial(layer_kernel, patches=patches, heads=hea...  25 us
    all_to_all x1, blocking collectives, on_device(): last_got = lax.all_to_all(payload, ('dp', 'tensor'), 0, 0, tiled=False)  10.1 us
    all_to_all x1, starting transfers between devices, on_device(): got = lax.all_to_all(chunks, 'dp', 0, 0, tiled=False)  8.23 us
    pallas_call x1, Pallas kernels, run_finish(): pl.pallas_call(functools.partial(finish_kernel, patches=patches, heads=pl...  7.79 us
    all_to_all x1, waiting for transfers between devices, on_device(): got = lax.all_to_all(chunks, 'dp', 0, 0, tiled=False)  6.46 us
    pallas_call x1, Pallas kernels, run_pack(): pl.pallas_call(pack_kernel, out_shape=(pltpu.VMEM((3 * depth + 16, wide),...  1.71 us
    ppermute x1, waiting for transfers between devices, on_device(): received = lax.ppermute(theirs, 'tensor', swap)  1.54 us
  transfers between devices with their start and end apart: 3, of which 3 were waited for; matrix products, arithmetic and copies ran while one was open for 0% of the time, Pallas kernels for 14%

profile of v4, /device:TPU:0, one launch (start us, length us, event | category | flops | bytes accessed | tf_op | source)
XLA Modules:
  0.0 67.6 jit_solution(7244769624666432819)
XLA Ops:
  0.7 1.7 %pack_weights.1 = (bf16[592,384]{1,0:T(8,128)(2,1)S(1)}, bf16[192,1568]{1,0:T(8,128)(2,1)S(1)}, bf16[192,1568]{1,0:T(8,128)(2,1)S(1)}, s32[16,196]{1,0:T(8,128)S(1)}) custom-call(f32[3,192,96]{2,1,0:T(8,128)} %refs_0_.1, f32[96,192]{1,0:T(8,128)} %out_ref.1, f32[192,384]{1,0:T(8,128)} %wid_ref.1, f32[192,384]{1,0:T(8,128)} %bitcast.14, f32[384]{0:T(512)} %hb_ref.1, ...), custom_call_target="tpu_custom_call" | custom-call | tf_op jit(solution)/shard_map/pack_weights/pallas_call | solution.py:239
  2.4 0.5 collective-permute-start
  2.9 0.9 %prepare.1 = (bf16[8,208,192]{2,1,0:T(8,128)(2,1)S(1)}, bf16[8,208,192]{2,1,0:T(8,128)(2,1)S(1)}, bf16[8,208,128]{2,1,0:T(8,128)(2,1)S(1)}) custom-call(bf16[192,1568]{1,0:T(8,128)(2,1)S(1)} %get-tuple-element.77.tok_ref, bf16[192,1568]{1,0:T(8,128)(2,1)S(1)} %get-tuple-element.78.cot_ref, s32[16,196]{1,0:T(8,128)S(1)} %get-tuple-element.79.keep_ref), custom_call_target="tpu_custom_call" | custom-call | tf_op jit(solution)/shard_map/prepare/pallas_call | solution.py:281
  3.8 0.5 collective-permute-done.refs_4_.refs_2_
  4.3 25.0 %layer.1 = (bf16[2048,768]{1,0:T(8,128)(2,1)}, f32[8,208,192]{2,1,0:T(8,128)}, f32[8,208,192]{2,1,0:T(8,128)}, bf16[3,2048,256]{2,1,0:T(8,128)(2,1)}, f32[4,208,...) custom-call(bf16[8,208,192]{2,1,0:T(8,128)(2,1)S(1)} %get-tuple-elem, ...), custom_call_target="tpu_custom_call" | custom-call | tf_op jit(solution)/shard_map/layer/pallas_call | solution.py:881
  29.3 0.0 copy-start
  29.3 0.0 copy-start.1
  29.3 0.0 copy-start.2
  29.3 0.0 copy-start.3
  29.4 0.4 collective-permute-start.1
  29.8 1.5 %collective-permute-done.1.got_ref = bf16[16,128,128]{2,1,0:T(8,128)(2,1)S(1)} collective-permute-done((bf16[16,128,128]{2,1,0:T(8,128)(2,1)S(1)}, bf16[16,128,128]{2,1,0:T(8,128)(2,1)S(1)}, u32[]{:S(2)}, u32[]{:S(2)}) %collective-permute-start.1) | collective-permute-done | bytes 524320 | tf_op jit(solution)/shard_map/ppermute | solution.py:1289
  31.3 0.9 %combine.1 = bf16[16,128,128]{2,1,0:T(8,128)(2,1)} custom-call(f32[16,128,128]{2,1,0:T(8,128)S(1)} %get-tuple-element.93.own_ref, bf16[16,128,128]{2,1,0:T(8,128)(2,1)S(1)} %collective-permute-done.1.got_ref), custom_call_target="tpu_custom_call" | custom-call | tf_op jit(solution)/shard_map/combine/pallas_call | solution.py:988
  32.2 8.2 %all-to-all-start = ((bf16[16,128,128]{2,1,0:T(8,128)(2,1)}), bf16[16,128,128]{2,1,0:T(8,128)(2,1)S(1)}, u32[]{:S(2)}, u32[]{:S(2)}) async-start(bf16[16,128,128]{2,1,0:T(8,128)(2,1)} %combine.1), calls=%async_computation | async-start | bytes 1048576 | tf_op jit(solution)/shard_map/all_to_all | solution.py:1291
  40.5 0.0 copy-done
  40.5 0.0 copy-done.1
  40.5 0.0 copy-done.2
  40.5 0.0 copy-done.3
  40.5 0.9 %weight_shares.1 = (f32[1,3456]{1,0:T(1,128)S(1)}, f32[1,1152]{1,0:T(1,128)S(1)}, f32[1,4608]{1,0:T(1,128)S(1)}, f32[1,4608]{1,0:T(1,128)S(1)}) custom-call(f32[8,256]{1,0:T(8,128)S(1)} %get-tuple-element.84.refs_4_._, f32[576,96]{1,0:T(8,128)S(1)} %bitcast.13, f32[96,192]{1,0:T(8,128)S(1)} %copy-done.3, f32[192,384]{1,0:T(8,128)S(1)} %copy-done.1, ...), custom_call_target="tpu_custom_call" | custom-call | tf_op jit(solution)/shard_map/weight_shares/pallas_call | solution.py:1041
  41.4 0.0 copy-done.4
  41.4 0.0 copy-start.5
  41.4 0.0 copy-start.6
  41.5 0.0 copy-start.7
  41.5 0.0 copy-start.8
  41.5 0.0 copy-start.9
  41.5 0.0 copy-start.10
  41.5 0.0 copy-start.11
  41.5 0.0 copy-start.12
  41.5 0.0 copy-start.13
  41.5 0.0 copy-start.14
  41.6 0.0 copy-start.15
  41.6 0.0 copy-start.16
  41.6 0.0 copy-start.17
  41.6 0.0 copy-start.18
  41.6 0.0 copy-start.19
  41.6 0.0 copy-start.20
  41.6 7.8 %finish.1 = (f32[192,1568]{1,0:T(8,128)}, f32[192,1568]{1,0:T(8,128)}, f32[2,192]{1,0:T(2,128)S(1)}, f32[1,128]{1,0:T(1,128)S(1)}) custom-call(bf16[8,208,192]{2,1,0:T(8,128)(2,1)S(1)} %get-tuple-element.80.refs_0_, bf16[592,384]{1,0:T(8,128)(2,1)S(1)} %get-tuple-element.81.refs_3_.refs_1_, bf16[592,384]{1,0:T(8,128)(2,1)S(1)} %collective-permute-done.refs_4_.refs_2_, ...), custom_call_target="tpu_custom_call" | custom-call | tf_op jit(solution)/shard_map/finish/pallas_call | solution.py:965
  49.4 6.5 %all-to-all-done.got_ref = bf16[16,128,128]{2,1,0:T(8,128)(2,1)S(1)} async-done(((bf16[16,128,128]{2,1,0:T(8,128)(2,1)}), bf16[16,128,128]{2,1,0:T(8,128)(2,1)S(1)}, u32[]{:S(2)}, u32[]{:S(2)}) %all-to-all-start) | async-done | bytes 524320 | tf_op jit(solution)/shard_map/all_to_all | solution.py:1291
  55.9 0.2 sums.1
  56.1 10.1 %all_to_all.10.got_ref = f32[32,4,128]{2,1,0:T(4,128)S(1)} all-to-all(f32[32,4,128]{2,1,0:T(4,128)S(1)} %get-tuple-element.98), channel_id=1, replica_groups=mesh['dp'=16,'tensor'=2] {'dp','tensor'}, dimensions={0} | all-to-all | bytes 131072 | tf_op jit(solution)/shard_map/all_to_all | solution.py:1336
  66.2 0.0 copy-done.5
  66.3 0.0 copy-done.6
  66.3 0.0 copy-done.7
  66.3 0.0 copy-done.8
  66.3 0.0 copy-done.9
  66.3 0.0 copy-done.10
  66.3 0.0 copy-done.11
  66.3 0.0 copy-done.12
  66.4 1.1 %adam.1 = (f32[1,3456]{1,0:T(1,128)}, f32[1,3456]{1,0:T(1,128)}, f32[1,3456]{1,0:T(1,128)}, f32[1,1152]{1,0:T(1,128)}, f32[1,1152]{1,0:T(1,128)}, /*index=5*/f32...) custom-call(f32[32,4,128]{2,1,0:T(4,128)S(1)} %all_to_all.10.got_ref, ...), custom_call_target="tpu_custom_call" | custom-call | tf_op jit(solution)/shard_map/adam/pallas_call | solution.py:1180
  (9 shorter events, 0.0 us)
Async XLA Ops:
  2.4 2.0 %collective-permute-start = (bf16[592,384]{1,0:T(8,128)(2,1)S(1)}, bf16[592,384]{1,0:T(8,128)(2,1)S(1)}, u32[]{:S(2)}, u32[]{:S(2)}) collective-permute-start(bf16[592,384]{1,0:T(8,128)(2,1)S(1)} %get-tuple-element.81.refs_3_.refs_1_), channel_id=1, source_target_pairs={{0,1},{1,0},{2,3},{3,2},{4,5},{5,4},{6,7},{7,6},{8,9},{9,8},{10,11... | collective-permute-start | bytes 1363976 | tf_op jit(solution)/shard_map/ppermute | solution.py:1260
  29.3 11.2 %copy-start = (f32[3,192,96]{2,1,0:T(8,128)S(1)}, f32[3,192,96]{2,1,0:T(8,128)}, u32[]{:S(2)}) copy-start(f32[3,192,96]{2,1,0:T(8,128)} %refs_0_.1) | copy-start | bytes 663556
  29.3 11.2 %copy-start.1 = (f32[192,384]{1,0:T(8,128)S(1)}, f32[192,384]{1,0:T(8,128)}, u32[]{:S(2)}) copy-start(f32[192,384]{1,0:T(8,128)} %wid_ref.1) | copy-start | bytes 884740
  29.3 11.2 %copy-start.2 = (f32[384,192]{0,1:T(8,128)S(1)}, f32[384,192]{0,1:T(8,128)}, u32[]{:S(2)}) copy-start(f32[384,192]{0,1:T(8,128)} %param.30) | copy-start | bytes 884740
  29.3 11.2 %copy-start.3 = (f32[96,192]{1,0:T(8,128)S(1)}, f32[96,192]{1,0:T(8,128)}, u32[]{:S(2)}) copy-start(f32[96,192]{1,0:T(8,128)} %out_ref.1) | copy-start | bytes 221188
  29.4 2.0 %collective-permute-start.1 = (bf16[16,128,128]{2,1,0:T(8,128)(2,1)S(1)}, bf16[16,128,128]{2,1,0:T(8,128)(2,1)S(1)}, u32[]{:S(2)}, u32[]{:S(2)}) collective-permute-start(bf16[16,128,128]{2,1,0:T(8,128)(2,1)S(1)} %get-tuple-element.94), channel_id=1, source_target_pairs={{0,1},{1,0},{2,3},{3,2},{4,5},{5,4},{6,7},{7,6},{8,9},{9,8},{10,11... | collective-permute-start | bytes 1572872 | tf_op jit(solution)/shard_map/ppermute | solution.py:1289
  31.3 10.1 %copy-start.4 = (f32[6,192]{1,0:T(8,128)S(1)}, f32[6,192]{1,0:T(8,128)}, u32[]{:S(2)}) copy-start(f32[6,192]{1,0:T(8,128)} %vec_ref.1) | copy-start | bytes 13828
  32.2 23.6 %all-to-all-start = ((bf16[16,128,128]{2,1,0:T(8,128)(2,1)}), bf16[16,128,128]{2,1,0:T(8,128)(2,1)S(1)}, u32[]{:S(2)}, u32[]{:S(2)}) async-start(bf16[16,128,128]{2,1,0:T(8,128)(2,1)} %combine.1), calls=%async_computation | async-start | bytes 1048576 | tf_op jit(solution)/shard_map/all_to_all | solution.py:1291
  41.4 24.8 %copy-start.5 = (f32[1,4608]{1,0:T(1,128)S(1)}, f32[1,4608]{1,0:T(1,128)}, u32[]{:S(2)}) copy-start(f32[1,4608]{1,0:T(1,128)} %refs_12_.1) | copy-start | bytes 55300
  41.4 24.8 %copy-start.6 = (f32[1,4608]{1,0:T(1,128)S(1)}, f32[1,4608]{1,0:T(1,128)}, u32[]{:S(2)}) copy-start(f32[1,4608]{1,0:T(1,128)} %refs_13_.1) | copy-start | bytes 55300
  41.5 24.8 %copy-start.7 = (f32[1,4608]{1,0:T(1,128)S(1)}, f32[1,4608]{1,0:T(1,128)}, u32[]{:S(2)}) copy-start(f32[1,4608]{1,0:T(1,128)} %refs_14_.1) | copy-start | bytes 55300
  41.5 24.8 %copy-start.8 = (f32[1,4608]{1,0:T(1,128)S(1)}, f32[1,4608]{1,0:T(1,128)}, u32[]{:S(2)}) copy-start(f32[1,4608]{1,0:T(1,128)} %refs_15_.1) | copy-start | bytes 55300
  41.5 24.8 %copy-start.9 = (f32[1,3456]{1,0:T(1,128)S(1)}, f32[1,3456]{1,0:T(1,128)}, u32[]{:S(2)}) copy-start(f32[1,3456]{1,0:T(1,128)} %refs_8_.3) | copy-start | bytes 41476
  41.5 24.8 %copy-start.10 = (f32[1,3456]{1,0:T(1,128)S(1)}, f32[1,3456]{1,0:T(1,128)}, u32[]{:S(2)}) copy-start(f32[1,3456]{1,0:T(1,128)} %refs_9_.1) | copy-start | bytes 41476
  41.5 24.8 %copy-start.11 = (f32[384]{0:T(512)S(1)}, f32[384]{0:T(512)}, u32[]{:S(2)}) copy-start(f32[384]{0:T(512)} %hb_ref.1) | copy-start | bytes 4612
  41.5 24.8 %copy-start.12 = (f32[6,192]{1,0:T(8,128)S(1)}, f32[6,192]{1,0:T(8,128)}, u32[]{:S(2)}) copy-start(f32[6,192]{1,0:T(8,128)} %refs_16_.1) | copy-start | bytes 13828
  41.5 24.8 %copy-start.13 = (f32[6,192]{1,0:T(8,128)S(1)}, f32[6,192]{1,0:T(8,128)}, u32[]{:S(2)}) copy-start(f32[6,192]{1,0:T(8,128)} %refs_17_.1) | copy-start | bytes 13828
  41.5 24.8 %copy-start.14 = (f32[1,1152]{1,0:T(1,128)S(1)}, f32[1,1152]{1,0:T(1,128)}, u32[]{:S(2)}) copy-start(f32[1,1152]{1,0:T(1,128)} %refs_10_.1) | copy-start | bytes 13828
  41.6 24.8 %copy-start.15 = (f32[1,1152]{1,0:T(1,128)S(1)}, f32[1,1152]{1,0:T(1,128)}, u32[]{:S(2)}) copy-start(f32[1,1152]{1,0:T(1,128)} %refs_11_.1) | copy-start | bytes 13828
  41.6 24.8 %copy-start.16 = (f32[4,2]{0,1:T(2,128)S(1)}, f32[4,2]{0,1:T(2,128)}, u32[]{:S(2)}) copy-start(f32[4,2]{0,1:T(2,128)} %param.33) | copy-start | bytes 100
  41.6 24.8 %copy-start.17 = (f32[384]{0:T(512)S(1)}, f32[384]{0:T(512)}, u32[]{:S(2)}) copy-start(f32[384]{0:T(512)} %refs_18_.1) | copy-start | bytes 4612
  41.6 24.8 %copy-start.18 = (f32[384]{0:T(512)S(1)}, f32[384]{0:T(512)}, u32[]{:S(2)}) copy-start(f32[384]{0:T(512)} %refs_19_.1) | copy-start | bytes 4612
  41.6 24.8 %copy-start.19 = (f32[4,2]{0,1:T(2,128)S(1)}, f32[4,2]{0,1:T(2,128)}, u32[]{:S(2)}) copy-start(f32[4,2]{0,1:T(2,128)} %param.46) | copy-start | bytes 100
  41.6 24.8 %copy-start.20 = (f32[4,2]{0,1:T(2,128)S(1)}, f32[4,2]{0,1:T(2,128)}, u32[]{:S(2)}) copy-start(f32[4,2]{0,1:T(2,128)} %param.47) | copy-start | bytes 100

commit v5 on v4

--- a/solution.py
+++ b/solution.py
@@ -24,7 +24,9 @@
 SMALL_VMEM = 16 * 1024 * 1024
 EARLY_ROWS = 96
 LATE_ROWS = 32
-CHUNK_ROWS = EARLY_ROWS + LATE_ROWS
+SENT_EARLY = 80
+SENT_ROWS = 112
+SMALL_AT = 16
 PAIR = 2
 VM = pl.BlockSpec(memory_space=pltpu.VMEM)
 ANYWHERE = pl.BlockSpec(memory_space=pl.ANY)
@@ -295,8 +297,8 @@
     gate_ref, hp_ref = refs[11:13]
     outs = refs[13:15] if data_count else refs[13:19]
     at = 13 + len(outs)
-    (wq, wk, wv, wo, wop, wi, wn, hb_s, hp_s, key_p, key_i, query_p) = refs[at : at + 12]
-    at += 12
+    (wq, wk, wv, wo, wop, wi, wn, hp_s, key_p, key_i, query_p) = refs[at : at + 11]
+    at += 11
     (fst_s, keys_s, vt_s, qm_s, dmm_s, v_s, kt_s, soft_s, mid_s, n2_s) = refs[at : at + 10]
     at += 10
     (sec_s, spr_s, low_s, stat_s, back_s) = refs[at : at + 5]
@@ -306,7 +308,7 @@
     (place_g, gate_g, da_buf, att_s, ds_s, wide_g, out_g, vec_g, hid_g, tri_p, sems) = refs[at : at + 11]
     at += 11
     if data_count:
-        nar_p, out_p, tmp = refs[at : at + 3]
+        nar_p, out_p, nar_f, out_f, tri_f, tmp = refs[at : at + 6]
     images, kp, width = x_ref.shape
     qp = soft_s.shape[4]
     hd = width // heads
@@ -332,6 +334,7 @@
             right_s[side, k * qp + kp : (k + 1) * qp, :] = jnp.zeros((qp - kp, hidden), BF)
         for c in range(3):
             dp_s[c, k * qp + kp : (k + 1) * qp, :] = jnp.zeros((qp - kp, 256), BF)
+    sec_s[:, width:] = (lax.broadcasted_iota(jnp.int32, (kp, 256 - width), 1) < 3).astype(BF)
     gap = jnp.zeros((qp - kp, width), BF)
     one_lane = (lax.broadcasted_iota(jnp.int32, (STRIP, 128), 1) == half).astype(BF)
     masks = [head_mask(hd, h) for h in range(half_heads)]
@@ -464,22 +467,21 @@
             n2 = centred * spread
             n2_s[rows_of(r), :] = n2
             spr_s[rows_of(r), :] = spread
-            sec_s[rows_of(r), :] = (n2 * v[2] + v[3]).astype(BF)
+            sec_s[rows_of(r), 0:width] = (n2 * v[2] + v[3]).astype(BF)
 
         yield from staged(strips, LAG, mean, vary, put)
         left_t[0, :, columns_at(i)] = jnp.concatenate([inc_ref[i], gap], axis=0).T
         yield
-        left_t[1, :, columns_at(i)] = jnp.concatenate([sec_s[...], gap], axis=0).T
+        left_t[1, :, columns_at(i)] = jnp.concatenate([sec_s[:, 0:width], gap], axis=0).T
 
     def chunk(i, c, on):
         lanes = pl.ds(c * 256, 256)
         before = nn(sec_s[...], wi[:, lanes])
         back = nn(inc_ref[i], wn[:, lanes])
-        bias_row = hb_s[0:1, lanes]
         total = jnp.zeros((8, 256), F32)
         for r in range(strips):
             yield
-            gelu, slope = gelu_parts(cut(before, r) + bias_row)
+            gelu, slope = gelu_parts(cut(before, r))
             right_s[0, strip_rows(i, r), lanes] = gelu.astype(BF)
             grad_before = cut(back, r) * slope
             right_s[1, strip_rows(i, r), lanes] = grad_before.astype(BF)
@@ -487,7 +489,7 @@
         hid_g[:, lanes] += jnp.where(on, total, 0.0)
 
     def end(i, on):
-        grad_second = nt(right_s[1, image_rows(i), :], wi[...])
+        grad_second = nt(right_s[1, image_rows(i), :], wi[0:width, :])
         totals = [jnp.zeros((8, width), F32)] * 4
         mids = []
         for _ in range(WAIT):
@@ -556,8 +558,8 @@
         return carry
 
     interleave(first_norm(0))
-    wi[:, pl.ds(0, wide)] = own_ref[0:width, :]
-    wi[:, pl.ds(wide, wide)] = oth_ref[0:width, :]
+    wi[0:width, pl.ds(0, wide)] = own_ref[0:width, :]
+    wi[0:width, pl.ds(wide, wide)] = oth_ref[0:width, :]
     wn[:, pl.ds(0, wide)] = own_ref[width : 2 * width, :]
     wn[:, pl.ds(wide, wide)] = oth_ref[width : 2 * width, :]
     own_tri = own_ref[2 * width : 3 * width, :]
@@ -571,7 +573,10 @@
         tail = ref[3 * width : 3 * width + 16, :].astype(F32)
         each = 1 + half_heads
         small.append(tail[0:each] + tail[each : 2 * each] + tail[2 * each : 3 * each])
-    hb_s[0:1, :] = jnp.concatenate([member[0:1] for member in small], axis=1)
+    hb = jnp.concatenate([member[0:1] for member in small], axis=1)
+    wi[width:, :] = jnp.concatenate(
+        [*bf_parts(hb), jnp.zeros((256 - width - 3, hidden), F32)], axis=0
+    ).astype(BF)
     hp_s[...] = jnp.concatenate(
         [member[1:, :128] for member in small] + [jnp.zeros((8 - heads, 128), F32)], axis=0
     )
@@ -579,8 +584,24 @@
         query_p[h, 0:16, :] = query_operand(hp_s, h, qp)
     for part in range(2):
         interleave(project(0, part))
+    def leaving(first_image, count):
+        rows = pl.ds(pl.multiple_of(first_image * qp, 16), count * qp)
+        images_out = pl.ds(first_image, count)
+        for k, (source, at_rows) in enumerate(
+            ((right_s.at[0], rows), (mid_s, images_out), (gm_s, images_out))
+        ):
+            pltpu.make_async_copy(
+                source.at[at_rows], far_refs[k].at[at_rows], sems.at[k]
+            ).start()
+
     def forward_pair(j, carry):
-        return forward_step(2 * j + 1, forward_step(2 * j, carry))
+        forward_step(2 * j + 1, forward_step(2 * j, carry))
+
+        @pl.when(j > 0)
+        def _():
+            leaving(2 * j - 2, 2)
+
+        return carry
 
     lax.fori_loop(0, images // 2, forward_pair, 0)
 
@@ -687,70 +708,67 @@
     interleave(chunk(last, 2, on), products(0, 0), partial[5])
     interleave(end(last, on), products(0, 1), *partial[6:])
 
-    def send(slots, *sources):
-        copies = [
-            pltpu.make_async_copy(source, far_refs[k], sems.at[k])
-            for k, source in zip(slots, sources)
-        ]
-        for member in copies:
-            member.start()
-        return copies
-
-    sent = send((0, 1, 2), right_s.at[0], mid_s, gm_s)
-
-
-    def piece_of(r, side):
-        return outs[0].at[r] if side == 0 else tmp.at[r % 4]
+    leaving(images - 2, 2)
+
 
     def early_chunks():
         put_planes(nar_p, wide_g[0].T)
-        yield
         put_planes(out_p, out_g[...])
-        early = jnp.sum(vec_g[...], axis=1)
-        hidden_sum = jnp.sum(hid_g[...], axis=0, keepdims=True)
-        rest = width - 128
-        wp, np_, op = width // data_count, wide // data_count // 2, half // data_count // 2
-        small_at = 3 * (wp + np_ + op)
+        for side in range(2):
+            for k, part in enumerate(even_odd_tiles(nar_p, side * wide, wide // 2)):
+                nar_f[side, k] = part
+            for k, part in enumerate(even_odd_tiles(out_p, side * half, half // 2)):
+                out_f[side, k] = part
+            yield
         for r in range(data_count):
             for side in range(2):
                 yield
-                piece = piece_of(r, side)
+                piece = outs[0].at[r] if side == 0 else tmp.at[r]
                 for k in range(3):
                     lanes = slice(side * wide + 128 * k, side * wide + 128 * (k + 1))
                     piece[k * wp : (k + 1) * wp, :] = wide_g[1, r * wp : (r + 1) * wp, lanes]
-                    piece[small_at + 8 + k : small_at + 9 + k, :] = hidden_sum[:, lanes]
-                base = 3 * wp
-                parts = even_odd_tiles(nar_p, side * wide + 2 * np_ * r, np_)
-                for k in range(3):
-                    piece[base + k * np_ : base + (k + 1) * np_, :] = parts[k]
-                base += 3 * np_
-                parts = even_odd_tiles(out_p, side * half + 2 * op * r, op)
-                for k in range(3):
-                    piece[base + k * op : base + (k + 1) * op, :] = parts[k]
-                piece[small_at : small_at + 4, :] = early[:, :128]
-                piece[small_at + 4 : small_at + 8, 0:rest] = early[:, 128:]
-                piece[small_at + 4 : small_at + 8, rest:] = jnp.zeros((4, 128 - rest), F32)
-                piece[small_at + 11 : EARLY_ROWS, :] = jnp.zeros(
-                    (EARLY_ROWS - small_at - 11, 128), F32
-                )
+                    row = 3 * wp + k * np_
+                    piece[row : row + np_, :] = nar_f[side, k, r * np_ : (r + 1) * np_, :]
+                    row = 3 * (wp + np_) + k * op
+                    piece[row : row + op, :] = out_f[side, k, r * op : (r + 1) * op, :]
                 if side:
-                    outs[1][r, 0:EARLY_ROWS, :] = piece[0:EARLY_ROWS, :].astype(BF)
+                    outs[1][r, 0:SENT_EARLY, :] = piece[0:SENT_EARLY, :].astype(BF)
 
     def late_chunks():
+        early = jnp.sum(vec_g[...], axis=1)
+        hidden_sum = jnp.sum(hid_g[...], axis=0, keepdims=True)
+        vec_n, hid_n = 4 * width // data_count, wide // data_count
+        rest = jnp.zeros((1, 128 - vec_n - hid_n), F32)
         groups = 3 * width // data_count // 4
+        small_at = 3 * (wp + np_ + op)
+        for side in range(2):
+            for k, part in enumerate(four_row_tiles(tri_p, side, 0, 3 * width // 4)):
+                tri_f[side, k] = part
+            yield
         for r in range(data_count):
             for side in range(2):
                 yield
-                piece = piece_of(r, side)
-                parts = four_row_tiles(tri_p, side, 4 * groups * r, groups)
+                piece = outs[0].at[r] if side == 0 else tmp.at[r]
+                row, lane = divmod(r * vec_n, width)
+                at_hidden = side * wide + r * hid_n
+                piece[small_at : small_at + 1, :] = jnp.concatenate(
+                    [
+                        early[row : row + 1, lane : lane + vec_n],
+                        hidden_sum[:, at_hidden : at_hidden + hid_n],
+                        rest,
+                    ],
+                    axis=1,
+                )
                 for k in range(3):
-                    row = EARLY_ROWS + k * groups
-                    piece[row : row + groups, :] = parts[k]
-                row = EARLY_ROWS + 3 * groups
-                piece[row:CHUNK_ROWS, :] = jnp.zeros((CHUNK_ROWS - row, 128), F32)
+                    row = small_at + 1 + k * groups
+                    piece[row : row + groups, :] = tri_f[side, k, r * groups : (r + 1) * groups, :]
+                row = small_at + 1 + 3 * groups
+                piece[row:SENT_ROWS, :] = jnp.zeros((SENT_ROWS - row, 128), F32)
                 if side:
-                    outs[1][r, EARLY_ROWS:, :] = piece[EARLY_ROWS:, :].astype(BF)
-
+                    outs[1][r, SENT_EARLY:, :] = piece[SENT_EARLY:, :].astype(BF)
+
+    if data_count:
+        wp, np_, op = width // data_count, wide // data_count // 2, half // data_count // 2
     chunking = early_chunks() if data_count else iter(())
     for i in range(1, images):
         before = i > 1
@@ -780,7 +798,8 @@
     interleave(back_spread(last, 3), *[triple_gradient(c, 0) for c in range(3)])
     interleave(products(last, 0), products(last, 1))
     interleave(chunking)
-    sent += send((3, 4), dp_s, place_g)
+    for k, source in ((3, dp_s), (4, place_g)):
+        pltpu.make_async_copy(source, far_refs[k], sems.at[k]).start()
     gate_ref[...] = gate_g[...]
     hp_ref[...] = hp_s[...]
     for c in range(3):
@@ -798,19 +817,20 @@
             outs[5][rows, :] = jnp.concatenate(
                 [tri_p[0, rows, 0:half], tri_p[1, rows, 0:half]], axis=1
             )
-    for member in sent:
-        member.wait()
+    for k, source in enumerate((right_s.at[0], mid_s, gm_s, dp_s, place_g)):
+        pltpu.make_async_copy(source, far_refs[k], sems.at[k]).wait()
 
 
 def run_layer(x, inc, bias, own, oth, vec, heads, patches, data_count):
     images, kp, width = x.shape
     qp = -(-patches // 128) * 128
-    hidden = 2 * own.shape[1]
+    wide, half = own.shape[1], width // 2
+    hidden = 2 * wide
     full = images * qp
     if data_count:
         outs = [
-            pltpu.VMEM((data_count, CHUNK_ROWS, 128), F32),
-            pltpu.VMEM((data_count, CHUNK_ROWS, 128), BF),
+            pltpu.VMEM((data_count, SENT_ROWS, 128), F32),
+            pltpu.VMEM((data_count, SENT_ROWS, 128), BF),
         ]
     else:
         outs = [
@@ -832,9 +852,8 @@
         *[bf(width, 256)] * 3,
         bf(width, width),
         bf(width, 256),
+        bf(256, hidden),
         bf(width, hidden),
-        bf(width, hidden),
-        f32(8, hidden),
         f32(8, 128),
         bf(kp, 128),
         bf(kp, 128),
@@ -849,7 +868,7 @@
         f32(images, heads, 2, kp, qp),
         f32(images, kp, width),
         f32(kp, width),
-        bf(kp, width),
+        bf(kp, 256),
         f32(kp, 1),
         bf(full, width),
         f32(4 * heads, qp),
@@ -877,7 +896,8 @@
     ]
     if data_count:
         scratch += [f32(2, hidden, 128), f32(2, width, 128)]
-        scratch.append(f32(4, CHUNK_ROWS, 128))
+        scratch += [f32(2, 3, wide // 2, 128), f32(2, 3, half // 2, 128)]
+        scratch += [f32(2, 3, 3 * width // 4, 128), f32(data_count, SENT_ROWS, 128)]
     return pl.pallas_call(
         functools.partial(layer_kernel, patches=patches, heads=heads, data_count=data_count),
         out_shape=(
@@ -1062,47 +1082,41 @@
             flat_ref[0:1, tile : tile + 128] = from_ref[at : at + 1, :]
 
 
-def sum_kernel(got_ref, late_ref, head_ref, _, *refs, blocks):
-    (tri_f, out_f, wid_f, nar_f, vec_ref, hid_ref, pay_ref, tot) = refs
-    width = late_ref.shape[1]
+def sum_kernel(got_ref, late_ref, head_ref, _, *refs, blocks, span):
+    (tri_f, out_f, wid_f, nar_f, pay_ref, tot) = refs
     tri_b, out_b, wid_b, nar_b = blocks
+    vec_n, hid_n = span
     tot[...] = jnp.sum(got_ref[...].astype(F32), axis=0)
     spread_rows(wid_f, tot, 0, wid_b)
     spread_rows(nar_f, tot, 3 * wid_b, nar_b)
     spread_rows(out_f, tot, 3 * (wid_b + nar_b), out_b)
-    spread_rows(tri_f, tot, EARLY_ROWS, tri_b)
     at = 3 * (wid_b + nar_b + out_b)
-    vec_ref[...] = jnp.concatenate(
-        [tot[at : at + 4, :], tot[at + 4 : at + 8, : width - 128]], axis=1
-    )
-    hid = jnp.concatenate([tot[at + 8 + k : at + 9 + k, :] for k in range(3)], axis=1)
-    hid_ref[...] = hid
+    spread_rows(tri_f, tot, at + 1, tri_b)
     early = tot[0:at, :]
-    late = tot[EARLY_ROWS : EARLY_ROWS + 3 * tri_b, :]
-    squares = jnp.sum(early * early) + jnp.sum(late * late)
-    squares = squares + jnp.where(lax.axis_index("dp") == 0, jnp.sum(hid * hid), 0.0)
+    late = tot[at + 1 : at + 1 + 3 * tri_b, :]
+    small = tot[at : at + 1, :]
+    hid = small[:, vec_n : vec_n + hid_n]
+    squares = jnp.sum(early * early) + jnp.sum(late * late) + jnp.sum(hid * hid)
     lane = lax.broadcasted_iota(jnp.int32, (1, 128), 1)
     tails = jnp.concatenate([late_ref[0:1, 128:], late_ref[1:2, 128:]], axis=1)
+    last = jnp.concatenate([head_ref[:, 0:SMALL_AT], small[:, 0 : 128 - SMALL_AT]], axis=1)
     payload = jnp.concatenate(
-        [late_ref[:, :128], tails, jnp.where(lane == 127, squares, head_ref[...])], axis=0
+        [late_ref[:, :128], tails, jnp.where(lane == 127, squares, last)], axis=0
     )
     pay_ref[...] = jnp.broadcast_to(payload[None], pay_ref.shape)
 
 
-def run_sums(got, late_vec, head, after, blocks, wide):
+def run_sums(got, late_vec, head, after, blocks, span):
     count = got.shape[0]
-    width = late_vec.shape[1]
     return pl.pallas_call(
-        functools.partial(sum_kernel, blocks=blocks),
+        functools.partial(sum_kernel, blocks=blocks, span=span),
         out_shape=(
             *[sds(1, 3 * 128 * member) for member in blocks],
-            sds(4, width),
-            sds(1, wide),
             sds(2 * count, 4, 128),
         ),
         in_specs=[VM] * 4,
-        out_specs=(VM,) * 7,
-        scratch_shapes=[pltpu.VMEM((CHUNK_ROWS, 128), F32)],
+        out_specs=(VM,) * 5,
+        scratch_shapes=[pltpu.VMEM((SENT_ROWS, 128), F32)],
         compiler_params=PARAMS,
         name="sums",
     )(got, late_vec, head, after)
@@ -1117,16 +1131,52 @@
     return moment_new, squares_new, weight - rate * (quotient + decay * weight)
 
 
-def adam_kernel(got_ref, early_ref, hid_ref, hp_ref, vec_ref, hb_ref, *refs):
+def gathered(last, width, wide):
+    count = last.shape[0] // 2
+    vec_n, hid_n = 4 * width // count, wide // count
+    even = last[pl.ds(0, count, stride=2), :]
+    odd = last[pl.ds(1, count, stride=2), :]
+    mine = jnp.where(lax.axis_index("tensor") == 0, even, odd)
+
+    def placed(part, times):
+        n = part.shape[1]
+        value = jnp.concatenate([part] * times, axis=1)
+        row = lax.broadcasted_iota(jnp.int32, value.shape, 0)
+        lane = lax.broadcasted_iota(jnp.int32, value.shape, 1)
+        at = jnp.floor((lane.astype(F32) + 0.5) * (1.0 / n)).astype(jnp.int32)
+        return value, row, at
+
+    per_row = width // vec_n
+    value, row, at = placed(even[:, SMALL_AT : SMALL_AT + vec_n], per_row)
+    vector = jnp.concatenate(
+        [
+            jnp.sum(jnp.where(row == at + v * per_row, value, 0.0), axis=0, keepdims=True)
+            for v in range(4)
+        ],
+        axis=0,
+    )
+    at_hidden = SMALL_AT + vec_n
+    value, row, at = placed(mine[:, at_hidden : at_hidden + hid_n], count)
+    return vector, jnp.sum(jnp.where(row == at, value, 0.0), axis=0, keepdims=True)
+
+
+def adam_kernel(got_ref, hp_ref, vec_ref, hb_ref, *refs, given_sums):
+    refs = list(refs)
+    sums = [refs.pop(0) for _ in range(2 * given_sums)]
     grads = refs[0:4]
     weights = refs[4:8]
     states = refs[8:22]
     outs = refs[22:43]
-    norm_ref = refs[43]
+    norm_ref, last = refs[43:45]
     width = vec_ref.shape[1]
     half_heads = hp_ref.shape[0]
     tail = width - 128
     total = jnp.sum(got_ref[...], axis=0)
+    if given_sums:
+        early, hid = sums[0][...], sums[1][...]
+    else:
+        last[...] = got_ref[:, 3, :]
+        early, hid = gathered(last, width, hb_ref.shape[0])
     late = jnp.concatenate(
         [
             total[0:2, :],
@@ -1134,7 +1184,7 @@
         ],
         axis=1,
     )
-    vector = jnp.concatenate([late, early_ref[...]], axis=0)
+    vector = jnp.concatenate([late, early], axis=0)
     lane = lax.broadcasted_iota(jnp.int32, (1, 128), 1)
     heads_row = jnp.where(lane < 8 * half_heads, total[3:4, :], 0.0)
     squares = (
@@ -1156,8 +1206,8 @@
         ],
         axis=0,
     )
-    given = [ref[...] for ref in grads] + [vector, hid_ref[...], head]
-    wide = hid_ref.shape[1]
+    given = [ref[...] for ref in grads] + [vector, hid, head]
+    wide = hid.shape[1]
     held = [ref[...] for ref in weights] + [vec_ref[...], hb_ref[...].reshape(1, wide), hp_ref[...]]
     for at in range(7):
         renewed = adam_parts(
@@ -1173,18 +1223,19 @@
             out[...] = renewed[step].reshape(out.shape)
 
 
-def run_adam(got, early, hid, hp_t, vec, hb, grads, weights, states):
+def run_adam(got, hp_t, vec, hb, sums, grads, weights, states):
     shapes = []
     for at in range(7):
         shapes += [sds(*states[2 * at].shape)] * 3
     return pl.pallas_call(
-        adam_kernel,
+        functools.partial(adam_kernel, given_sums=len(sums) // 2),
         out_shape=(*shapes, sds(1)),
-        in_specs=[VM] * (6 + 4 + 4 + 14),
+        in_specs=[VM] * (4 + len(sums) + 4 + 4 + 14),
         out_specs=(VM,) * 21 + (SM,),
+        scratch_shapes=[pltpu.VMEM((got.shape[0], 128), F32)],
         compiler_params=PARAMS,
         name="adam",
-    )(got, early, hid, hp_t, vec, hb, *grads, *weights, *states)
+    )(got, hp_t, vec, hb, *sums, *grads, *weights, *states)
 
 
 def plain_chunks(halves, data_count, rows):
@@ -1243,6 +1294,10 @@
         and half % (2 * data_count) == 0
         and 3 * depth % (4 * data_count) == 0
     )
+    if fast:
+        early_rows = (2 * depth * wide + half * depth) // data_count // 128
+        late_rows = 3 * depth * half // data_count // 128
+        fast = SENT_EARLY <= early_rows and early_rows + 1 + late_rows <= SENT_ROWS
     chunked = data_count if fast else 0
     swap = [(0, 1), (1, 0)]
 
@@ -1300,9 +1355,11 @@
             member.size // data_count // 384
             for member in (triple_rows, outward_weight, widen_weight, narrow_t)
         ]
-        tri_f, out_f, wid_f, nar_f, early_vec, hid, payload = run_sums(
-            got, late_vec, head_row, wo_f, blocks, wide
+        span = (4 * depth // data_count, wide // data_count)
+        tri_f, out_f, wid_f, nar_f, payload = run_sums(
+            got, late_vec, head_row, wo_f, blocks, span
         )
+        sums = ()
     else:
         total = jnp.sum(got.astype(F32), axis=0)
         early_sum = total[:EARLY_ROWS].reshape(1, -1)
@@ -1333,14 +1390,14 @@
             ]
         )
         payload = jnp.broadcast_to(payload[None], (2 * data_count, 4, 128))
+        sums = (early_vec, hid)
     last_got = lax.all_to_all(payload, ("dp", "tensor"), 0, 0, tiled=False)
     renewed = run_adam(
         last_got,
-        early_vec,
-        hid,
         head_t,
         vectors,
         hidden_bias,
+        sums,
         (tri_f, out_f, wid_f, nar_f),
         (wt_f, wo_f, ww_f, wn_f),
         (

time: 67.9 us -> 65.9 us (0.971)
  waiting for transfers between devices: 8.54 us -> 7.24 us
    all_to_all x1, waiting for transfers between devices: 6.46 us -> 5.24 us  [on_device(): got = lax.all_to_all(chunks, 'dp', 0, 0, tiled=False)]
  transfers between devices with their start and end apart: 3 -> 3, of which waited for: 3 -> 3; matrix products, arithmetic and copies ran while one was open for 0% -> 0% of each run, Pallas kernels for 14% -> 15%
where the time goes in v5:
time: 65.9 us; the launch traced here: 65.6 us
  Pallas kernels  38 us (58%)
  blocking collectives  9.96 us (15%)
  starting transfers between devices  9.17 us (14%)
  waiting for transfers between devices  7.24 us (11%)
  between operations  1.18 us (2%)
    pallas_call x1, Pallas kernels, run_layer(): pl.pallas_call(functools.partial(layer_kernel, patches=patches, heads=hea...  24.5 us
    all_to_all x1, blocking collectives, on_device(): last_got = lax.all_to_all(payload, ('dp', 'tensor'), 0, 0, tiled=False)  9.96 us
    all_to_all x1, starting transfers between devices, on_device(): got = lax.all_to_all(chunks, 'dp', 0, 0, tiled=False)  8.22 us
    pallas_call x1, Pallas kernels, run_finish(): pl.pallas_call(functools.partial(finish_kernel, patches=patches, heads=pl...  7.79 us
    all_to_all x1, waiting for transfers between devices, on_device(): got = lax.all_to_all(chunks, 'dp', 0, 0, tiled=False)  5.24 us
    pallas_call x1, Pallas kernels, run_pack(): pl.pallas_call(pack_kernel, out_shape=(pltpu.VMEM((3 * depth + 16, wide),...  1.71 us
    ppermute x1, waiting for transfers between devices, on_device(): received = lax.ppermute(theirs, 'tensor', swap)  1.45 us
  transfers between devices with their start and end apart: 3, of which 3 were waited for; matrix products, arithmetic and copies ran while one was open for 0% of the time, Pallas kernels for 15%

profile of v5, /device:TPU:0, one launch (start us, length us, event | category | flops | bytes accessed | tf_op | source)
XLA Modules:
  0.0 65.6 jit_solution(5071969443295569345)
XLA Ops:
  0.7 1.7 %pack_weights.1 = (bf16[592,384]{1,0:T(8,128)(2,1)S(1)}, bf16[192,1568]{1,0:T(8,128)(2,1)S(1)}, bf16[192,1568]{1,0:T(8,128)(2,1)S(1)}, s32[16,196]{1,0:T(8,128)S(1)}) custom-call(f32[3,192,96]{2,1,0:T(8,128)} %refs_0_.1, f32[96,192]{1,0:T(8,128)} %out_ref.1, f32[192,384]{1,0:T(8,128)} %wid_ref.1, f32[192,384]{1,0:T(8,128)} %bitcast.14, f32[384]{0:T(512)} %hb_ref.1, ...), custom_call_target="tpu_custom_call" | custom-call | tf_op jit(solution)/shard_map/pack_weights/pallas_call | solution.py:241
  2.4 0.5 collective-permute-start
  2.9 0.9 %prepare.1 = (bf16[8,208,192]{2,1,0:T(8,128)(2,1)S(1)}, bf16[8,208,192]{2,1,0:T(8,128)(2,1)S(1)}, bf16[8,208,128]{2,1,0:T(8,128)(2,1)S(1)}) custom-call(bf16[192,1568]{1,0:T(8,128)(2,1)S(1)} %get-tuple-element.75.tok_ref, bf16[192,1568]{1,0:T(8,128)(2,1)S(1)} %get-tuple-element.76.cot_ref, s32[16,196]{1,0:T(8,128)S(1)} %get-tuple-element.77.keep_ref), custom_call_target="tpu_custom_call" | custom-call | tf_op jit(solution)/shard_map/prepare/pallas_call | solution.py:283
  3.8 0.5 collective-permute-done.refs_4_.refs_2_
  4.3 24.5 %layer.1 = (bf16[2048,768]{1,0:T(8,128)(2,1)}, f32[8,208,192]{2,1,0:T(8,128)}, f32[8,208,192]{2,1,0:T(8,128)}, bf16[3,2048,256]{2,1,0:T(8,128)(2,1)}, f32[4,208,...) custom-call(bf16[8,208,192]{2,1,0:T(8,128)(2,1)S(1)} %get-tuple-elem, ...), custom_call_target="tpu_custom_call" | custom-call | tf_op jit(solution)/shard_map/layer/pallas_call | solution.py:901
  28.9 0.0 copy-start
  28.9 0.0 copy-start.1
  28.9 0.0 copy-start.2
  28.9 0.0 copy-start.3
  28.9 0.4 collective-permute-start.1
  29.3 1.4 %collective-permute-done.1.got_ref = bf16[16,112,128]{2,1,0:T(8,128)(2,1)S(1)} collective-permute-done((bf16[16,112,128]{2,1,0:T(8,128)(2,1)S(1)}, bf16[16,112,128]{2,1,0:T(8,128)(2,1)S(1)}, u32[]{:S(2)}, u32[]{:S(2)}) %collective-permute-start.1) | collective-permute-done | bytes 458784 | tf_op jit(solution)/shard_map/ppermute | solution.py:1344
  30.8 0.9 %combine.1 = bf16[16,112,128]{2,1,0:T(8,128)(2,1)} custom-call(f32[16,112,128]{2,1,0:T(8,128)S(1)} %get-tuple-element.91.own_ref, bf16[16,112,128]{2,1,0:T(8,128)(2,1)S(1)} %collective-permute-done.1.got_ref), custom_call_target="tpu_custom_call" | custom-call | tf_op jit(solution)/shard_map/combine/pallas_call | solution.py:1008
  31.7 8.2 %all-to-all-start = ((bf16[16,112,128]{2,1,0:T(8,128)(2,1)}), bf16[16,112,128]{2,1,0:T(8,128)(2,1)S(1)}, u32[]{:S(2)}, u32[]{:S(2)}) async-start(bf16[16,112,128]{2,1,0:T(8,128)(2,1)} %combine.1), calls=%async_computation | async-start | bytes 917504 | tf_op jit(solution)/shard_map/all_to_all | solution.py:1346
  39.9 0.0 copy-done
  39.9 0.0 copy-done.1
  39.9 0.0 copy-done.2
  39.9 0.0 copy-done.3
  39.9 0.9 %weight_shares.1 = (f32[1,3456]{1,0:T(1,128)S(1)}, f32[1,1152]{1,0:T(1,128)S(1)}, f32[1,4608]{1,0:T(1,128)S(1)}, f32[1,4608]{1,0:T(1,128)S(1)}) custom-call(f32[8,256]{1,0:T(8,128)S(1)} %get-tuple-element.82.refs_4_._, f32[576,96]{1,0:T(8,128)S(1)} %bitcast.13, f32[96,192]{1,0:T(8,128)S(1)} %copy-done.3, f32[192,384]{1,0:T(8,128)S(1)} %copy-done.1, ...), custom_call_target="tpu_custom_call" | custom-call | tf_op jit(solution)/shard_map/weight_shares/pallas_call | solution.py:1061
  40.9 0.0 copy-start.5
  40.9 0.0 copy-start.6
  40.9 0.0 copy-start.7
  40.9 0.0 copy-start.8
  40.9 0.0 copy-start.9
  40.9 0.0 copy-start.10
  40.9 0.0 copy-start.11
  40.9 0.0 copy-start.12
  40.9 0.0 copy-start.13
  41.0 0.0 copy-start.14
  41.0 0.0 copy-start.15
  41.0 0.0 copy-start.16
  41.0 0.0 copy-start.17
  41.0 0.0 copy-start.18
  41.0 0.0 copy-start.19
  41.0 0.0 copy-start.20
  41.0 7.8 %finish.1 = (f32[192,1568]{1,0:T(8,128)}, f32[192,1568]{1,0:T(8,128)}, f32[2,192]{1,0:T(2,128)S(1)}, f32[1,128]{1,0:T(1,128)S(1)}) custom-call(bf16[8,208,192]{2,1,0:T(8,128)(2,1)S(1)} %get-tuple-element.78.refs_0_, bf16[592,384]{1,0:T(8,128)(2,1)S(1)} %get-tuple-element.79.refs_3_.refs_1_, bf16[592,384]{1,0:T(8,128)(2,1)S(1)} %collective-permute-done.refs_4_.refs_2_, ...), custom_call_target="tpu_custom_call" | custom-call | tf_op jit(solution)/shard_map/finish/pallas_call | solution.py:985
  48.8 5.2 %all-to-all-done.got_ref = bf16[16,112,128]{2,1,0:T(8,128)(2,1)S(1)} async-done(((bf16[16,112,128]{2,1,0:T(8,128)(2,1)}), bf16[16,112,128]{2,1,0:T(8,128)(2,1)S(1)}, u32[]{:S(2)}, u32[]{:S(2)}) %all-to-all-start) | async-done | bytes 458784 | tf_op jit(solution)/shard_map/all_to_all | solution.py:1346
  54.1 0.2 sums.1
  54.3 10.0 %all_to_all.10.got_ref = f32[32,4,128]{2,1,0:T(4,128)S(1)} all-to-all(f32[32,4,128]{2,1,0:T(4,128)S(1)} %get-tuple-element.96), channel_id=1, replica_groups=mesh['dp'=16,'tensor'=2] {'dp','tensor'}, dimensions={0} | all-to-all | bytes 131072 | tf_op jit(solution)/shard_map/all_to_all | solution.py:1394
  64.3 0.0 copy-done.8
  64.3 0.0 copy-done.9
  64.3 0.0 copy-done.10
  64.3 0.0 copy-done.11
  64.3 0.0 copy-done.12
  64.3 0.0 copy-done.13
  64.3 0.0 copy-done.14
  64.4 0.0 copy-done.15
  64.4 0.0 copy-done.16
  64.4 1.1 %adam.1 = (f32[1,3456]{1,0:T(1,128)}, f32[1,3456]{1,0:T(1,128)}, f32[1,3456]{1,0:T(1,128)}, f32[1,1152]{1,0:T(1,128)}, f32[1,1152]{1,0:T(1,128)}, /*index=5*/f32...) custom-call(f32[32,4,128]{2,1,0:T(4,128)S(1)} %all_to_all.10.got_ref, ...), custom_call_target="tpu_custom_call" | custom-call | tf_op jit(solution)/shard_map/adam/pallas_call | solution.py:1230
  (9 shorter events, 0.0 us)
Async XLA Ops:
  2.4 2.0 %collective-permute-start = (bf16[592,384]{1,0:T(8,128)(2,1)S(1)}, bf16[592,384]{1,0:T(8,128)(2,1)S(1)}, u32[]{:S(2)}, u32[]{:S(2)}) collective-permute-start(bf16[592,384]{1,0:T(8,128)(2,1)S(1)} %get-tuple-element.79.refs_3_.refs_1_), channel_id=1, source_target_pairs={{0,1},{1,0},{2,3},{3,2},{4,5},{5,4},{6,7},{7,6},{8,9},{9,8},{10,11... | collective-permute-start | bytes 1363976 | tf_op jit(solution)/shard_map/ppermute | solution.py:1315
  28.9 11.0 %copy-start = (f32[3,192,96]{2,1,0:T(8,128)S(1)}, f32[3,192,96]{2,1,0:T(8,128)}, u32[]{:S(2)}) copy-start(f32[3,192,96]{2,1,0:T(8,128)} %refs_0_.1) | copy-start | bytes 663556
  28.9 11.0 %copy-start.1 = (f32[192,384]{1,0:T(8,128)S(1)}, f32[192,384]{1,0:T(8,128)}, u32[]{:S(2)}) copy-start(f32[192,384]{1,0:T(8,128)} %wid_ref.1) | copy-start | bytes 884740
  28.9 11.0 %copy-start.2 = (f32[384,192]{0,1:T(8,128)S(1)}, f32[384,192]{0,1:T(8,128)}, u32[]{:S(2)}) copy-start(f32[384,192]{0,1:T(8,128)} %param.30) | copy-start | bytes 884740
  28.9 11.0 %copy-start.3 = (f32[96,192]{1,0:T(8,128)S(1)}, f32[96,192]{1,0:T(8,128)}, u32[]{:S(2)}) copy-start(f32[96,192]{1,0:T(8,128)} %out_ref.1) | copy-start | bytes 221188
  28.9 1.9 %collective-permute-start.1 = (bf16[16,112,128]{2,1,0:T(8,128)(2,1)S(1)}, bf16[16,112,128]{2,1,0:T(8,128)(2,1)S(1)}, u32[]{:S(2)}, u32[]{:S(2)}) collective-permute-start(bf16[16,112,128]{2,1,0:T(8,128)(2,1)S(1)} %get-tuple-element.92), channel_id=1, source_target_pairs={{0,1},{1,0},{2,3},{3,2},{4,5},{5,4},{6,7},{7,6},{8,9},{9,8},{10,11... | collective-permute-start | bytes 1376264 | tf_op jit(solution)/shard_map/ppermute | solution.py:1344
  30.8 10.1 %copy-start.4 = (f32[6,192]{1,0:T(8,128)S(1)}, f32[6,192]{1,0:T(8,128)}, u32[]{:S(2)}) copy-start(f32[6,192]{1,0:T(8,128)} %vec_ref.1) | copy-start | bytes 13828
  31.7 22.4 %all-to-all-start = ((bf16[16,112,128]{2,1,0:T(8,128)(2,1)}), bf16[16,112,128]{2,1,0:T(8,128)(2,1)S(1)}, u32[]{:S(2)}, u32[]{:S(2)}) async-start(bf16[16,112,128]{2,1,0:T(8,128)(2,1)} %combine.1), calls=%async_computation | async-start | bytes 917504 | tf_op jit(solution)/shard_map/all_to_all | solution.py:1346
  40.9 23.4 %copy-start.5 = (f32[1,4608]{1,0:T(1,128)S(1)}, f32[1,4608]{1,0:T(1,128)}, u32[]{:S(2)}) copy-start(f32[1,4608]{1,0:T(1,128)} %refs_12_.1) | copy-start | bytes 55300
  40.9 23.4 %copy-start.6 = (f32[1,4608]{1,0:T(1,128)S(1)}, f32[1,4608]{1,0:T(1,128)}, u32[]{:S(2)}) copy-start(f32[1,4608]{1,0:T(1,128)} %refs_13_.1) | copy-start | bytes 55300
  40.9 23.4 %copy-start.7 = (f32[1,4608]{1,0:T(1,128)S(1)}, f32[1,4608]{1,0:T(1,128)}, u32[]{:S(2)}) copy-start(f32[1,4608]{1,0:T(1,128)} %refs_14_.1) | copy-start | bytes 55300
  40.9 23.4 %copy-start.8 = (f32[1,4608]{1,0:T(1,128)S(1)}, f32[1,4608]{1,0:T(1,128)}, u32[]{:S(2)}) copy-start(f32[1,4608]{1,0:T(1,128)} %refs_15_.1) | copy-start | bytes 55300
  40.9 23.4 %copy-start.9 = (f32[1,3456]{1,0:T(1,128)S(1)}, f32[1,3456]{1,0:T(1,128)}, u32[]{:S(2)}) copy-start(f32[1,3456]{1,0:T(1,128)} %refs_8_.3) | copy-start | bytes 41476
  40.9 23.4 %copy-start.10 = (f32[1,3456]{1,0:T(1,128)S(1)}, f32[1,3456]{1,0:T(1,128)}, u32[]{:S(2)}) copy-start(f32[1,3456]{1,0:T(1,128)} %refs_9_.1) | copy-start | bytes 41476
  40.9 23.4 %copy-start.11 = (f32[384]{0:T(512)S(1)}, f32[384]{0:T(512)}, u32[]{:S(2)}) copy-start(f32[384]{0:T(512)} %hb_ref.1) | copy-start | bytes 4612
  40.9 23.4 %copy-start.12 = (f32[6,192]{1,0:T(8,128)S(1)}, f32[6,192]{1,0:T(8,128)}, u32[]{:S(2)}) copy-start(f32[6,192]{1,0:T(8,128)} %refs_16_.1) | copy-start | bytes 13828
  40.9 23.4 %copy-start.13 = (f32[6,192]{1,0:T(8,128)S(1)}, f32[6,192]{1,0:T(8,128)}, u32[]{:S(2)}) copy-start(f32[6,192]{1,0:T(8,128)} %refs_17_.1) | copy-start | bytes 13828
  41.0 23.4 %copy-start.14 = (f32[1,1152]{1,0:T(1,128)S(1)}, f32[1,1152]{1,0:T(1,128)}, u32[]{:S(2)}) copy-start(f32[1,1152]{1,0:T(1,128)} %refs_10_.1) | copy-start | bytes 13828
  41.0 23.4 %copy-start.15 = (f32[1,1152]{1,0:T(1,128)S(1)}, f32[1,1152]{1,0:T(1,128)}, u32[]{:S(2)}) copy-start(f32[1,1152]{1,0:T(1,128)} %refs_11_.1) | copy-start | bytes 13828
  41.0 23.4 %copy-start.16 = (f32[4,2]{0,1:T(2,128)S(1)}, f32[4,2]{0,1:T(2,128)}, u32[]{:S(2)}) copy-start(f32[4,2]{0,1:T(2,128)} %param.33) | copy-start | bytes 100
  41.0 23.4 %copy-start.17 = (f32[384]{0:T(512)S(1)}, f32[384]{0:T(512)}, u32[]{:S(2)}) copy-start(f32[384]{0:T(512)} %refs_18_.1) | copy-start | bytes 4612
  41.0 23.4 %copy-start.18 = (f32[384]{0:T(512)S(1)}, f32[384]{0:T(512)}, u32[]{:S(2)}) copy-start(f32[384]{0:T(512)} %refs_19_.1) | copy-start | bytes 4612
  41.0 23.4 %copy-start.19 = (f32[4,2]{0,1:T(2,128)S(1)}, f32[4,2]{0,1:T(2,128)}, u32[]{:S(2)}) copy-start(f32[4,2]{0,1:T(2,128)} %param.46) | copy-start | bytes 100
  41.0 23.4 %copy-start.20 = (f32[4,2]{0,1:T(2,128)S(1)}, f32[4,2]{0,1:T(2,128)}, u32[]{:S(2)}) copy-start(f32[4,2]{0,1:T(2,128)} %param.47) | copy-start | bytes 100

commit v6 on v5

--- a/solution.py
+++ b/solution.py
@@ -770,6 +770,17 @@
     if data_count:
         wp, np_, op = width // data_count, wide // data_count // 2, half // data_count // 2
     chunking = early_chunks() if data_count else iter(())
+    def leaving_back(first_row, count):
+        for c in range(3):
+            rows = pl.ds(first_row, count)
+            pltpu.make_async_copy(
+                dp_s.at[c, rows], far_refs[3].at[c, rows], sems.at[3]
+            ).start()
+
+    def leaving_places(first, count):
+        span = pl.ds(first, count)
+        pltpu.make_async_copy(place_g.at[span], far_refs[4].at[span], sems.at[4]).start()
+
     for i in range(1, images):
         before = i > 1
         done = i == last
@@ -791,15 +802,20 @@
         interleave(
             back_scores(i, 3),
             back_spread(i, 2),
-            weight_gradient(i - 1, 1) if i <= 2 * blocks else None,
+            weight_gradient(i - 1, 1) if i <= 2 * blocks else triple_gradient(0, 0),
+            triple_gradient(1, 0) if done else None,
+            triple_gradient(2, 0) if done else None,
         )
+        leaving_back((i - 1) * qp, qp)
+        if done:
+            leaving_places(0, heads - 1)
     for unit in range(last, 2 * blocks):
         interleave(weight_gradient(unit, 1))
-    interleave(back_spread(last, 3), *[triple_gradient(c, 0) for c in range(3)])
+    interleave(back_spread(last, 3))
     interleave(products(last, 0), products(last, 1))
     interleave(chunking)
-    for k, source in ((3, dp_s), (4, place_g)):
-        pltpu.make_async_copy(source, far_refs[k], sems.at[k]).start()
+    leaving_back(last * qp, qp)
+    leaving_places(heads - 1, 1)
     gate_ref[...] = gate_g[...]
     hp_ref[...] = hp_s[...]
     for c in range(3):

time: 65.9 us -> 64.4 us (0.977)
  Pallas kernels: 38 us -> 36.4 us
    pallas_call x1, Pallas kernels: 24.5 us -> 23 us  [run_layer(): pl.pallas_call(functools.partial(layer_kernel, patches=patches, heads=hea...]
where the time goes in v6:
time: 64.4 us; the launch traced here: 64.1 us
  Pallas kernels  36.4 us (57%)
  blocking collectives  9.96 us (15%)
  starting transfers between devices  9.16 us (14%)
  waiting for transfers between devices  7.24 us (11%)
  between operations  1.18 us (2%)
    pallas_call x1, Pallas kernels, run_layer(): pl.pallas_call(functools.partial(layer_kernel, patches=patches, heads=hea...  23 us
    all_to_all x1, blocking collectives, on_device(): last_got = lax.all_to_all(payload, ('dp', 'tensor'), 0, 0, tiled=False)  9.96 us
    all_to_all x1, starting transfers between devices, on_device(): got = lax.all_to_all(chunks, 'dp', 0, 0, tiled=False)  8.21 us
    pallas_call x1, Pallas kernels, run_finish(): pl.pallas_call(functools.partial(finish_kernel, patches=patches, heads=pl...  7.79 us
    all_to_all x1, waiting for transfers between devices, on_device(): got = lax.all_to_all(chunks, 'dp', 0, 0, tiled=False)  5.25 us
    pallas_call x1, Pallas kernels, run_pack(): pl.pallas_call(pack_kernel, out_shape=(pltpu.VMEM((3 * depth + 16, wide),...  1.71 us
    ppermute x1, waiting for transfers between devices, on_device(): received = lax.ppermute(theirs, 'tensor', swap)  1.45 us
  transfers between devices with their start and end apart: 3, of which 3 were waited for; matrix products, arithmetic and copies ran while one was open for 0% of the time, Pallas kernels for 15%

profile of v6, /device:TPU:0, one launch (start us, length us, event | category | flops | bytes accessed | tf_op | source)
XLA Modules:
  0.0 64.1 jit_solution(17528637748519136463)
XLA Ops:
  0.7 1.7 %pack_weights.1 = (bf16[592,384]{1,0:T(8,128)(2,1)S(1)}, bf16[192,1568]{1,0:T(8,128)(2,1)S(1)}, bf16[192,1568]{1,0:T(8,128)(2,1)S(1)}, s32[16,196]{1,0:T(8,128)S(1)}) custom-call(f32[3,192,96]{2,1,0:T(8,128)} %refs_0_.1, f32[96,192]{1,0:T(8,128)} %out_ref.1, f32[192,384]{1,0:T(8,128)} %wid_ref.1, f32[192,384]{1,0:T(8,128)} %bitcast.14, f32[384]{0:T(512)} %hb_ref.1, ...), custom_call_target="tpu_custom_call" | custom-call | tf_op jit(solution)/shard_map/pack_weights/pallas_call | solution.py:241
  2.4 0.5 collective-permute-start
  2.9 0.9 %prepare.1 = (bf16[8,208,192]{2,1,0:T(8,128)(2,1)S(1)}, bf16[8,208,192]{2,1,0:T(8,128)(2,1)S(1)}, bf16[8,208,128]{2,1,0:T(8,128)(2,1)S(1)}) custom-call(bf16[192,1568]{1,0:T(8,128)(2,1)S(1)} %get-tuple-element.75.tok_ref, bf16[192,1568]{1,0:T(8,128)(2,1)S(1)} %get-tuple-element.76.cot_ref, s32[16,196]{1,0:T(8,128)S(1)} %get-tuple-element.77.keep_ref), custom_call_target="tpu_custom_call" | custom-call | tf_op jit(solution)/shard_map/prepare/pallas_call | solution.py:283
  3.8 0.5 collective-permute-done.refs_4_.refs_2_
  4.3 23.0 %layer.1 = (bf16[2048,768]{1,0:T(8,128)(2,1)}, f32[8,208,192]{2,1,0:T(8,128)}, f32[8,208,192]{2,1,0:T(8,128)}, bf16[3,2048,256]{2,1,0:T(8,128)(2,1)}, f32[4,208,...) custom-call(bf16[8,208,192]{2,1,0:T(8,128)(2,1)S(1)} %get-tuple-elem, ...), custom_call_target="tpu_custom_call" | custom-call | tf_op jit(solution)/shard_map/layer/pallas_call | solution.py:917
  27.3 0.0 copy-start
  27.3 0.0 copy-start.1
  27.3 0.0 copy-start.2
  27.4 0.0 copy-start.3
  27.4 0.4 collective-permute-start.1
  27.8 1.4 %collective-permute-done.1.got_ref = bf16[16,112,128]{2,1,0:T(8,128)(2,1)S(1)} collective-permute-done((bf16[16,112,128]{2,1,0:T(8,128)(2,1)S(1)}, bf16[16,112,128]{2,1,0:T(8,128)(2,1)S(1)}, u32[]{:S(2)}, u32[]{:S(2)}) %collective-permute-start.1) | collective-permute-done | bytes 458784 | tf_op jit(solution)/shard_map/ppermute | solution.py:1360
  29.3 0.9 %combine.1 = bf16[16,112,128]{2,1,0:T(8,128)(2,1)} custom-call(f32[16,112,128]{2,1,0:T(8,128)S(1)} %get-tuple-element.91.own_ref, bf16[16,112,128]{2,1,0:T(8,128)(2,1)S(1)} %collective-permute-done.1.got_ref), custom_call_target="tpu_custom_call" | custom-call | tf_op jit(solution)/shard_map/combine/pallas_call | solution.py:1024
  30.1 8.2 %all-to-all-start = ((bf16[16,112,128]{2,1,0:T(8,128)(2,1)}), bf16[16,112,128]{2,1,0:T(8,128)(2,1)S(1)}, u32[]{:S(2)}, u32[]{:S(2)}) async-start(bf16[16,112,128]{2,1,0:T(8,128)(2,1)} %combine.1), calls=%async_computation | async-start | bytes 917504 | tf_op jit(solution)/shard_map/all_to_all | solution.py:1362
  38.4 0.0 copy-done
  38.4 0.0 copy-done.1
  38.4 0.0 copy-done.2
  38.4 0.0 copy-done.3
  38.4 0.9 %weight_shares.1 = (f32[1,3456]{1,0:T(1,128)S(1)}, f32[1,1152]{1,0:T(1,128)S(1)}, f32[1,4608]{1,0:T(1,128)S(1)}, f32[1,4608]{1,0:T(1,128)S(1)}) custom-call(f32[8,256]{1,0:T(8,128)S(1)} %get-tuple-element.82.refs_4_._, f32[576,96]{1,0:T(8,128)S(1)} %bitcast.13, f32[96,192]{1,0:T(8,128)S(1)} %copy-done.3, f32[192,384]{1,0:T(8,128)S(1)} %copy-done.1, ...), custom_call_target="tpu_custom_call" | custom-call | tf_op jit(solution)/shard_map/weight_shares/pallas_call | solution.py:1077
  39.3 0.0 copy-start.5
  39.3 0.0 copy-start.6
  39.3 0.0 copy-start.7
  39.3 0.0 copy-start.8
  39.3 0.0 copy-start.9
  39.4 0.0 copy-start.10
  39.4 0.0 copy-start.11
  39.4 0.0 copy-start.12
  39.4 0.0 copy-start.13
  39.4 0.0 copy-start.14
  39.4 0.0 copy-start.15
  39.4 0.0 copy-start.16
  39.4 0.0 copy-start.17
  39.5 0.0 copy-start.18
  39.5 0.0 copy-start.19
  39.5 0.0 copy-start.20
  39.5 7.8 %finish.1 = (f32[192,1568]{1,0:T(8,128)}, f32[192,1568]{1,0:T(8,128)}, f32[2,192]{1,0:T(2,128)S(1)}, f32[1,128]{1,0:T(1,128)S(1)}) custom-call(bf16[8,208,192]{2,1,0:T(8,128)(2,1)S(1)} %get-tuple-element.78.refs_0_, bf16[592,384]{1,0:T(8,128)(2,1)S(1)} %get-tuple-element.79.refs_3_.refs_1_, bf16[592,384]{1,0:T(8,128)(2,1)S(1)} %collective-permute-done.refs_4_.refs_2_, ...), custom_call_target="tpu_custom_call" | custom-call | tf_op jit(solution)/shard_map/finish/pallas_call | solution.py:1001
  47.3 5.3 %all-to-all-done.got_ref = bf16[16,112,128]{2,1,0:T(8,128)(2,1)S(1)} async-done(((bf16[16,112,128]{2,1,0:T(8,128)(2,1)}), bf16[16,112,128]{2,1,0:T(8,128)(2,1)S(1)}, u32[]{:S(2)}, u32[]{:S(2)}) %all-to-all-start) | async-done | bytes 458784 | tf_op jit(solution)/shard_map/all_to_all | solution.py:1362
  52.5 0.2 sums.1
  52.8 10.0 %all_to_all.10.got_ref = f32[32,4,128]{2,1,0:T(4,128)S(1)} all-to-all(f32[32,4,128]{2,1,0:T(4,128)S(1)} %get-tuple-element.96), channel_id=1, replica_groups=mesh['dp'=16,'tensor'=2] {'dp','tensor'}, dimensions={0} | all-to-all | bytes 131072 | tf_op jit(solution)/shard_map/all_to_all | solution.py:1410
  62.7 0.0 copy-done.8
  62.8 0.0 copy-done.9
  62.8 0.0 copy-done.10
  62.8 0.0 copy-done.11
  62.8 0.0 copy-done.12
  62.8 0.0 copy-done.13
  62.8 0.0 copy-done.14
  62.8 0.0 copy-done.15
  62.8 0.0 copy-done.16
  62.9 1.1 %adam.1 = (f32[1,3456]{1,0:T(1,128)}, f32[1,3456]{1,0:T(1,128)}, f32[1,3456]{1,0:T(1,128)}, f32[1,1152]{1,0:T(1,128)}, f32[1,1152]{1,0:T(1,128)}, /*index=5*/f32...) custom-call(f32[32,4,128]{2,1,0:T(4,128)S(1)} %all_to_all.10.got_ref, ...), custom_call_target="tpu_custom_call" | custom-call | tf_op jit(solution)/shard_map/adam/pallas_call | solution.py:1246
  (9 shorter events, 0.0 us)
Async XLA Ops:
  2.4 2.0 %collective-permute-start = (bf16[592,384]{1,0:T(8,128)(2,1)S(1)}, bf16[592,384]{1,0:T(8,128)(2,1)S(1)}, u32[]{:S(2)}, u32[]{:S(2)}) collective-permute-start(bf16[592,384]{1,0:T(8,128)(2,1)S(1)} %get-tuple-element.79.refs_3_.refs_1_), channel_id=1, source_target_pairs={{0,1},{1,0},{2,3},{3,2},{4,5},{5,4},{6,7},{7,6},{8,9},{9,8},{10,11... | collective-permute-start | bytes 1363976 | tf_op jit(solution)/shard_map/ppermute | solution.py:1331
  27.3 11.0 %copy-start = (f32[3,192,96]{2,1,0:T(8,128)S(1)}, f32[3,192,96]{2,1,0:T(8,128)}, u32[]{:S(2)}) copy-start(f32[3,192,96]{2,1,0:T(8,128)} %refs_0_.1) | copy-start | bytes 663556
  27.3 11.0 %copy-start.1 = (f32[192,384]{1,0:T(8,128)S(1)}, f32[192,384]{1,0:T(8,128)}, u32[]{:S(2)}) copy-start(f32[192,384]{1,0:T(8,128)} %wid_ref.1) | copy-start | bytes 884740
  27.3 11.0 %copy-start.2 = (f32[384,192]{0,1:T(8,128)S(1)}, f32[384,192]{0,1:T(8,128)}, u32[]{:S(2)}) copy-start(f32[384,192]{0,1:T(8,128)} %param.30) | copy-start | bytes 884740
  27.4 11.0 %copy-start.3 = (f32[96,192]{1,0:T(8,128)S(1)}, f32[96,192]{1,0:T(8,128)}, u32[]{:S(2)}) copy-start(f32[96,192]{1,0:T(8,128)} %out_ref.1) | copy-start | bytes 221188
  27.4 1.9 %collective-permute-start.1 = (bf16[16,112,128]{2,1,0:T(8,128)(2,1)S(1)}, bf16[16,112,128]{2,1,0:T(8,128)(2,1)S(1)}, u32[]{:S(2)}, u32[]{:S(2)}) collective-permute-start(bf16[16,112,128]{2,1,0:T(8,128)(2,1)S(1)} %get-tuple-element.92), channel_id=1, source_target_pairs={{0,1},{1,0},{2,3},{3,2},{4,5},{5,4},{6,7},{7,6},{8,9},{9,8},{10,11... | collective-permute-start | bytes 1376264 | tf_op jit(solution)/shard_map/ppermute | solution.py:1360
  29.3 10.0 %copy-start.4 = (f32[6,192]{1,0:T(8,128)S(1)}, f32[6,192]{1,0:T(8,128)}, u32[]{:S(2)}) copy-start(f32[6,192]{1,0:T(8,128)} %vec_ref.1) | copy-start | bytes 13828
  30.1 22.4 %all-to-all-start = ((bf16[16,112,128]{2,1,0:T(8,128)(2,1)}), bf16[16,112,128]{2,1,0:T(8,128)(2,1)S(1)}, u32[]{:S(2)}, u32[]{:S(2)}) async-start(bf16[16,112,128]{2,1,0:T(8,128)(2,1)} %combine.1), calls=%async_computation | async-start | bytes 917504 | tf_op jit(solution)/shard_map/all_to_all | solution.py:1362
  39.3 23.4 %copy-start.5 = (f32[1,4608]{1,0:T(1,128)S(1)}, f32[1,4608]{1,0:T(1,128)}, u32[]{:S(2)}) copy-start(f32[1,4608]{1,0:T(1,128)} %refs_12_.1) | copy-start | bytes 55300
  39.3 23.4 %copy-start.6 = (f32[1,4608]{1,0:T(1,128)S(1)}, f32[1,4608]{1,0:T(1,128)}, u32[]{:S(2)}) copy-start(f32[1,4608]{1,0:T(1,128)} %refs_13_.1) | copy-start | bytes 55300
  39.3 23.4 %copy-start.7 = (f32[1,4608]{1,0:T(1,128)S(1)}, f32[1,4608]{1,0:T(1,128)}, u32[]{:S(2)}) copy-start(f32[1,4608]{1,0:T(1,128)} %refs_14_.1) | copy-start | bytes 55300
  39.3 23.4 %copy-start.8 = (f32[1,4608]{1,0:T(1,128)S(1)}, f32[1,4608]{1,0:T(1,128)}, u32[]{:S(2)}) copy-start(f32[1,4608]{1,0:T(1,128)} %refs_15_.1) | copy-start | bytes 55300
  39.3 23.4 %copy-start.9 = (f32[1,3456]{1,0:T(1,128)S(1)}, f32[1,3456]{1,0:T(1,128)}, u32[]{:S(2)}) copy-start(f32[1,3456]{1,0:T(1,128)} %refs_8_.3) | copy-start | bytes 41476
  39.4 23.4 %copy-start.10 = (f32[1,3456]{1,0:T(1,128)S(1)}, f32[1,3456]{1,0:T(1,128)}, u32[]{:S(2)}) copy-start(f32[1,3456]{1,0:T(1,128)} %refs_9_.1) | copy-start | bytes 41476
  39.4 23.4 %copy-start.11 = (f32[384]{0:T(512)S(1)}, f32[384]{0:T(512)}, u32[]{:S(2)}) copy-start(f32[384]{0:T(512)} %hb_ref.1) | copy-start | bytes 4612
  39.4 23.4 %copy-start.12 = (f32[6,192]{1,0:T(8,128)S(1)}, f32[6,192]{1,0:T(8,128)}, u32[]{:S(2)}) copy-start(f32[6,192]{1,0:T(8,128)} %refs_16_.1) | copy-start | bytes 13828
  39.4 23.4 %copy-start.13 = (f32[6,192]{1,0:T(8,128)S(1)}, f32[6,192]{1,0:T(8,128)}, u32[]{:S(2)}) copy-start(f32[6,192]{1,0:T(8,128)} %refs_17_.1) | copy-start | bytes 13828
  39.4 23.4 %copy-start.14 = (f32[1,1152]{1,0:T(1,128)S(1)}, f32[1,1152]{1,0:T(1,128)}, u32[]{:S(2)}) copy-start(f32[1,1152]{1,0:T(1,128)} %refs_10_.1) | copy-start | bytes 13828
  39.4 23.4 %copy-start.15 = (f32[1,1152]{1,0:T(1,128)S(1)}, f32[1,1152]{1,0:T(1,128)}, u32[]{:S(2)}) copy-start(f32[1,1152]{1,0:T(1,128)} %refs_11_.1) | copy-start | bytes 13828
  39.4 23.4 %copy-start.16 = (f32[4,2]{0,1:T(2,128)S(1)}, f32[4,2]{0,1:T(2,128)}, u32[]{:S(2)}) copy-start(f32[4,2]{0,1:T(2,128)} %param.33) | copy-start | bytes 100
  39.4 23.4 %copy-start.17 = (f32[384]{0:T(512)S(1)}, f32[384]{0:T(512)}, u32[]{:S(2)}) copy-start(f32[384]{0:T(512)} %refs_18_.1) | copy-start | bytes 4612
  39.5 23.4 %copy-start.18 = (f32[384]{0:T(512)S(1)}, f32[384]{0:T(512)}, u32[]{:S(2)}) copy-start(f32[384]{0:T(512)} %refs_19_.1) | copy-start | bytes 4612
  39.5 23.4 %copy-start.19 = (f32[4,2]{0,1:T(2,128)S(1)}, f32[4,2]{0,1:T(2,128)}, u32[]{:S(2)}) copy-start(f32[4,2]{0,1:T(2,128)} %param.46) | copy-start | bytes 100
  39.5 23.4 %copy-start.20 = (f32[4,2]{0,1:T(2,128)S(1)}, f32[4,2]{0,1:T(2,128)}, u32[]{:S(2)}) copy-start(f32[4,2]{0,1:T(2,128)} %param.47) | copy-start | bytes 100

commit v7 on v6

--- a/solution.py
+++ b/solution.py
@@ -180,9 +180,9 @@
 
 
 def put_planes(ref, value):
-    width = value.shape[1]
-    ref[0] = value[:, :128]
-    ref[1, :, 0 : width - 128] = value[:, 128:]
+    rows, width = value.shape
+    ref[0, 0:rows, :] = value[:, :128]
+    ref[1, 0:rows, 0 : width - 128] = value[:, 128:]
 
 
 def even_odd_tiles(ref, start, pairs):
@@ -665,9 +665,9 @@
         value = nn(left_t[side, :, spans[part]], right_s[side, spans[part], lanes])
         yield
         if part:
-            wide_g[side, :, lanes] += value
+            wide_g[side, 0:width, lanes] += value
         else:
-            wide_g[side, :, lanes] = value
+            wide_g[side, 0:width, lanes] = value
 
     def outward_gradient(part):
         value = nn(mix_t[:, spans[part]], low_s[spans[part], :])
@@ -712,18 +712,18 @@
 
 
     def early_chunks():
-        put_planes(nar_p, wide_g[0].T)
+        put_planes(nar_p, wide_g[0, 0:width, :].T)
         put_planes(out_p, out_g[...])
         for side in range(2):
             for k, part in enumerate(even_odd_tiles(nar_p, side * wide, wide // 2)):
-                nar_f[side, k] = part
+                nar_f[side, k, 0 : wide // 2, :] = part
             for k, part in enumerate(even_odd_tiles(out_p, side * half, half // 2)):
-                out_f[side, k] = part
+                out_f[side, k, 0 : half // 2, :] = part
             yield
         for r in range(data_count):
             for side in range(2):
                 yield
-                piece = outs[0].at[r] if side == 0 else tmp.at[r]
+                piece = tmp.at[side, r]
                 for k in range(3):
                     lanes = slice(side * wide + 128 * k, side * wide + 128 * (k + 1))
                     piece[k * wp : (k + 1) * wp, :] = wide_g[1, r * wp : (r + 1) * wp, lanes]
@@ -731,8 +731,7 @@
                     piece[row : row + np_, :] = nar_f[side, k, r * np_ : (r + 1) * np_, :]
                     row = 3 * (wp + np_) + k * op
                     piece[row : row + op, :] = out_f[side, k, r * op : (r + 1) * op, :]
-                if side:
-                    outs[1][r, 0:SENT_EARLY, :] = piece[0:SENT_EARLY, :].astype(BF)
+                outs[side][r, 0:SENT_EARLY, :] = piece[0:SENT_EARLY, :].astype(outs[side].dtype)
 
     def late_chunks():
         early = jnp.sum(vec_g[...], axis=1)
@@ -743,12 +742,12 @@
         small_at = 3 * (wp + np_ + op)
         for side in range(2):
             for k, part in enumerate(four_row_tiles(tri_p, side, 0, 3 * width // 4)):
-                tri_f[side, k] = part
+                tri_f[side, k, 0 : 3 * width // 4, :] = part
             yield
         for r in range(data_count):
             for side in range(2):
                 yield
-                piece = outs[0].at[r] if side == 0 else tmp.at[r]
+                piece = tmp.at[side, r]
                 row, lane = divmod(r * vec_n, width)
                 at_hidden = side * wide + r * hid_n
                 piece[small_at : small_at + 1, :] = jnp.concatenate(
@@ -764,8 +763,9 @@
                     piece[row : row + groups, :] = tri_f[side, k, r * groups : (r + 1) * groups, :]
                 row = small_at + 1 + 3 * groups
                 piece[row:SENT_ROWS, :] = jnp.zeros((SENT_ROWS - row, 128), F32)
-                if side:
-                    outs[1][r, SENT_EARLY:, :] = piece[SENT_EARLY:, :].astype(BF)
+                outs[side][r, SENT_EARLY:, :] = piece[SENT_EARLY:SENT_ROWS, :].astype(
+                    outs[side].dtype
+                )
 
     if data_count:
         wp, np_, op = width // data_count, wide // data_count // 2, half // data_count // 2
@@ -823,8 +823,8 @@
     if data_count:
         interleave(late_chunks())
     else:
-        outs[0][...] = wide_g[0].T
-        outs[1][...] = wide_g[1]
+        outs[0][...] = wide_g[0, 0:width, :].T
+        outs[1][...] = wide_g[1, 0:width, :]
         outs[2][...] = out_g[...]
         outs[3][...] = vec_g[...]
         outs[4][...] = hid_g[...]
@@ -903,7 +903,7 @@
         f32(2, kp, qp),
         bf(kp, heads * qp),
         bf(kp, heads * qp),
-        f32(2, width, hidden),
+        f32(2, width + 8, hidden),
         f32(width, width),
         f32(4, 8, width),
         f32(8, hidden),
@@ -912,8 +912,8 @@
     ]
     if data_count:
         scratch += [f32(2, hidden, 128), f32(2, width, 128)]
-        scratch += [f32(2, 3, wide // 2, 128), f32(2, 3, half // 2, 128)]
-        scratch += [f32(2, 3, 3 * width // 4, 128), f32(data_count, SENT_ROWS, 128)]
+        scratch += [f32(2, 3, wide // 2 + 8, 128), f32(2, 3, half // 2 + 8, 128)]
+        scratch += [f32(2, 3, 3 * width // 4 + 8, 128), f32(2, data_count, SENT_ROWS + 8, 128)]
     return pl.pallas_call(
         functools.partial(layer_kernel, patches=patches, heads=heads, data_count=data_count),
         out_shape=(
@@ -965,7 +965,7 @@
     for i in range(images):
         rows = mid_s[i] + nt(act_s[i * qp : i * qp + kp, :], wn[...]) + shift
         rows_s[i * patches : (i + 1) * patches, :] = rows[0:patches]
-    res_out[...] = rows_s[...].T
+    res_out[...] = rows_s[0 : images * patches, :].T
     for member in copies[2:]:
         member.wait()
     for i in range(images):
@@ -975,7 +975,7 @@
         vec_g[1] += fold(g)
         rows = gm_s[i] + norm_back(g * gain, n1, spread)
         rows_s[i * patches : (i + 1) * patches, :] = rows[0:patches]
-    gi_out[...] = rows_s[...].T
+    gi_out[...] = rows_s[0 : images * patches, :].T
     vec_out[...] = jnp.sum(vec_g[...], axis=1)
     parts = offsets(kp, qp)
     rank = lax.axis_index("tensor")
@@ -1008,7 +1008,7 @@
             pltpu.VMEM((3, width, 256), BF),
             pltpu.VMEM((width, 2 * own.shape[1]), BF),
             pltpu.VMEM((2, 8, width), F32),
-            pltpu.VMEM((rows, width), F32),
+            pltpu.VMEM((rows + 8, width), F32),
             pltpu.SemaphoreType.DMA((5,)),
         ],
         compiler_params=pltpu.CompilerParams(vmem_limit_bytes=32 * 1024 * 1024),
@@ -1052,9 +1052,11 @@
     wp, np_, op = width // data_count, wide // data_count // 2, half // data_count // 2
     data_rank = lax.axis_index("dp")
     groups = tri_ref.shape[0] // data_count // 4
-    st[0, :, 0 : tri_ref.shape[1]] = pick_rows(tri_ref, data_rank * 4 * groups, 4 * groups)
+    st[0, 0 : 4 * groups, 0 : tri_ref.shape[1]] = pick_rows(
+        tri_ref, data_rank * 4 * groups, 4 * groups
+    )
     put_planes(so, pick_rows(out_ref, data_rank * 2 * op, 2 * op))
-    sw[...] = pick_rows(wid_ref, data_rank * wp, wp)
+    sw[0:wp, :] = pick_rows(wid_ref, data_rank * wp, wp)
     put_planes(sn, pick_rows(nar_ref, data_rank * 2 * np_, 2 * np_, flip=True))
     tiles = four_row_tiles(st, 0, 0, groups)
     for p in range(groups):
@@ -1080,10 +1082,10 @@
         in_specs=[VM] * 5,
         out_specs=(VM,) * 4,
         scratch_shapes=[
-            pltpu.VMEM((1, share[0], 128), F32),
-            pltpu.VMEM((2, share[1], 128), F32),
-            pltpu.VMEM((share[2], wide), F32),
-            pltpu.VMEM((2, wide // data_count, 128), F32),
+            pltpu.VMEM((1, share[0] + 40, 128), F32),
+            pltpu.VMEM((2, share[1] + 18, 128), F32),
+            pltpu.VMEM((share[2] + 12, wide), F32),
+            pltpu.VMEM((2, wide // data_count + 16, 128), F32),
         ],
         compiler_params=PARAMS,
         name="weight_shares",
@@ -1102,7 +1104,7 @@
     (tri_f, out_f, wid_f, nar_f, pay_ref, tot) = refs
     tri_b, out_b, wid_b, nar_b = blocks
     vec_n, hid_n = span
-    tot[...] = jnp.sum(got_ref[...].astype(F32), axis=0)
+    tot[0:SENT_ROWS, :] = jnp.sum(got_ref[...].astype(F32), axis=0)
     spread_rows(wid_f, tot, 0, wid_b)
     spread_rows(nar_f, tot, 3 * wid_b, nar_b)
     spread_rows(out_f, tot, 3 * (wid_b + nar_b), out_b)
@@ -1132,7 +1134,7 @@
         ),
         in_specs=[VM] * 4,
         out_specs=(VM,) * 5,
-        scratch_shapes=[pltpu.VMEM((SENT_ROWS, 128), F32)],
+        scratch_shapes=[pltpu.VMEM((SENT_ROWS + 8, 128), F32)],
         compiler_params=PARAMS,
         name="sums",
     )(got, late_vec, head, after)

time: 64.4 us -> 64.6 us (level)
  no operation moved by 1% of the time
where the time goes in v7:
time: 64.6 us; the launch traced here: 64.3 us
  Pallas kernels  36.7 us (57%)
  blocking collectives  9.96 us (15%)
  starting transfers between devices  9.19 us (14%)
  waiting for transfers between devices  7.21 us (11%)
  between operations  1.18 us (2%)
    pallas_call x1, Pallas kernels, run_layer(): pl.pallas_call(functools.partial(layer_kernel, patches=patches, heads=hea...  23.2 us
    all_to_all x1, blocking collectives, on_device(): last_got = lax.all_to_all(payload, ('dp', 'tensor'), 0, 0, tiled=False)  9.96 us
    all_to_all x1, starting transfers between devices, on_device(): got = lax.all_to_all(chunks, 'dp', 0, 0, tiled=False)  8.24 us
    pallas_call x1, Pallas kernels, run_finish(): pl.pallas_call(functools.partial(finish_kernel, patches=patches, heads=pl...  7.79 us
    all_to_all x1, waiting for transfers between devices, on_device(): got = lax.all_to_all(chunks, 'dp', 0, 0, tiled=False)  5.22 us
    pallas_call x1, Pallas kernels, run_pack(): pl.pallas_call(pack_kernel, out_shape=(pltpu.VMEM((3 * depth + 16, wide),...  1.71 us
    ppermute x1, waiting for transfers between devices, on_device(): received = lax.ppermute(theirs, 'tensor', swap)  1.44 us
  transfers between devices with their start and end apart: 3, of which 3 were waited for; matrix products, arithmetic and copies ran while one was open for 0% of the time, Pallas kernels for 15%

profile of v7, /device:TPU:0, one launch (start us, length us, event | category | flops | bytes accessed | tf_op | source)
XLA Modules:
  0.0 64.3 jit_solution(8456164816264946359)
XLA Ops:
  0.7 1.7 %pack_weights.1 = (bf16[592,384]{1,0:T(8,128)(2,1)S(1)}, bf16[192,1568]{1,0:T(8,128)(2,1)S(1)}, bf16[192,1568]{1,0:T(8,128)(2,1)S(1)}, s32[16,196]{1,0:T(8,128)S(1)}) custom-call(f32[3,192,96]{2,1,0:T(8,128)} %refs_0_.1, f32[96,192]{1,0:T(8,128)} %out_ref.1, f32[192,384]{1,0:T(8,128)} %wid_ref.1, f32[192,384]{1,0:T(8,128)} %bitcast.14, f32[384]{0:T(512)} %hb_ref.1, ...), custom_call_target="tpu_custom_call" | custom-call | tf_op jit(solution)/shard_map/pack_weights/pallas_call | solution.py:241
  2.4 0.5 collective-permute-start
  2.9 0.9 %prepare.1 = (bf16[8,208,192]{2,1,0:T(8,128)(2,1)S(1)}, bf16[8,208,192]{2,1,0:T(8,128)(2,1)S(1)}, bf16[8,208,128]{2,1,0:T(8,128)(2,1)S(1)}) custom-call(bf16[192,1568]{1,0:T(8,128)(2,1)S(1)} %get-tuple-element.75.tok_ref, bf16[192,1568]{1,0:T(8,128)(2,1)S(1)} %get-tuple-element.76.cot_ref, s32[16,196]{1,0:T(8,128)S(1)} %get-tuple-element.77.keep_ref), custom_call_target="tpu_custom_call" | custom-call | tf_op jit(solution)/shard_map/prepare/pallas_call | solution.py:283
  3.8 0.5 collective-permute-done.refs_4_.refs_2_
  4.3 23.2 %layer.1 = (bf16[2048,768]{1,0:T(8,128)(2,1)}, f32[8,208,192]{2,1,0:T(8,128)}, f32[8,208,192]{2,1,0:T(8,128)}, bf16[3,2048,256]{2,1,0:T(8,128)(2,1)}, f32[4,208,...) custom-call(bf16[8,208,192]{2,1,0:T(8,128)(2,1)S(1)} %get-tuple-elem, ...), custom_call_target="tpu_custom_call" | custom-call | tf_op jit(solution)/shard_map/layer/pallas_call | solution.py:917
  27.6 0.0 copy-start
  27.6 0.0 copy-start.1
  27.6 0.0 copy-start.2
  27.6 0.0 copy-start.3
  27.6 0.4 collective-permute-start.1
  28.0 1.4 %collective-permute-done.1.got_ref = bf16[16,112,128]{2,1,0:T(8,128)(2,1)S(1)} collective-permute-done((bf16[16,112,128]{2,1,0:T(8,128)(2,1)S(1)}, bf16[16,112,128]{2,1,0:T(8,128)(2,1)S(1)}, u32[]{:S(2)}, u32[]{:S(2)}) %collective-permute-start.1) | collective-permute-done | bytes 458784 | tf_op jit(solution)/shard_map/ppermute | solution.py:1362
  29.5 0.9 %combine.1 = bf16[16,112,128]{2,1,0:T(8,128)(2,1)} custom-call(f32[16,112,128]{2,1,0:T(8,128)S(1)} %get-tuple-element.91.own_ref, bf16[16,112,128]{2,1,0:T(8,128)(2,1)S(1)} %collective-permute-done.1.got_ref), custom_call_target="tpu_custom_call" | custom-call | tf_op jit(solution)/shard_map/combine/pallas_call | solution.py:1024
  30.4 8.2 %all-to-all-start = ((bf16[16,112,128]{2,1,0:T(8,128)(2,1)}), bf16[16,112,128]{2,1,0:T(8,128)(2,1)S(1)}, u32[]{:S(2)}, u32[]{:S(2)}) async-start(bf16[16,112,128]{2,1,0:T(8,128)(2,1)} %combine.1), calls=%async_computation | async-start | bytes 917504 | tf_op jit(solution)/shard_map/all_to_all | solution.py:1364
  38.6 0.0 copy-done
  38.6 0.0 copy-done.1
  38.6 0.0 copy-done.2
  38.6 0.0 copy-done.3
  38.7 0.9 %weight_shares.1 = (f32[1,3456]{1,0:T(1,128)S(1)}, f32[1,1152]{1,0:T(1,128)S(1)}, f32[1,4608]{1,0:T(1,128)S(1)}, f32[1,4608]{1,0:T(1,128)S(1)}) custom-call(f32[8,256]{1,0:T(8,128)S(1)} %get-tuple-element.82.refs_4_._, f32[576,96]{1,0:T(8,128)S(1)} %bitcast.13, f32[96,192]{1,0:T(8,128)S(1)} %copy-done.3, f32[192,384]{1,0:T(8,128)S(1)} %copy-done.1, ...), custom_call_target="tpu_custom_call" | custom-call | tf_op jit(solution)/shard_map/weight_shares/pallas_call | solution.py:1079
  39.5 0.0 copy-done.4
  39.6 0.0 copy-start.5
  39.6 0.0 copy-start.6
  39.6 0.0 copy-start.7
  39.6 0.0 copy-start.8
  39.6 0.0 copy-start.9
  39.6 0.0 copy-start.10
  39.6 0.0 copy-start.11
  39.6 0.0 copy-start.12
  39.7 0.0 copy-start.13
  39.7 0.0 copy-start.14
  39.7 0.0 copy-start.15
  39.7 0.0 copy-start.16
  39.7 0.0 copy-start.17
  39.7 0.0 copy-start.18
  39.7 0.0 copy-start.19
  39.7 0.0 copy-start.20
  39.8 7.8 %finish.1 = (f32[192,1568]{1,0:T(8,128)}, f32[192,1568]{1,0:T(8,128)}, f32[2,192]{1,0:T(2,128)S(1)}, f32[1,128]{1,0:T(1,128)S(1)}) custom-call(bf16[8,208,192]{2,1,0:T(8,128)(2,1)S(1)} %get-tuple-element.78.refs_0_, bf16[592,384]{1,0:T(8,128)(2,1)S(1)} %get-tuple-element.79.refs_3_.refs_1_, bf16[592,384]{1,0:T(8,128)(2,1)S(1)} %collective-permute-done.refs_4_.refs_2_, ...), custom_call_target="tpu_custom_call" | custom-call | tf_op jit(solution)/shard_map/finish/pallas_call | solution.py:1001
  47.6 5.2 %all-to-all-done.got_ref = bf16[16,112,128]{2,1,0:T(8,128)(2,1)S(1)} async-done(((bf16[16,112,128]{2,1,0:T(8,128)(2,1)}), bf16[16,112,128]{2,1,0:T(8,128)(2,1)S(1)}, u32[]{:S(2)}, u32[]{:S(2)}) %all-to-all-start) | async-done | bytes 458784 | tf_op jit(solution)/shard_map/all_to_all | solution.py:1364
  52.8 0.2 sums.1
  53.0 10.0 %all_to_all.10.got_ref = f32[32,4,128]{2,1,0:T(4,128)S(1)} all-to-all(f32[32,4,128]{2,1,0:T(4,128)S(1)} %get-tuple-element.96), channel_id=1, replica_groups=mesh['dp'=16,'tensor'=2] {'dp','tensor'}, dimensions={0} | all-to-all | bytes 131072 | tf_op jit(solution)/shard_map/all_to_all | solution.py:1412
  63.0 0.0 copy-done.5
  63.0 0.0 copy-done.6
  63.0 0.0 copy-done.7
  63.0 0.0 copy-done.8
  63.0 0.0 copy-done.9
  63.0 0.0 copy-done.10
  63.0 0.0 copy-done.11
  63.0 0.0 copy-done.12
  63.1 1.1 %adam.1 = (f32[1,3456]{1,0:T(1,128)}, f32[1,3456]{1,0:T(1,128)}, f32[1,3456]{1,0:T(1,128)}, f32[1,1152]{1,0:T(1,128)}, f32[1,1152]{1,0:T(1,128)}, /*index=5*/f32...) custom-call(f32[32,4,128]{2,1,0:T(4,128)S(1)} %all_to_all.10.got_ref, ...), custom_call_target="tpu_custom_call" | custom-call | tf_op jit(solution)/shard_map/adam/pallas_call | solution.py:1248
  (9 shorter events, 0.0 us)
Async XLA Ops:
  2.4 2.0 %collective-permute-start = (bf16[592,384]{1,0:T(8,128)(2,1)S(1)}, bf16[592,384]{1,0:T(8,128)(2,1)S(1)}, u32[]{:S(2)}, u32[]{:S(2)}) collective-permute-start(bf16[592,384]{1,0:T(8,128)(2,1)S(1)} %get-tuple-element.79.refs_3_.refs_1_), channel_id=1, source_target_pairs={{0,1},{1,0},{2,3},{3,2},{4,5},{5,4},{6,7},{7,6},{8,9},{9,8},{10,11... | collective-permute-start | bytes 1363976 | tf_op jit(solution)/shard_map/ppermute | solution.py:1333
  27.6 11.1 %copy-start = (f32[3,192,96]{2,1,0:T(8,128)S(1)}, f32[3,192,96]{2,1,0:T(8,128)}, u32[]{:S(2)}) copy-start(f32[3,192,96]{2,1,0:T(8,128)} %refs_0_.1) | copy-start | bytes 663556
  27.6 11.1 %copy-start.1 = (f32[192,384]{1,0:T(8,128)S(1)}, f32[192,384]{1,0:T(8,128)}, u32[]{:S(2)}) copy-start(f32[192,384]{1,0:T(8,128)} %wid_ref.1) | copy-start | bytes 884740
  27.6 11.1 %copy-start.2 = (f32[384,192]{0,1:T(8,128)S(1)}, f32[384,192]{0,1:T(8,128)}, u32[]{:S(2)}) copy-start(f32[384,192]{0,1:T(8,128)} %param.30) | copy-start | bytes 884740
  27.6 11.1 %copy-start.3 = (f32[96,192]{1,0:T(8,128)S(1)}, f32[96,192]{1,0:T(8,128)}, u32[]{:S(2)}) copy-start(f32[96,192]{1,0:T(8,128)} %out_ref.1) | copy-start | bytes 221188
  27.6 1.9 %collective-permute-start.1 = (bf16[16,112,128]{2,1,0:T(8,128)(2,1)S(1)}, bf16[16,112,128]{2,1,0:T(8,128)(2,1)S(1)}, u32[]{:S(2)}, u32[]{:S(2)}) collective-permute-start(bf16[16,112,128]{2,1,0:T(8,128)(2,1)S(1)} %get-tuple-element.92), channel_id=1, source_target_pairs={{0,1},{1,0},{2,3},{3,2},{4,5},{5,4},{6,7},{7,6},{8,9},{9,8},{10,11... | collective-permute-start | bytes 1376264 | tf_op jit(solution)/shard_map/ppermute | solution.py:1362
  29.5 10.1 %copy-start.4 = (f32[6,192]{1,0:T(8,128)S(1)}, f32[6,192]{1,0:T(8,128)}, u32[]{:S(2)}) copy-start(f32[6,192]{1,0:T(8,128)} %vec_ref.1) | copy-start | bytes 13828
  30.4 22.4 %all-to-all-start = ((bf16[16,112,128]{2,1,0:T(8,128)(2,1)}), bf16[16,112,128]{2,1,0:T(8,128)(2,1)S(1)}, u32[]{:S(2)}, u32[]{:S(2)}) async-start(bf16[16,112,128]{2,1,0:T(8,128)(2,1)} %combine.1), calls=%async_computation | async-start | bytes 917504 | tf_op jit(solution)/shard_map/all_to_all | solution.py:1364
  39.6 23.4 %copy-start.5 = (f32[1,4608]{1,0:T(1,128)S(1)}, f32[1,4608]{1,0:T(1,128)}, u32[]{:S(2)}) copy-start(f32[1,4608]{1,0:T(1,128)} %refs_12_.1) | copy-start | bytes 55300
  39.6 23.4 %copy-start.6 = (f32[1,4608]{1,0:T(1,128)S(1)}, f32[1,4608]{1,0:T(1,128)}, u32[]{:S(2)}) copy-start(f32[1,4608]{1,0:T(1,128)} %refs_13_.1) | copy-start | bytes 55300
  39.6 23.4 %copy-start.7 = (f32[1,4608]{1,0:T(1,128)S(1)}, f32[1,4608]{1,0:T(1,128)}, u32[]{:S(2)}) copy-start(f32[1,4608]{1,0:T(1,128)} %refs_14_.1) | copy-start | bytes 55300
  39.6 23.4 %copy-start.8 = (f32[1,4608]{1,0:T(1,128)S(1)}, f32[1,4608]{1,0:T(1,128)}, u32[]{:S(2)}) copy-start(f32[1,4608]{1,0:T(1,128)} %refs_15_.1) | copy-start | bytes 55300
  39.6 23.4 %copy-start.9 = (f32[1,3456]{1,0:T(1,128)S(1)}, f32[1,3456]{1,0:T(1,128)}, u32[]{:S(2)}) copy-start(f32[1,3456]{1,0:T(1,128)} %refs_8_.3) | copy-start | bytes 41476
  39.6 23.4 %copy-start.10 = (f32[1,3456]{1,0:T(1,128)S(1)}, f32[1,3456]{1,0:T(1,128)}, u32[]{:S(2)}) copy-start(f32[1,3456]{1,0:T(1,128)} %refs_9_.1) | copy-start | bytes 41476
  39.6 23.4 %copy-start.11 = (f32[384]{0:T(512)S(1)}, f32[384]{0:T(512)}, u32[]{:S(2)}) copy-start(f32[384]{0:T(512)} %hb_ref.1) | copy-start | bytes 4612
  39.6 23.4 %copy-start.12 = (f32[6,192]{1,0:T(8,128)S(1)}, f32[6,192]{1,0:T(8,128)}, u32[]{:S(2)}) copy-start(f32[6,192]{1,0:T(8,128)} %refs_16_.1) | copy-start | bytes 13828
  39.7 23.4 %copy-start.13 = (f32[6,192]{1,0:T(8,128)S(1)}, f32[6,192]{1,0:T(8,128)}, u32[]{:S(2)}) copy-start(f32[6,192]{1,0:T(8,128)} %refs_17_.1) | copy-start | bytes 13828
  39.7 23.4 %copy-start.14 = (f32[1,1152]{1,0:T(1,128)S(1)}, f32[1,1152]{1,0:T(1,128)}, u32[]{:S(2)}) copy-start(f32[1,1152]{1,0:T(1,128)} %refs_10_.1) | copy-start | bytes 13828
  39.7 23.4 %copy-start.15 = (f32[1,1152]{1,0:T(1,128)S(1)}, f32[1,1152]{1,0:T(1,128)}, u32[]{:S(2)}) copy-start(f32[1,1152]{1,0:T(1,128)} %refs_11_.1) | copy-start | bytes 13828
  39.7 23.4 %copy-start.16 = (f32[4,2]{0,1:T(2,128)S(1)}, f32[4,2]{0,1:T(2,128)}, u32[]{:S(2)}) copy-start(f32[4,2]{0,1:T(2,128)} %param.33) | copy-start | bytes 100
  39.7 23.4 %copy-start.17 = (f32[384]{0:T(512)S(1)}, f32[384]{0:T(512)}, u32[]{:S(2)}) copy-start(f32[384]{0:T(512)} %refs_18_.1) | copy-start | bytes 4612
  39.7 23.4 %copy-start.18 = (f32[384]{0:T(512)S(1)}, f32[384]{0:T(512)}, u32[]{:S(2)}) copy-start(f32[384]{0:T(512)} %refs_19_.1) | copy-start | bytes 4612
  39.7 23.4 %copy-start.19 = (f32[4,2]{0,1:T(2,128)S(1)}, f32[4,2]{0,1:T(2,128)}, u32[]{:S(2)}) copy-start(f32[4,2]{0,1:T(2,128)} %param.46) | copy-start | bytes 100
  39.7 23.4 %copy-start.20 = (f32[4,2]{0,1:T(2,128)S(1)}, f32[4,2]{0,1:T(2,128)}, u32[]{:S(2)}) copy-start(f32[4,2]{0,1:T(2,128)} %param.47) | copy-start | bytes 100
